TPU v7x, 256 devices: a whole 4x4x8 slice. The times are simulated.
256 devices in a mesh: dp: 2 (over x_lo), seq: 64 (over y, x_hi, z), mp: 2 (over core).
Axes of the slice: x: 4 (x_hi: 2, x_lo: 2; x = x_hi * 2 + x_lo), y: 4, z: 8, core: 2. Of those that a mesh axis runs over, the one named last changes fastest.
Arguments:
- queries: bfloat16 [2, 16384, 4096], P('dp', 'seq', 'mp'), may hold values from -6 to 6
- vision: bfloat16 [2, 1024, 8192], P('dp', 'seq'), may hold values from -6 to 6
- key_matrix: bfloat16 [8192, 512], P('seq', 'mp'), may hold values from -0.0625 to 0.0625
- value_matrix: bfloat16 [8192, 512], P('seq', 'mp'), may hold values from -0.0625 to 0.0625
- output_cotangent: bfloat16 [2, 16384, 4096], P('dp', 'seq', 'mp'), may hold values from -6 to 6
Outputs:
- attended: bfloat16 [2, 16384, 4096], P('dp', 'seq', 'mp')
- d_queries: bfloat16 [2, 16384, 4096], P('dp', 'seq', 'mp')
- d_vision: bfloat16 [2, 1024, 8192], P('dp', 'seq')
- d_k_weight: float32 [8192, 512], P('seq', 'mp')
- d_v_weight: float32 [8192, 512], P('seq', 'mp')
All inputs are finite; a program needn't handle non-finite values.
Results may differ from a plain program's by a relative error of at most 0.014.
Values may be sent and summed in bfloat16 or wider, within the bound.
No kernel may reach another device: no remote copies, remote signals or barrier semaphores. Data moves between devices by JAX's collectives and lax.ppermute only.
A program may use at most 128 MiB of HBM per device.

v0:
```python
import math

import jax
import jax.numpy as jnp
from jax import lax
from jax.sharding import PartitionSpec as P

HEAD_SIZE = 128


epsilon = 1e-05


def rms_forward(values_in):
    factor = lax.rsqrt(jnp.mean(values_in * values_in, axis=-1, keepdims=True) + epsilon)
    return (values_in * factor, factor)


def root_mean_square_backward(values_in, factor, upstream):
    inner = jnp.mean(values_in * upstream, axis=-1, keepdims=True)
    return factor * upstream - values_in * (factor * factor * factor) * inner


def gather_weights(both_weights):
    return lax.all_gather(both_weights, "seq", axis=0, tiled=True)


def attend_head(query_rows, grad_rows, key_rows, value_rows, score_scale):
    row_total = query_rows.shape[0]
    rows_per_block = math.gcd(row_total, 512)
    count_of_blocks = row_total // rows_per_block
    width = query_rows.shape[1]

    def block_step(running, piece_list):
        key_acc, value_acc = running
        query_block, grad_block = piece_list
        scores = (
            jnp.einsum("rd,jd->rj", query_block, key_rows, preferred_element_type=jnp.float32)
            * score_scale
        )
        expo = jnp.exp(scores)
        weights = expo / jnp.sum(expo, axis=-1, keepdims=True)
        weights_low = weights.astype(jnp.bfloat16)
        out_block = jnp.einsum(
            "rj,jd->rd", weights_low, value_rows, preferred_element_type=jnp.float32
        ).astype(jnp.bfloat16)
        score_grad = jnp.einsum(
            "rd,jd->rj", grad_block, value_rows, preferred_element_type=jnp.float32
        )
        delta = jnp.sum(weights * score_grad, axis=-1, keepdims=True)
        logit_grad = (weights * (score_grad - delta)).astype(jnp.bfloat16)
        norm_gradient = (
            jnp.einsum("rj,jd->rd", logit_grad, key_rows, preferred_element_type=jnp.float32)
            * score_scale
        )
        key_acc = (
            key_acc
            + jnp.einsum("rj,rd->jd", logit_grad, query_block, preferred_element_type=jnp.float32)
            * score_scale
        )
        value_acc = value_acc + jnp.einsum(
            "rj,rd->jd", weights_low, grad_block, preferred_element_type=jnp.float32
        )
        return ((key_acc, value_acc), (out_block, norm_gradient))

    initial_accumulator = (
        jnp.zeros(key_rows.shape, jnp.float32),
        jnp.zeros(value_rows.shape, jnp.float32),
    )
    piece_list = (
        query_rows.reshape(count_of_blocks, rows_per_block, width),
        grad_rows.reshape(count_of_blocks, rows_per_block, width),
    )
    (key_gradient, value_gradient), (out_blocks, normed_block_list) = lax.scan(
        block_step, initial_accumulator, piece_list
    )
    return (
        out_blocks.reshape(row_total, width),
        normed_block_list.reshape(row_total, width),
        key_gradient,
        value_gradient,
    )


def body(queries, vision, key_matrix, value_matrix, output_cotangent):
    token_count = queries.shape[1]
    head_count = queries.shape[2] // HEAD_SIZE
    kv_heads = key_matrix.shape[1] // HEAD_SIZE
    query_group_size = head_count // kv_heads
    kv_width = key_matrix.shape[1]
    score_scale = HEAD_SIZE ** (-0.5)
    both_weights = jnp.concatenate([key_matrix, value_matrix], axis=1)
    own_rows = vision[0]
    own_count = own_rows.shape[0]
    full_weights = gather_weights(both_weights)
    raw_own = jnp.dot(own_rows, full_weights, preferred_element_type=jnp.float32)
    key_unnormed = raw_own[:, :kv_width].reshape(own_count, kv_heads, HEAD_SIZE)
    key_norm, key_norm_factor = rms_forward(key_unnormed)
    kv_own = jnp.concatenate(
        [key_norm.reshape(own_count, kv_width), raw_own[:, kv_width:]], axis=1
    ).astype(jnp.bfloat16)
    kv_all = lax.all_gather(kv_own, "seq", axis=0, tiled=True)
    vis_total = kv_all.shape[0]
    key_all = kv_all[:, :kv_width].reshape(vis_total, kv_heads, HEAD_SIZE)
    value_all = kv_all[:, kv_width:].reshape(vis_total, kv_heads, HEAD_SIZE)
    query_unnormed = (
        queries[0].astype(jnp.float32).reshape(token_count, kv_heads, query_group_size, HEAD_SIZE)
    )
    query_norm, query_factor = rms_forward(query_unnormed)
    query_rows = (
        query_norm.astype(jnp.bfloat16)
        .transpose(1, 2, 0, 3)
        .reshape(kv_heads, query_group_size * token_count, HEAD_SIZE)
    )
    grad_rows = (
        output_cotangent[0]
        .reshape(token_count, kv_heads, query_group_size, HEAD_SIZE)
        .transpose(1, 2, 0, 3)
        .reshape(kv_heads, query_group_size * token_count, HEAD_SIZE)
    )
    out_list = []
    norm_list = []
    key_list = []
    value_list = []
    for kv_index in range(kv_heads):
        out_head, norm_head, key_head, value_head = attend_head(
            query_rows[kv_index],
            grad_rows[kv_index],
            key_all[:, kv_index],
            value_all[:, kv_index],
            score_scale,
        )
        out_list.append(out_head)
        norm_list.append(norm_head)
        key_list.append(key_head)
        value_list.append(value_head)
    attended = (
        jnp.stack(out_list)
        .reshape(kv_heads, query_group_size, token_count, HEAD_SIZE)
        .transpose(2, 0, 1, 3)
        .reshape(1, token_count, head_count * HEAD_SIZE)
    )
    norm_gradient = (
        jnp.stack(norm_list)
        .reshape(kv_heads, query_group_size, token_count, HEAD_SIZE)
        .transpose(2, 0, 1, 3)
    )
    d_queries = (
        root_mean_square_backward(query_unnormed, query_factor, norm_gradient)
        .astype(jnp.bfloat16)
        .reshape(1, token_count, head_count * HEAD_SIZE)
    )
    kv_terms = jnp.concatenate(
        [
            jnp.stack(key_list, axis=1).reshape(vis_total, kv_width),
            jnp.stack(value_list, axis=1).reshape(vis_total, kv_width),
        ],
        axis=1,
    )
    kv_grad = lax.psum_scatter(kv_terms, "seq", scatter_dimension=0, tiled=True)
    key_gradient = root_mean_square_backward(
        key_unnormed, key_norm_factor, kv_grad[:, :kv_width].reshape(own_count, kv_heads, HEAD_SIZE)
    )
    raw_grad = jnp.concatenate(
        [key_gradient.reshape(own_count, kv_width), kv_grad[:, kv_width:]], axis=1
    ).astype(jnp.bfloat16)
    weight_part = lax.psum_scatter(
        jnp.einsum("jd,jc->dc", own_rows, raw_grad, preferred_element_type=jnp.float32),
        "seq",
        scatter_dimension=0,
        tiled=True,
    )
    vision_part = jnp.einsum(
        "jc,dc->jd", raw_grad, full_weights, preferred_element_type=jnp.float32
    )
    weight_total = lax.psum(weight_part.astype(jnp.bfloat16), "dp").astype(jnp.float32)
    vision_total = lax.psum(vision_part.astype(jnp.bfloat16), "mp")
    d_vision = vision_total[None]
    return (attended, d_queries, d_vision, weight_total[:, :kv_width], weight_total[:, kv_width:])


def solution(mesh):
    in_specs = (
        P("dp", "seq", "mp"),
        P("dp", "seq", None),
        P("seq", "mp"),
        P("seq", "mp"),
        P("dp", "seq", "mp"),
    )
    out_specs = (
        P("dp", "seq", "mp"),
        P("dp", "seq", "mp"),
        P("dp", "seq", None),
        P("seq", "mp"),
        P("seq", "mp"),
    )
    return jax.shard_map(body, mesh=mesh, in_specs=in_specs, out_specs=out_specs, check_vma=False)
```

profile of v0, /device:TPU:1, one launch (start us, length us, event | category | flops | bytes accessed | tf_op | source)
XLA Modules:
  0.0 1222.3 jit_solution(4770219448731895770)
XLA Ops:
  8.9 155.4 %all-gather.3.cloned.1.call-done = bf16[8192,512]{1,0:T(8,128)(2,1)} async-done(((bf16[128,512]{1,0:T(8,128)(2,1)}), bf16[8192,512]{1,0:T(8,128)(2,1)}) %all-gather.3.cloned.1.call-update) | async-done | bytes 8388624 | tf_op jit(solution)/shard_map/all_gather | solution.py:25
  164.2 4.6 convolution_bitcast_fusion.1
  176.4 102.6 %all-gather.5.cloned.1.call-done = bf16[1024,512]{1,0:T(8,128)(2,1)} async-done(((bf16[16,512]{1,0:T(8,128)(2,1)}), bf16[1024,512]{1,0:T(8,128)(2,1)}) %all-gather.5.cloned.1.call-update) | async-done | bytes 1048592 | tf_op jit(solution)/shard_map/all_gather | solution.py:102
  285.6 48.7 %while.35 = (s32[]{:T(128)}, f32[1024,128]{1,0:T(8,128)}, f32[1024,128]{1,0:T(8,128)}, bf16[4,512,128]{2,1,0:T(8,128)(2,1)}, f32[4,512,128]{2,1,0:T(8,128)}, /*i...) while((s32[]{:T(128)}, f32[1024,128]{1,0:T(8,128)}, ...), condition=%wide.region_9.10_spmd.clone, body=%wide.region_6.9_spmd.clone.sunk | while | flops 815004672 | bytes 26097872 | solution.py:74
  287.2 1.7 multiply_reduce_fusion.7
  289.4 2.2 fusion.132
  291.6 1.6 convolution_add_fusion.5
  293.2 2.3 fusion.133
  295.6 2.1 fusion.134
  299.2 1.7 multiply_reduce_fusion.7
  301.4 2.4 fusion.132
  303.8 1.6 convolution_add_fusion.5
  305.5 2.3 fusion.133
  307.8 2.1 fusion.134
  311.4 1.7 multiply_reduce_fusion.7
  313.6 2.4 fusion.132
  316.1 1.6 convolution_add_fusion.5
  317.7 2.3 fusion.133
  320.0 2.1 fusion.134
  323.7 1.7 multiply_reduce_fusion.7
  325.9 2.4 fusion.132
  328.3 1.6 convolution_add_fusion.5
  329.9 2.3 fusion.133
  332.3 2.1 fusion.134
  336.2 40.4 %while.34 = (s32[]{:T(128)}, f32[1024,128]{1,0:T(8,128)}, f32[1024,128]{1,0:T(8,128)}, bf16[4,512,128]{2,1,0:T(8,128)(2,1)}, f32[4,512,128]{2,1,0:T(8,128)}, /*i...) while((s32[]{:T(128)}, f32[1024,128]{1,0:T(8,128)}, ...), condition=%wide.region_5.6_spmd.clone, body=%wide.region_2.5_spmd.clone.sunk | while | flops 815004672 | bytes 29243684 | solution.py:74
  336.2 1.6 fusion.117
  339.9 2.2 fusion.118
  342.2 1.7 convolution_add_fusion.4
  346.2 1.6 fusion.117
  349.9 2.4 fusion.118
  352.3 1.7 convolution_add_fusion.4
  356.4 1.6 fusion.117
  360.1 2.4 fusion.118
  362.5 1.7 convolution_add_fusion.4
  366.5 1.6 fusion.117
  370.2 2.4 fusion.118
  372.6 1.7 convolution_add_fusion.4
  378.2 1.7 pad_maximum_fusion
  380.2 315.7 %reduce-scatter.3.cloned.1.call-done = f32[16,512]{1,0:T(8,128)} async-done(((f32[1024,512]{1,0:T(8,128)}), f32[16,512]{1,0:T(8,128)}) %reduce-scatter.3.cloned.1.call-update) | async-done | bytes 32784 | tf_op jit(solution)/shard_map/reduce_scatter | solution.py:160
  698.4 8.1 convolution_bitcast_fusion
  709.8 2.0 copy.55
  716.9 4.4 subtract_convert_fusion
  721.2 379.7 %reduce-scatter.5.cloned.1.call-done = f32[128,512]{0,1:T(8,128)} async-done(((f32[8192,512]{0,1:T(8,128)}), f32[128,512]{0,1:T(8,128)}) %reduce-scatter.5.cloned.1.call-update) | async-done | bytes 262160 | tf_op jit(solution)/shard_map/reduce_scatter | solution.py:167
  1100.9 1.6 convert_element_type.51
  1102.6 6.5 fusion.50
  1111.8 67.5 %all-reduce.5.cloned.1.call-done = bf16[128,512]{0,1:T(8,128)(2,1)} async-done(((bf16[128,512]{0,1:T(8,128)(2,1)}), bf16[128,512]{0,1:T(8,128)(2,1)}) %all-reduce.5.cloned.1.call-update) | async-done | bytes 131088 | tf_op jit(solution)/shard_map/psum | solution.py:176
  1181.7 32.0 %all-reduce.3.cloned.1.call-done = bf16[1,16,8192]{2,1,0:T(8,128)(2,1)} async-done(((bf16[1,16,8192]{2,1,0:T(8,128)(2,1)}), bf16[1,16,8192]{2,1,0:T(8,128)(2,1)}) %all-reduce.3.cloned.1.call-update) | async-done | bytes 262160 | tf_op jit(solution)/shard_map/psum | solution.py:177
  1213.8 1.7 copy.124
  (183 shorter events, 61.4 us)
Async XLA Ops:
  7.2 157.1 %copy-start = (bf16[1,16,8192]{2,1,0:T(8,128)(2,1)S(1)}, bf16[1,16,8192]{2,1,0:T(8,128)(2,1)}, u32[]{:S(2)}) copy-start(bf16[1,16,8192]{2,1,0:T(8,128)(2,1)} %param.10) | copy-start | bytes 786436
  7.2 157.1 %all-gather.3.cloned.1.call-start = ((), (), s32[]{:S(2)}) async-start(), calls=%async_computation.2 | async-start | bytes 8519680 | tf_op jit(solution)/shard_map/all_gather | solution.py:25
  8.8 161.0 %copy-start.14 = (bf16[1,256,2048]{2,1,0:T(8,128)(2,1)S(1)}, bf16[1,256,2048]{2,1,0:T(8,128)(2,1)}, u32[]{:S(2)}) copy-start(bf16[1,256,2048]{2,1,0:T(8,128)(2,1)} %param.9) | copy-start | bytes 3145732
  8.8 270.1 %all-gather.5.cloned.1.call-start = ((), (), s32[]{:S(2)}) async-start(), calls=%async_computation.3 | async-start | bytes 1064960 | tf_op jit(solution)/shard_map/all_gather | solution.py:102
  169.7 526.2 %reduce-scatter.3.cloned.1.call-start = ((), (), s32[]{:S(2)}) async-start(), calls=%async_computation.4 | async-start | bytes 2129920 | tf_op jit(solution)/shard_map/reduce_scatter | solution.py:160
  170.4 2.1 copy-start.1
  171.6 1.0 copy-start.9
  172.5 1.4 copy-start.15
  289.4 2.2 copy-start.18
  293.2 2.3 copy-start.19
  301.4 2.4 copy-start.18
  305.5 2.3 copy-start.19
  313.6 2.4 copy-start.18
  317.7 2.3 copy-start.19
  325.9 2.4 copy-start.18
  329.9 2.3 copy-start.19
  336.2 1.6 copy-start.20
  339.9 2.2 copy-start.16
  342.2 1.7 copy-start.21
  343.8 1.2 copy-start.17
  343.9 1.2 copy-start.3
  346.2 1.6 copy-start.20
  349.9 2.4 copy-start.16
  352.3 1.7 copy-start.21
  354.0 1.2 copy-start.17
  354.0 1.2 copy-start.3
  356.4 1.6 copy-start.20
  360.0 2.4 copy-start.16
  362.5 1.7 copy-start.21
  364.2 1.2 copy-start.17
  364.2 1.2 copy-start.3
  366.5 1.6 copy-start.20
  370.2 2.4 copy-start.16
  372.6 1.7 copy-start.21
  374.3 1.2 copy-start.17
  374.3 1.2 copy-start.3
  376.7 1.4 copy-start.4
  376.7 1.5 copy-start.5
  379.9 721.0 %reduce-scatter.5.cloned.1.call-start = ((), (), s32[]{:S(2)}) async-start(), calls=%async_computation.6 | async-start | bytes 17039360 | tf_op jit(solution)/shard_map/reduce_scatter | solution.py:167
  706.5 1.0 copy-start.11
  706.5 2.2 copy-start.10
  706.5 472.8 %all-reduce.5.cloned.1.call-start = ((), (), s32[]{:S(2)}) async-start(), calls=%async_computation.7 | async-start | bytes 262144 | tf_op jit(solution)/shard_map/psum | solution.py:176
  707.5 4.3 copy-start.7
  709.8 3.6 copy-start.2
  1102.6 6.6 copy-start.12
  1102.6 6.6 copy-start.13
  1102.6 111.2 %all-reduce.3.cloned.1.call-start = ((), (), s32[]{:S(2)}) async-start(), calls=%async_computation.5 | async-start | bytes 524288 | tf_op jit(solution)/shard_map/psum | solution.py:177
  1109.1 1.5 copy-start.8
  (1 other events, 1.0 us)
Sparse Core Ops, SparseCore 0:
  12.2 151.9 all-gather.2
  169.8 109.1 all-gather.4
  380.0 315.8 reduce-scatter.2
  706.6 394.2 reduce-scatter.4
  1104.1 75.2 all-reduce.4
  1182.5 31.2 all-reduce.2
where the time goes:
time: 1220 us
  waiting for transfers between devices  1050 us (86%)
  matrix products  104 us (9%)
  local copies, waits for them, and re-layouts  29.6 us (2%)
  other arithmetic  20.9 us (2%)
  between operations  14.5 us (1%)
    reduce_scatter x1, waiting for transfers between devices, body(): lax.psum_scatter(jnp.einsum('jd,jc->dc', own_rows, raw_grad, preferred_el...  380 us
    reduce_scatter x1, waiting for transfers between devices, body(): kv_grad = lax.psum_scatter(kv_terms, 'seq', scatter_dimension=0, tiled=True)  316 us
    all_gather x1, waiting for transfers between devices, gather_weights(): return lax.all_gather(both_weights, 'seq', axis=0, tiled=True)  155 us
    all_gather x1, waiting for transfers between devices, body(): kv_all = lax.all_gather(kv_own, 'seq', axis=0, tiled=True)  103 us
    psum x1, waiting for transfers between devices, body(): lax.psum(weight_part.astype(jnp.bfloat16), 'dp').astype(jnp.float32)  67.5 us
    psum x1, waiting for transfers between devices, body(): vision_total = lax.psum(vision_part.astype(jnp.bfloat16), 'mp')  32 us
  transfers between devices with their start and end apart: 6, of which 6 were waited for; matrix products, arithmetic and copies ran while one was open for 3% of the time, Pallas kernels for 0%

commit v1 on v0

v1 whole, which is shorter than its diff:
```python
import functools
import math

import jax
import jax.numpy as jnp
from jax import lax
from jax.experimental import pallas as pl
from jax.experimental.pallas import tpu as pltpu
from jax.sharding import Mesh
from jax.sharding import PartitionSpec as P

HEAD = 128
EPS = 1e-5
SCALE = HEAD**-0.5
F32 = jnp.float32
BF = jnp.bfloat16
NT = ((1,), (1,))
NN = ((1,), (0,))
TN = ((0,), (0,))
PARTS = (("y", 4), ("xh", 2), ("z", 8))
SEQ = ("y", "xh", "z")
COL = ("xh", "z")
Y_COUNT = 4
COL_COUNT = 16


def dot(a, b, dims):
    return lax.dot_general(a, b, (dims, ((), ())), preferred_element_type=F32)


def attend_one(query, cotangent, key_rows, value_rows):
    query_f = query.astype(F32)
    factor = lax.rsqrt(jnp.mean(query_f * query_f, axis=-1, keepdims=True) + EPS)
    query_norm = (query_f * factor).astype(BF)
    scores = dot(query_norm, key_rows, NT)
    expo = jnp.exp2(scores * (SCALE * math.log2(math.e)))
    inverse = 1.0 / jnp.sum(expo, axis=1, keepdims=True)
    expo_low = expo.astype(BF)
    out = dot(expo_low, value_rows, NN) * inverse
    scaled = cotangent.astype(F32) * inverse
    scaled_low = scaled.astype(BF)
    score_grad = dot(scaled_low, value_rows, NT)
    delta = jnp.sum(scaled * out, axis=1, keepdims=True)
    logit_grad = (expo * (score_grad - delta)).astype(BF)
    norm_grad = dot(logit_grad, key_rows, NN) * SCALE
    key_grad = dot(logit_grad, query_norm, TN)
    value_grad = dot(expo_low, scaled_low, TN)
    inner = jnp.mean(query_f * norm_grad, axis=-1, keepdims=True)
    d_query = factor * norm_grad - query_f * (factor * factor * factor) * inner
    return out.astype(BF), d_query.astype(BF), key_grad, value_grad


def attend_kernel(heads, steps, q_ref, c_ref, k_ref, v_ref, o_ref, dq_ref, dk_ref, dv_ref, dk_sum, dv_sum):
    step = pl.program_id(1)

    @pl.when(step == 0)
    def _():
        dk_sum[...] = jnp.zeros_like(dk_sum)
        dv_sum[...] = jnp.zeros_like(dv_sum)

    key_rows = k_ref[...]
    value_rows = v_ref[...]
    for head in range(heads):
        cols = slice(head * HEAD, (head + 1) * HEAD)
        out, d_query, key_grad, value_grad = attend_one(q_ref[:, cols], c_ref[:, cols], key_rows, value_rows)
        o_ref[:, cols] = out
        dq_ref[:, cols] = d_query
        dk_sum[...] += key_grad
        dv_sum[...] += value_grad

    @pl.when(step == steps - 1)
    def _():
        dk_ref[...] = (dk_sum[...] * SCALE).astype(BF)
        dv_ref[...] = dv_sum[...].astype(BF)


def attend(queries, cotangent, kv, heads=2):
    rows, width = queries.shape
    vis_total = kv.shape[0]
    kv_heads = kv.shape[1] // HEAD // 2
    steps = width // HEAD // kv_heads // heads
    q_spec = pl.BlockSpec((rows, heads * HEAD), lambda a, g: (0, a * steps + g))
    k_spec = pl.BlockSpec((vis_total, HEAD), lambda a, g: (0, a))
    v_spec = pl.BlockSpec((vis_total, HEAD), lambda a, g: (0, kv_heads + a))
    return pl.pallas_call(
        functools.partial(attend_kernel, heads, steps),
        grid=(kv_heads, steps),
        in_specs=[q_spec, q_spec, k_spec, v_spec],
        out_specs=[q_spec, q_spec, k_spec, k_spec],
        out_shape=[jax.ShapeDtypeStruct((rows, width), BF)] * 2
        + [jax.ShapeDtypeStruct((vis_total, kv_heads * HEAD), BF)] * 2,
        scratch_shapes=[pltpu.VMEM((vis_total, HEAD), F32)] * 2,
        compiler_params=pltpu.CompilerParams(
            vmem_limit_bytes=48 * 1024 * 1024, dimension_semantics=("arbitrary", "arbitrary")
        ),
        cost_estimate=pl.CostEstimate(
            flops=12 * rows * width * vis_total,
            bytes_accessed=8 * rows * width,
            transcendentals=rows * (width // HEAD) * vis_total,
        ),
        name="attend",
    )(queries, cotangent, kv, kv)


def swap(x, axis):
    return lax.ppermute(x, axis, [(0, 1), (1, 0)])


def shift(x, axis, count, by):
    return lax.ppermute(x, axis, [(i, (i + by) % count) for i in range(count)])


def gather_y(x):
    own = lax.axis_index("y")
    whole = jnp.zeros((Y_COUNT,) + x.shape, x.dtype)
    pieces = [(x, 0)] + [(shift(x, "y", Y_COUNT, by), by) for by in (1, 3, 2)]
    for piece, by in pieces:
        whole = lax.dynamic_update_index_in_dim(whole, piece, (own + Y_COUNT - by) % Y_COUNT, 0)
    return whole.reshape((Y_COUNT * x.shape[0],) + x.shape[1:])


def gather_col(x):
    copies = jnp.broadcast_to(x[None], (COL_COUNT,) + x.shape).reshape((COL_COUNT * x.shape[0],) + x.shape[1:])
    return lax.all_to_all(copies, COL, 0, 0, tiled=True)


def norm_heads(rows):
    shaped = rows.reshape(rows.shape[0], rows.shape[1] // HEAD, HEAD)
    factor = lax.rsqrt(jnp.mean(shaped * shaped, axis=-1, keepdims=True) + EPS)
    return shaped, factor


def body(queries, vision, key_matrix, value_matrix, output_cotangent):
    kv_width = key_matrix.shape[1]
    width = 2 * kv_width
    own_rows = vision[0]
    own_count, model_width = own_rows.shape
    weight_rows = key_matrix.shape[0]
    weights = jnp.concatenate([key_matrix, value_matrix], axis=1)

    full_weights = lax.all_gather(weights, SEQ, axis=0, tiled=True)

    columns = own_rows.reshape(own_count, Y_COUNT, COL_COUNT, weight_rows).transpose(2, 0, 1, 3)
    columns = columns.reshape(COL_COUNT * own_count, Y_COUNT * weight_rows)
    vision_block = lax.all_to_all(columns, COL, 0, 0, tiled=True)
    weight_block = gather_y(weights)
    part = jnp.dot(vision_block, weight_block, preferred_element_type=F32).astype(BF)
    parts = lax.all_to_all(part, COL, 0, 0, tiled=True)
    raw_own = jnp.sum(parts.reshape(COL_COUNT, own_count, width).astype(F32), axis=0)

    key_raw, key_factor = norm_heads(raw_own[:, :kv_width])
    key_norm = (key_raw * key_factor).reshape(own_count, kv_width)
    kv_own = jnp.concatenate([key_norm, raw_own[:, kv_width:]], axis=1).astype(BF)
    kv_all = gather_y(gather_col(kv_own))

    attended, d_queries, key_terms, value_terms = attend(queries[0], output_cotangent[0], kv_all)

    terms = jnp.concatenate([key_terms, value_terms], axis=1)
    terms = lax.all_to_all(terms, SEQ, 0, 0, tiled=True)
    kv_grad = jnp.sum(terms.reshape(-1, own_count, width).astype(F32), axis=0)
    upstream = kv_grad[:, :kv_width].reshape(key_raw.shape)
    inner = jnp.mean(key_raw * upstream, axis=-1, keepdims=True)
    key_grad = key_factor * upstream - key_raw * (key_factor * key_factor * key_factor) * inner
    raw_grad = jnp.concatenate([key_grad.reshape(own_count, kv_width), kv_grad[:, kv_width:]], axis=1).astype(BF)

    grad_block = gather_col(raw_grad)
    vision_part = jnp.einsum("jc,dc->jd", raw_grad, full_weights, preferred_element_type=F32).astype(BF)
    d_vision = (vision_part.astype(F32) + swap(vision_part, "mp").astype(F32)).astype(BF)

    weight_part = jnp.einsum("jd,jc->dc", vision_block, grad_block, preferred_element_type=F32).astype(BF)
    weight_parts = lax.all_to_all(weight_part, "y", 0, 0, tiled=True)
    weight_sum = jnp.sum(weight_parts.reshape(Y_COUNT, weight_rows, width).astype(F32), axis=0).astype(BF)
    weight_total = weight_sum.astype(F32) + swap(weight_sum, "dp").astype(F32)
    return (attended[None], d_queries[None], d_vision[None], weight_total[:, :kv_width], weight_total[:, kv_width:])


def solution(mesh):
    fine = Mesh(mesh.devices.reshape((2,) + tuple(n for _, n in PARTS) + (2,)), ("dp",) + SEQ + ("mp",))
    rows = P("dp", SEQ, "mp")
    vision = P("dp", SEQ, None)
    weights = P(SEQ, "mp")
    return jax.shard_map(
        body,
        mesh=fine,
        in_specs=(rows, vision, weights, weights, rows),
        out_specs=(rows, rows, vision, weights, weights),
        check_vma=False,
    )
```

time: 1220 us -> 200 us (0.16)
  waiting for transfers between devices: 1050 us -> 26.9 us
  blocking collectives: 0 us -> 102 us
  matrix products: 104 us -> 6.3 us
  starting transfers between devices: 0.47 us -> 24.1 us
  local copies, waits for them, and re-layouts: 29.6 us -> 6.6 us
  other arithmetic: 20.9 us -> 1.4 us
  Pallas kernels: 0 us -> 17.1 us
    reduce_scatter x2 -> x0, waiting for transfers between devices: 695 us -> none  [the longest x1 380 us: body(): lax.psum_scatter(jnp.einsum('jd,jc->dc', own_rows, raw_grad, preferred_el...]
    all_gather x2 -> x1, waiting for transfers between devices: 258 us -> 8.55 us  [body(): full_weights = lax.all_gather(weights, SEQ, axis=0, tiled=True)]
    all_to_all x0 -> x5, blocking collectives: none -> 102 us  [the longest x1 42.2 us: body(): terms = lax.all_to_all(terms, SEQ, 0, 0, tiled=True)]
    psum x2 -> x0, waiting for transfers between devices: 99.5 us -> none  [the longest x1 67.5 us: body(): lax.psum(weight_part.astype(jnp.bfloat16), 'dp').astype(jnp.float32)]
    dot_general x51 -> x3, matrix products: 104 us -> 6.3 us  [the longest x1 5.66 us: body(): jnp.einsum('jc,dc->jd', raw_grad, full_weights, preferred_element_type=F32)]
    pallas_call x0 -> x1, Pallas kernels: none -> 17.1 us  [attend(): pl.pallas_call(functools.partial(attend_kernel, heads, steps), grid=(kv_h...]
    ppermute x0 -> x8, starting transfers between devices: none -> 13.3 us  [the longest x6 8.37 us: shift(): return lax.ppermute(x, axis, [(i, (i + by) % count) for i in range(count)])]
  transfers between devices with their start and end apart: 6 -> 10, of which waited for: 6 -> 6; matrix products, arithmetic and copies ran while one was open for 3% -> 5% of each run, Pallas kernels for 0% -> 9%
where the time goes in v1:
time: 200 us; the launch traced here: 199 us
  blocking collectives  102 us (51%)
  waiting for transfers between devices  26.9 us (13%)
  starting transfers between devices  24.1 us (12%)
  Pallas kernels  17.1 us (9%)
  between operations  14.4 us (7%)
  local copies, waits for them, and re-layouts  6.6 us (3%)
  matrix products  6.3 us (3%)
    all_to_all x1, blocking collectives, body(): terms = lax.all_to_all(terms, SEQ, 0, 0, tiled=True)  42.2 us
    all_to_all x2, blocking collectives, gather_col(): return lax.all_to_all(copies, COL, 0, 0, tiled=True)  29.4 us
    pallas_call x1, Pallas kernels, attend(): pl.pallas_call(functools.partial(attend_kernel, heads, steps), grid=(kv_h...  17.1 us
    all_to_all x1, blocking collectives, body(): parts = lax.all_to_all(part, COL, 0, 0, tiled=True)  16.8 us
    all_to_all x1, blocking collectives, body(): weight_parts = lax.all_to_all(weight_part, 'y', 0, 0, tiled=True)  14.1 us
    all_to_all x1, starting transfers between devices, body(): vision_block = lax.all_to_all(columns, COL, 0, 0, tiled=True)  10.7 us
    ppermute x6, waiting for transfers between devices, shift(): return lax.ppermute(x, axis, [(i, (i + by) % count) for i in range(count)])  9.82 us
    all_gather x1, waiting for transfers between devices, body(): full_weights = lax.all_gather(weights, SEQ, axis=0, tiled=True)  8.55 us
  transfers between devices with their start and end apart: 10, of which 6 were waited for; matrix products, arithmetic and copies ran while one was open for 5% of the time, Pallas kernels for 9%

profile of v1, /device:TPU:1, one launch (start us, length us, event | category | flops | bytes accessed | tf_op | source)
XLA Modules:
  0.0 199.2 jit_solution(6861054127424162321)
XLA Ops:
  7.2 0.0 all-gather.2.cloned.1.call-start
  7.2 1.0 constant_dynamic-update-slice_fusion.1
  8.2 0.8 constant_dynamic-update-slice_fusion
  9.1 0.7 copy-done.2
  9.7 0.0 all-gather.2.cloned.1.call-update
  9.7 2.2 %collective-permute-start = (bf16[128,512]{1,0:T(8,128)(2,1)}, bf16[128,512]{1,0:T(8,128)(2,1)S(1)}, u32[]{:S(2)}, u32[]{:S(2)}) collective-permute-start(bf16[128,512]{1,0:T(8,128)(2,1)} %copy-done.2), channel_id=1, source_target_pairs={{0,32},{32,64},{64,96},{96,0},{1,33},{33,65},{65,97},{97,1},{2,34}... | collective-permute-start | bytes 393224 | tf_op jit(solution)/shard_map/ppermute | solution.py:110
  11.9 1.5 collective-permute-start.1
  13.5 1.6 collective-permute-start.2
  15.0 1.0 copy.11
  16.0 0.1 copy.20
  16.2 0.8 all_to_all.36
  17.0 10.7 %all-to-all-start = ((bf16[16,16,512]{2,1,0:T(8,128)(2,1)}), bf16[16,16,512]{2,1,0:T(8,128)(2,1)S(1)}, u32[]{:S(2)}, u32[]{:S(2)}) async-start(bf16[16,16,512]{2,1,0:T(8,128)(2,1)} %all_to_all.36), calls=%async_computation | async-start | bytes 524288 | tf_op jit(solution)/shard_map/all_to_all | solution.py:145
  27.8 0.9 bitcast_dynamic-update-slice_fusion.7
  28.7 0.0 collective-permute-done
  28.8 0.0 collective-permute-done.1
  28.8 0.0 collective-permute-done.2
  28.9 8.1 %all-to-all-done = bf16[16,16,512]{2,1,0:T(8,128)(2,1)S(1)} async-done(((bf16[16,16,512]{2,1,0:T(8,128)(2,1)}), bf16[16,16,512]{2,1,0:T(8,128)(2,1)S(1)}, u32[]{:S(2)}, u32[]{:S(2)}) %all-to-all-start) | async-done | bytes 262176 | tf_op jit(solution)/shard_map/all_to_all | solution.py:145
  37.0 0.3 convolution_convert_fusion.1
  37.3 16.8 %all_to_all.54 = bf16[16,16,512]{2,1,0:T(8,128)(2,1)S(1)} all-to-all(bf16[16,16,512]{2,1,0:T(8,128)(2,1)S(1)} %bitcast.84), channel_id=1, replica_groups=mesh['dp'=2,'y'=4,'xh'=2,'z'=8,'mp'=2] {'xh','z'}, dimensions={0} | all-to-all | bytes 524288 | tf_op jit(solution)/shard_map/all_to_all | solution.py:148
  54.1 0.1 reduce_sum.49
  54.3 0.1 mul.70
  54.4 14.8 %all_to_all.55 = bf16[16,16,512]{2,1,0:T(8,128)(2,1)S(1)} all-to-all(bf16[16,16,512]{2,1,0:T(8,128)(2,1)S(1)} %broadcast_in_dim.61), channel_id=1, replica_groups=mesh['dp'=2,'y'=4,'xh'=2,'z'=8,'mp'=2] {'xh','z'}, dimensions={0} | all-to-all | bytes 524288 | tf_op jit(solution)/shard_map/all_to_all | solution.py:124
  69.2 0.0 collective-permute-start.3
  69.2 2.7 %collective-permute-start.4 = (bf16[256,512]{1,0:T(8,128)(2,1)S(1)}, bf16[256,512]{1,0:T(8,128)(2,1)S(1)}, u32[]{:S(2)}, u32[]{:S(2)}) collective-permute-start(bf16[256,512]{1,0:T(8,128)(2,1)S(1)} %bitcast.79), channel_id=1, source_target_pairs={{0,96},{32,0},{64,32},{96,64},{1,97},{33,1},{65,33},{97,65},{2,98}... | collective-permute-start | bytes 786440 | tf_op jit(solution)/shard_map/ppermute | solution.py:110
  71.9 0.4 collective-permute-start.5
  72.3 0.1 broadcast_in_dim.55
  72.4 3.9 %collective-permute-done.3 = bf16[256,512]{1,0:T(8,128)(2,1)S(1)} collective-permute-done((bf16[256,512]{1,0:T(8,128)(2,1)S(1)}, bf16[256,512]{1,0:T(8,128)(2,1)S(1)}, u32[]{:S(2)}, u32[]{:S(2)}) %collective-permute-start.3) | collective-permute-done | bytes 262176 | tf_op jit(solution)/shard_map/ppermute | solution.py:110
  76.3 2.7 %collective-permute-done.4 = bf16[256,512]{1,0:T(8,128)(2,1)S(1)} collective-permute-done((bf16[256,512]{1,0:T(8,128)(2,1)S(1)}, bf16[256,512]{1,0:T(8,128)(2,1)S(1)}, u32[]{:S(2)}, u32[]{:S(2)}) %collective-permute-start.4) | collective-permute-done | bytes 262176 | tf_op jit(solution)/shard_map/ppermute | solution.py:110
  79.1 3.2 %collective-permute-done.5 = bf16[256,512]{1,0:T(8,128)(2,1)S(1)} collective-permute-done((bf16[256,512]{1,0:T(8,128)(2,1)S(1)}, bf16[256,512]{1,0:T(8,128)(2,1)S(1)}, u32[]{:S(2)}, u32[]{:S(2)}) %collective-permute-start.5) | collective-permute-done | bytes 262176 | tf_op jit(solution)/shard_map/ppermute | solution.py:110
  82.3 17.1 %attend.1 = (bf16[256,2048]{1,0:T(8,128)(2,1)}, bf16[256,2048]{1,0:T(8,128)(2,1)}, bf16[1024,256]{1,0:T(8,128)(2,1)S(1)}, bf16[1024,256]{1,0:T(8,128)(2,1)S(1)}) custom-call(bf16[256,2048]{1,0:T(8,128)(2,1)S(1)} %bitcast.72, bf16[256,2048]{1,0:T(8,128)(2,1)S(1)} %bitcast.73, bf16[1024,512]{1,0:T(8,128)(2,1)S(1)} %bitcast.70, bf16[1024,512]{1,0:T(8,128)(2,1)S(1)} %bitcast.71), custom_call_target="tpu_custom_call" | custom-call | flops 6442450944 | bytes 4194304 | tf_op jit(solution)/shard_map/attend/pallas_call | solution.py:85
  99.5 0.1 pad_maximum_fusion
  99.5 42.2 %all_to_all.56 = bf16[64,16,512]{2,1,0:T(8,128)(2,1)S(1)} all-to-all(bf16[64,16,512]{2,1,0:T(8,128)(2,1)S(1)} %bitcast.74), channel_id=1, replica_groups=mesh['dp'=2,'y'=4,'xh'=2,'z'=8,'mp'=2] {'y','xh','z'}, dimensions={0} | all-to-all | bytes 2097152 | tf_op jit(solution)/shard_map/all_to_all | solution.py:159
  141.7 0.2 convert_reduce_fusion
  141.9 0.1 reduce_sum.51
  142.1 0.1 mul.81
  142.1 0.1 mul.76
  142.3 14.6 %all_to_all.57 = bf16[16,16,512]{2,1,0:T(8,128)(2,1)S(1)} all-to-all(bf16[16,16,512]{2,1,0:T(8,128)(2,1)S(1)} %broadcast_in_dim.69), channel_id=1, replica_groups=mesh['dp'=2,'y'=4,'xh'=2,'z'=8,'mp'=2] {'xh','z'}, dimensions={0} | all-to-all | bytes 524288 | tf_op jit(solution)/shard_map/all_to_all | solution.py:124
  156.8 0.3 fusion
  157.2 14.1 %all_to_all.58 = bf16[4,128,512]{2,1,0:T(8,128)(2,1)S(1)} all-to-all(bf16[4,128,512]{2,1,0:T(8,128)(2,1)S(1)} %bitcast.76), channel_id=1, replica_groups=mesh['dp'=2,'y'=4,'xh'=2,'z'=8,'mp'=2] {'y'}, dimensions={0} | all-to-all | bytes 1048576 | tf_op jit(solution)/shard_map/all_to_all | solution.py:171
  171.2 0.1 reduce_sum.52
  171.3 2.7 %collective-permute-start.7 = (bf16[128,512]{1,0:T(8,128)(2,1)S(1)}, bf16[128,512]{1,0:T(8,128)(2,1)S(1)}, u32[]{:S(2)}, u32[]{:S(2)}) collective-permute-start(bf16[128,512]{1,0:T(8,128)(2,1)S(1)} %reduce_sum.52), channel_id=1, source_target_pairs={{0,128},{128,0},{1,129},{129,1},{2,130},{130,2},{3,131},{131,3},{4... | collective-permute-start | bytes 393224 | tf_op jit(solution)/shard_map/ppermute | solution.py:106
  174.0 8.5 %all-gather.2.cloned.1.call-done = bf16[8192,512]{1,0:T(8,128)(2,1)} async-done(((bf16[128,512]{1,0:T(8,128)(2,1)}), bf16[8192,512]{1,0:T(8,128)(2,1)}) %all-gather.2.cloned.1.call-update) | async-done | bytes 8388624 | tf_op jit(solution)/shard_map/all_gather | solution.py:141
  182.6 5.7 %convolution_convert_fusion = bf16[16,8192]{1,0:T(8,128)(2,1)S(1)} fusion(bf16[8192,512]{1,0:T(8,128)(2,1)} %all-gather.2.cloned.1.call-done, bf16[16,256]{1,0:T(8,128)(2,1)S(1)} %slice.40, bf16[16,256]{1,0:T(8,128)(2,1)S(1)} %fusion.3), kind=kOutput, calls=%fused_computation | convolution fusion | flops 134381568 | bytes 8667136 | tf_op jit(solution)/shard_map/jc,dc->jd/dot_general | solution.py:167
  188.2 2.2 %collective-permute-start.6 = (bf16[16,8192]{1,0:T(8,128)(2,1)S(1)}, bf16[16,8192]{1,0:T(8,128)(2,1)S(1)}, u32[]{:S(2)}, u32[]{:S(2)}) collective-permute-start(bf16[16,8192]{1,0:T(8,128)(2,1)S(1)} %convolution_convert_fusion), channel_id=1, source_target_pairs={{0,1},{1,0},{2,3},{3,2},{4,5},{5,4},{6,7},{7,6},{8,9},{9,8},{10,11... | collective-permute-start | bytes 786440 | tf_op jit(solution)/shard_map/ppermute | solution.py:106
  190.5 0.0 collective-permute-done.7
  190.5 0.7 fusion.5
  191.2 0.4 collective-permute-done.6
  191.6 0.8 fusion.1
  (29 shorter events, 0.4 us)
Async XLA Ops:
  7.2 75.1 %copy-start = (bf16[1,256,2048]{2,1,0:T(8,128)(2,1)S(1)}, bf16[1,256,2048]{2,1,0:T(8,128)(2,1)}, u32[]{:S(2)}) copy-start(bf16[1,256,2048]{2,1,0:T(8,128)(2,1)} %param.5) | copy-start | bytes 3145732
  7.2 75.1 %copy-start.1 = (bf16[1,256,2048]{2,1,0:T(8,128)(2,1)S(1)}, bf16[1,256,2048]{2,1,0:T(8,128)(2,1)}, u32[]{:S(2)}) copy-start(bf16[1,256,2048]{2,1,0:T(8,128)(2,1)} %param.9) | copy-start | bytes 3145732
  7.2 175.4 %all-gather.2.cloned.1.call-start = ((), (), s32[]{:S(2)}) async-start(), calls=%async_computation.6 | async-start | bytes 8519680 | tf_op jit(solution)/shard_map/all_gather | solution.py:141
  9.1 0.7 copy-start.2
  9.7 19.0 %collective-permute-start = (bf16[128,512]{1,0:T(8,128)(2,1)}, bf16[128,512]{1,0:T(8,128)(2,1)S(1)}, u32[]{:S(2)}, u32[]{:S(2)}) collective-permute-start(bf16[128,512]{1,0:T(8,128)(2,1)} %copy-done.2), channel_id=1, source_target_pairs={{0,32},{32,64},{64,96},{96,0},{1,33},{33,65},{65,97},{97,1},{2,34}... | collective-permute-start | bytes 393224 | tf_op jit(solution)/shard_map/ppermute | solution.py:110
  11.9 16.8 %collective-permute-start.1 = (bf16[128,512]{1,0:T(8,128)(2,1)}, bf16[128,512]{1,0:T(8,128)(2,1)S(1)}, u32[]{:S(2)}, u32[]{:S(2)}) collective-permute-start(bf16[128,512]{1,0:T(8,128)(2,1)} %copy-done.2), channel_id=1, source_target_pairs={{0,96},{32,0},{64,32},{96,64},{1,97},{33,1},{65,33},{97,65},{2,98}... | collective-permute-start | bytes 393224 | tf_op jit(solution)/shard_map/ppermute | solution.py:110
  13.5 15.3 %collective-permute-start.2 = (bf16[128,512]{1,0:T(8,128)(2,1)}, bf16[128,512]{1,0:T(8,128)(2,1)S(1)}, u32[]{:S(2)}, u32[]{:S(2)}) collective-permute-start(bf16[128,512]{1,0:T(8,128)(2,1)} %copy-done.2), channel_id=1, source_target_pairs={{0,64},{32,96},{64,0},{96,32},{1,65},{33,97},{65,1},{97,33},{2,66}... | collective-permute-start | bytes 393224 | tf_op jit(solution)/shard_map/ppermute | solution.py:110
  17.0 20.0 %all-to-all-start = ((bf16[16,16,512]{2,1,0:T(8,128)(2,1)}), bf16[16,16,512]{2,1,0:T(8,128)(2,1)S(1)}, u32[]{:S(2)}, u32[]{:S(2)}) async-start(bf16[16,16,512]{2,1,0:T(8,128)(2,1)} %all_to_all.36), calls=%async_computation | async-start | bytes 524288 | tf_op jit(solution)/shard_map/all_to_all | solution.py:145
  69.2 7.1 %collective-permute-start.3 = (bf16[256,512]{1,0:T(8,128)(2,1)S(1)}, bf16[256,512]{1,0:T(8,128)(2,1)S(1)}, u32[]{:S(2)}, u32[]{:S(2)}) collective-permute-start(bf16[256,512]{1,0:T(8,128)(2,1)S(1)} %bitcast.78), channel_id=1, source_target_pairs={{0,32},{32,64},{64,96},{96,0},{1,33},{33,65},{65,97},{97,1},{2,34}... | collective-permute-start | bytes 786440 | tf_op jit(solution)/shard_map/ppermute | solution.py:110
  69.2 9.8 %collective-permute-start.4 = (bf16[256,512]{1,0:T(8,128)(2,1)S(1)}, bf16[256,512]{1,0:T(8,128)(2,1)S(1)}, u32[]{:S(2)}, u32[]{:S(2)}) collective-permute-start(bf16[256,512]{1,0:T(8,128)(2,1)S(1)} %bitcast.79), channel_id=1, source_target_pairs={{0,96},{32,0},{64,32},{96,64},{1,97},{33,1},{65,33},{97,65},{2,98}... | collective-permute-start | bytes 786440 | tf_op jit(solution)/shard_map/ppermute | solution.py:110
  71.9 10.4 %collective-permute-start.5 = (bf16[256,512]{1,0:T(8,128)(2,1)S(1)}, bf16[256,512]{1,0:T(8,128)(2,1)S(1)}, u32[]{:S(2)}, u32[]{:S(2)}) collective-permute-start(bf16[256,512]{1,0:T(8,128)(2,1)S(1)} %bitcast.80), channel_id=1, source_target_pairs={{0,64},{32,96},{64,0},{96,32},{1,65},{33,97},{65,1},{97,33},{2,66}... | collective-permute-start | bytes 786440 | tf_op jit(solution)/shard_map/ppermute | solution.py:110
  171.3 19.1 %collective-permute-start.7 = (bf16[128,512]{1,0:T(8,128)(2,1)S(1)}, bf16[128,512]{1,0:T(8,128)(2,1)S(1)}, u32[]{:S(2)}, u32[]{:S(2)}) collective-permute-start(bf16[128,512]{1,0:T(8,128)(2,1)S(1)} %reduce_sum.52), channel_id=1, source_target_pairs={{0,128},{128,0},{1,129},{129,1},{2,130},{130,2},{3,131},{131,3},{4... | collective-permute-start | bytes 393224 | tf_op jit(solution)/shard_map/ppermute | solution.py:106
  188.2 3.4 %collective-permute-start.6 = (bf16[16,8192]{1,0:T(8,128)(2,1)S(1)}, bf16[16,8192]{1,0:T(8,128)(2,1)S(1)}, u32[]{:S(2)}, u32[]{:S(2)}) collective-permute-start(bf16[16,8192]{1,0:T(8,128)(2,1)S(1)} %convolution_convert_fusion), channel_id=1, source_target_pairs={{0,1},{1,0},{2,3},{3,2},{4,5},{5,4},{6,7},{7,6},{8,9},{9,8},{10,11... | collective-permute-start | bytes 786440 | tf_op jit(solution)/shard_map/ppermute | solution.py:106
Sparse Core Ops, SparseCore 0:
  12.2 170.2 all-gather.1

commit v2 on v1

v2 whole, which is shorter than its diff:
```python
import functools
import math

import jax
import jax.numpy as jnp
from jax import lax
from jax.experimental import pallas as pl
from jax.experimental.pallas import tpu as pltpu
from jax.sharding import Mesh
from jax.sharding import PartitionSpec as P

HEAD = 128
EPS = 1e-5
SCALE = HEAD**-0.5
F32 = jnp.float32
BF = jnp.bfloat16
NT = ((1,), (1,))
NN = ((1,), (0,))
TN = ((0,), (0,))
PARTS = (("y", 4), ("xh", 2), ("z", 8))
SEQ = ("y", "xh", "z")
COL = ("xh", "z")
Y_COUNT = 4
COL_COUNT = 16
VMEM = 48 * 1024 * 1024


def dot(a, b, dims):
    return lax.dot_general(a, b, (dims, ((), ())), preferred_element_type=F32)


def whole():
    return pl.BlockSpec(memory_space=pltpu.VMEM)


def back(by):
    return lax.rem(lax.axis_index("y") + Y_COUNT - by, Y_COUNT)


def pack_kernel(vision_ref, key_ref, value_ref, columns_ref, weights_ref):
    count = vision_ref.shape[0]
    wide = key_ref.shape[0]
    for by in range(Y_COUNT):
        start = back(by) * (COL_COUNT * wide)
        for j in range(COL_COUNT):
            columns_ref[j * count : (j + 1) * count, by * wide : (by + 1) * wide] = vision_ref[
                :, pl.ds(pl.multiple_of(start + j * wide, wide), wide)
            ]
    for head in range(key_ref.shape[1] // HEAD):
        cols = slice(head * HEAD, (head + 1) * HEAD)
        weights_ref[:, 2 * head * HEAD : (2 * head + 1) * HEAD] = key_ref[:, cols]
        weights_ref[:, (2 * head + 1) * HEAD : (2 * head + 2) * HEAD] = value_ref[:, cols]


def pack(own_rows, key_matrix, value_matrix):
    count, model_width = own_rows.shape
    weight_rows, kv_width = key_matrix.shape
    return pl.pallas_call(
        pack_kernel,
        in_specs=[whole()] * 3,
        out_specs=[whole()] * 2,
        out_shape=[
            jax.ShapeDtypeStruct((COL_COUNT * count, Y_COUNT * weight_rows), BF),
            jax.ShapeDtypeStruct((weight_rows, 2 * kv_width), BF),
        ],
        name="pack",
    )(own_rows, key_matrix, value_matrix)


def project_kernel(vision_ref, *refs):
    part_ref = refs[-1]
    total = None
    for by, weights_ref in enumerate(refs[:-1]):
        wide = weights_ref.shape[0]
        term = dot(vision_ref[:, by * wide : (by + 1) * wide], weights_ref[...], NN)
        total = term if total is None else total + term
    part_ref[...] = total.astype(BF)


def project(vision_block, weights):
    return pl.pallas_call(
        project_kernel,
        in_specs=[whole()] * 5,
        out_specs=whole(),
        out_shape=jax.ShapeDtypeStruct((vision_block.shape[0], weights[0].shape[1]), BF),
        name="project",
    )(vision_block, *weights)


def tail_kernel(vision_ref, grad_ref, *refs):
    weights, vision_part, parts = refs[:Y_COUNT], refs[Y_COUNT], refs[Y_COUNT + 1 :]
    grad = grad_ref[...]
    for by in range(Y_COUNT):
        wide = weights[by].shape[0]
        cols = slice(by * wide, (by + 1) * wide)
        vision_part[:, cols] = dot(grad, weights[by][...], NT).astype(BF)
        parts[by][...] = dot(vision_ref[:, cols], grad, TN).astype(BF)


def tail(vision_block, grad_block, weights):
    out = pl.pallas_call(
        tail_kernel,
        in_specs=[whole()] * 6,
        out_specs=[whole()] * 5,
        out_shape=[jax.ShapeDtypeStruct(vision_block.shape, BF)]
        + [jax.ShapeDtypeStruct(weights[0].shape, BF)] * Y_COUNT,
        name="tail",
    )(vision_block, grad_block, *weights)
    return out[0], out[1:]


def unpack_kernel(mine_ref, other_ref, out_ref):
    count = out_ref.shape[0]
    wide = mine_ref.shape[1] // Y_COUNT
    for by in range(Y_COUNT):
        start = back(by) * (COL_COUNT * wide)
        for j in range(COL_COUNT):
            place = (slice(j * count, (j + 1) * count), slice(by * wide, (by + 1) * wide))
            total = mine_ref[place].astype(F32) + other_ref[place].astype(F32)
            out_ref[:, pl.ds(pl.multiple_of(start + j * wide, wide), wide)] = total.astype(BF)


def unpack(mine, other):
    count = mine.shape[0] // COL_COUNT
    return pl.pallas_call(
        unpack_kernel,
        in_specs=[whole()] * 2,
        out_specs=whole(),
        out_shape=jax.ShapeDtypeStruct((count, COL_COUNT * mine.shape[1]), BF),
        name="unpack",
    )(mine, other)


def attend_one(query, cotangent, key_rows, value_rows):
    query_f = query.astype(F32)
    factor = lax.rsqrt(jnp.mean(query_f * query_f, axis=-1, keepdims=True) + EPS)
    query_norm = (query_f * factor).astype(BF)
    scores = dot(query_norm, key_rows, NT)
    expo = jnp.exp2(scores * (SCALE * math.log2(math.e)))
    inverse = 1.0 / jnp.sum(expo, axis=1, keepdims=True)
    expo_low = expo.astype(BF)
    out = dot(expo_low, value_rows, NN) * inverse
    scaled = cotangent.astype(F32) * inverse
    scaled_low = scaled.astype(BF)
    score_grad = dot(scaled_low, value_rows, NT)
    delta = jnp.sum(scaled * out, axis=1, keepdims=True)
    logit_grad = (expo * (score_grad - delta)).astype(BF)
    norm_grad = dot(logit_grad, key_rows, NN) * SCALE
    key_grad = dot(logit_grad, query_norm, TN)
    value_grad = dot(expo_low, scaled_low, TN)
    inner = jnp.mean(query_f * norm_grad, axis=-1, keepdims=True)
    d_query = factor * norm_grad - query_f * (factor * factor * factor) * inner
    return out.astype(BF), d_query.astype(BF), key_grad, value_grad


def attend_kernel(heads, steps, aliased, q_ref, c_ref, *refs):
    blocks = refs[:Y_COUNT]
    refs = refs[Y_COUNT + aliased :]
    o_ref, dq_ref = refs[:2]
    grads = refs[2 : 2 + Y_COUNT]
    keys, values, dk_sum, dv_sum = refs[2 + Y_COUNT :]
    step = pl.program_id(0)
    count = blocks[0].shape[0]

    @pl.when(step == 0)
    def _():
        dk_sum[...] = jnp.zeros_like(dk_sum)
        dv_sum[...] = jnp.zeros_like(dv_sum)
        for by in range(Y_COUNT):
            keys[by * count : (by + 1) * count, :] = blocks[by][:, :HEAD]
            values[by * count : (by + 1) * count, :] = blocks[by][:, HEAD:]

    key_rows = keys[...]
    value_rows = values[...]
    for head in range(heads):
        cols = slice(head * HEAD, (head + 1) * HEAD)
        out, d_query, key_grad, value_grad = attend_one(q_ref[:, cols], c_ref[:, cols], key_rows, value_rows)
        o_ref[:, cols] = out
        dq_ref[:, cols] = d_query
        dk_sum[...] += key_grad
        dv_sum[...] += value_grad

    @pl.when(step == steps - 1)
    def _():
        for by in range(Y_COUNT):
            rows = slice(by * count, (by + 1) * count)
            grads[by][:, :HEAD] = (dk_sum[rows, :] * SCALE).astype(BF)
            grads[by][:, HEAD:] = dv_sum[rows, :].astype(BF)


def attend(queries, cotangent, blocks, kv_head, kv_heads, before, heads=2):
    rows, width = queries.shape
    count = blocks[0].shape[0]
    steps = width // HEAD // kv_heads // heads
    q_spec = pl.BlockSpec((rows, heads * HEAD), lambda g: (0, kv_head * steps + g))
    b_spec = pl.BlockSpec((count, 2 * HEAD), lambda g: (0, 0))
    any_spec = pl.BlockSpec(memory_space=pl.ANY)
    vis_total = Y_COUNT * count
    flops = 12 * rows * (width // kv_heads) * vis_total
    out = pl.pallas_call(
        functools.partial(attend_kernel, heads, steps, len(before)),
        grid=(steps,),
        in_specs=[q_spec, q_spec] + [b_spec] * Y_COUNT + [any_spec] * len(before),
        out_specs=[q_spec, q_spec] + [b_spec] * Y_COUNT,
        out_shape=[jax.ShapeDtypeStruct((rows, width), BF)] * 2
        + [jax.ShapeDtypeStruct((count, 2 * HEAD), BF)] * Y_COUNT,
        scratch_shapes=[pltpu.VMEM((vis_total, HEAD), BF)] * 2 + [pltpu.VMEM((vis_total, HEAD), F32)] * 2,
        input_output_aliases={2 + Y_COUNT + i: i for i in range(len(before))},
        compiler_params=pltpu.CompilerParams(vmem_limit_bytes=VMEM, dimension_semantics=("arbitrary",)),
        cost_estimate=pl.CostEstimate(
            flops=flops, bytes_accessed=4 * rows * width, transcendentals=rows * (width // HEAD // kv_heads) * vis_total
        ),
        name="attend",
    )(queries, cotangent, *blocks, *before)
    return out[:2], out[2:]


def swap(x, axis):
    return lax.ppermute(x, axis, [(0, 1), (1, 0)])


def shift(x, by):
    return x if by == 0 else lax.ppermute(x, "y", [(i, (i + by) % Y_COUNT) for i in range(Y_COUNT)])


def from_behind(x):
    return [shift(x, by) for by in range(Y_COUNT)]


def sum_behind(pieces):
    return sum(shift(piece, Y_COUNT - by if by else 0).astype(F32) for by, piece in enumerate(pieces))


def gather_col(x):
    copies = jnp.broadcast_to(x[None], (COL_COUNT,) + x.shape).reshape((COL_COUNT * x.shape[0],) + x.shape[1:])
    return lax.all_to_all(copies, COL, 0, 0, tiled=True)


def sum_col(x):
    count = x.shape[0] // COL_COUNT
    parts = lax.all_to_all(x, COL, 0, 0, tiled=True)
    return jnp.sum(parts.reshape((COL_COUNT, count) + x.shape[1:]).astype(F32), axis=0)


def body(queries, vision, key_matrix, value_matrix, output_cotangent):
    kv_heads = key_matrix.shape[1] // HEAD
    own_rows = vision[0]

    columns, weights = pack(own_rows, key_matrix, value_matrix)
    vision_block = lax.all_to_all(columns, COL, 0, 0, tiled=True)
    weight_blocks = from_behind(weights)
    raw_own = sum_col(project(vision_block, weight_blocks))
    heads = [(raw_own[:, 2 * a * HEAD : (2 * a + 1) * HEAD], raw_own[:, (2 * a + 1) * HEAD : 2 * (a + 1) * HEAD]) for a in range(kv_heads)]

    factors = [lax.rsqrt(jnp.mean(key * key, axis=-1, keepdims=True) + EPS) for key, _ in heads]
    kv_own = [x for (key, value), factor in zip(heads, factors) for x in (key * factor, value)]
    kv_own = jnp.concatenate(kv_own, axis=1).astype(BF)
    kv_block = gather_col(kv_own)

    done = []
    sums = []
    head_blocks = [from_behind(kv_block[:, 2 * a * HEAD : 2 * (a + 1) * HEAD]) for a in range(kv_heads)]
    for kv_head in range(kv_heads):
        done, grads = attend(queries[0], output_cotangent[0], head_blocks[kv_head], kv_head, kv_heads, done)
        sums.append(sum_behind(grads))
    attended, d_queries = done

    kv_grad = sum_col(jnp.concatenate(sums, axis=1).astype(BF))
    raw_grad = []
    for a, ((key, _), factor) in enumerate(zip(heads, factors)):
        upstream = kv_grad[:, 2 * a * HEAD : (2 * a + 1) * HEAD]
        inner = jnp.mean(key * upstream, axis=-1, keepdims=True)
        raw_grad.append(factor * upstream - key * (factor * factor * factor) * inner)
        raw_grad.append(kv_grad[:, (2 * a + 1) * HEAD : 2 * (a + 1) * HEAD])
    raw_grad = jnp.concatenate(raw_grad, axis=1).astype(BF)

    grad_block = gather_col(raw_grad)
    vision_part, weight_parts = tail(vision_block, grad_block, weight_blocks)
    vision_own = lax.all_to_all(vision_part, COL, 0, 0, tiled=True)
    d_vision = unpack(vision_own, swap(vision_own, "mp"))

    weight_sum = sum_behind(weight_parts).astype(BF)
    total = weight_sum.astype(F32) + swap(weight_sum, "dp").astype(F32)
    pieces = [total[:, c * HEAD : (c + 1) * HEAD] for c in range(2 * kv_heads)]
    d_k = jnp.concatenate(pieces[0::2], axis=1)
    d_v = jnp.concatenate(pieces[1::2], axis=1)
    return attended[None], d_queries[None], d_vision[None], d_k, d_v


def solution(mesh):
    fine = Mesh(mesh.devices.reshape((2,) + tuple(n for _, n in PARTS) + (2,)), ("dp",) + SEQ + ("mp",))
    rows = P("dp", SEQ, "mp")
    vision = P("dp", SEQ, None)
    weights = P(SEQ, "mp")
    return jax.shard_map(
        body,
        mesh=fine,
        in_specs=(rows, vision, weights, weights, rows),
        out_specs=(rows, rows, vision, weights, weights),
        check_vma=False,
    )
```

time: 200 us -> 161 us (0.81)
  blocking collectives: 102 us -> 58.6 us
  starting transfers between devices: 24.1 us -> 51.9 us
  between operations: 14.4 us -> 0.82 us
  Pallas kernels: 17.1 us -> 26 us
  waiting for transfers between devices: 26.9 us -> 19.1 us
  matrix products: 6.3 us -> 0 us
  local copies, waits for them, and re-layouts: 6.6 us -> 1.51 us
    all_to_all x3 -> x2, blocking collectives: 73 us -> 31.3 us  [sum_col(): parts = lax.all_to_all(x, COL, 0, 0, tiled=True)]
    ppermute x6 -> x18, starting transfers between devices: 8.37 us -> 21.1 us  [shift(): lax.ppermute(x, 'y', [(i, (i + by) % Y_COUNT) for i in range(Y_COUNT)])]
    ppermute x2, starting transfers between devices: 4.91 us -> 15 us  [swap(): return lax.ppermute(x, axis, [(0, 1), (1, 0)])]
    pallas_call x1 -> x6, Pallas kernels: 17.1 us -> 26 us  [the longest x2 17.6 us: attend(): pl.pallas_call(functools.partial(attend_kernel, heads, steps, len(before)...]
    all_gather x1 -> x0, waiting for transfers between devices: 8.55 us -> none  [body(): full_weights = lax.all_gather(weights, SEQ, axis=0, tiled=True)]
    all_to_all x1, waiting for transfers between devices: 8.13 us -> 0.79 us  [body(): vision_block = lax.all_to_all(columns, COL, 0, 0, tiled=True)]
    dot_general x3 -> x0, matrix products: 6.3 us -> none  [the longest x1 5.66 us: body(): jnp.einsum('jc,dc->jd', raw_grad, full_weights, preferred_element_type=F32)]
    all_to_all x0 -> x1, starting transfers between devices: none -> 3.98 us  [body(): vision_own = lax.all_to_all(vision_part, COL, 0, 0, tiled=True)]
  transfers between devices with their start and end apart: 10 -> 22, of which waited for: 6 -> 10; matrix products, arithmetic and copies ran while one was open for 5% -> 1% of each run, Pallas kernels for 9% -> 11%
where the time goes in v2:
time: 161 us; the launch traced here: 160 us
  blocking collectives  58.6 us (36%)
  starting transfers between devices  51.9 us (32%)
  Pallas kernels  26 us (16%)
  waiting for transfers between devices  19.1 us (12%)
  other arithmetic  2.09 us (1%)
    all_to_all x2, blocking collectives, sum_col(): parts = lax.all_to_all(x, COL, 0, 0, tiled=True)  31.3 us
    all_to_all x2, blocking collectives, gather_col(): return lax.all_to_all(copies, COL, 0, 0, tiled=True)  27.3 us
    ppermute x18, starting transfers between devices, shift(): lax.ppermute(x, 'y', [(i, (i + by) % Y_COUNT) for i in range(Y_COUNT)])  21.1 us
    pallas_call x2, Pallas kernels, attend(): pl.pallas_call(functools.partial(attend_kernel, heads, steps, len(before)...  17.6 us
    ppermute x2, starting transfers between devices, swap(): return lax.ppermute(x, axis, [(0, 1), (1, 0)])  15 us
    ppermute x18, waiting for transfers between devices, shift(): lax.ppermute(x, 'y', [(i, (i + by) % Y_COUNT) for i in range(Y_COUNT)])  11.9 us
    all_to_all x1, starting transfers between devices, body(): vision_block = lax.all_to_all(columns, COL, 0, 0, tiled=True)  11.7 us
    ppermute x2, waiting for transfers between devices, swap(): return lax.ppermute(x, axis, [(0, 1), (1, 0)])  4.19 us
  transfers between devices with their start and end apart: 22, of which 10 were waited for; matrix products, arithmetic and copies ran while one was open for 1% of the time, Pallas kernels for 11%

profile of v2, /device:TPU:1, one launch (start us, length us, event | category | flops | bytes accessed | tf_op | source)
XLA Modules:
  0.0 160.0 jit_solution(17131777094811369920)
XLA Ops:
  0.6 1.8 %pack.1 = (bf16[256,512]{1,0:T(8,128)(2,1)}, bf16[128,512]{1,0:T(8,128)(2,1)}) custom-call(bf16[16,8192]{1,0:T(8,128)(2,1)} %bitcast.29, bf16[128,256]{1,0:T(8,128)(2,1)} %key_ref.1, bf16[128,256]{1,0:T(8,128)(2,1)} %value_ref.1), custom_call_target="tpu_custom_call" | custom-call | tf_op jit(solution)/shard_map/pack/pallas_call | solution.py:58
  2.5 11.7 %all-to-all-start = ((bf16[16,16,512]{2,1,0:T(8,128)(2,1)}), bf16[16,16,512]{2,1,0:T(8,128)(2,1)S(1)}, u32[]{:S(2)}, u32[]{:S(2)}) async-start(bf16[16,16,512]{2,1,0:T(8,128)(2,1)} %bitcast.31), calls=%async_computation | async-start | bytes 524288 | tf_op jit(solution)/shard_map/all_to_all | solution.py:250
  14.2 1.4 collective-permute-start
  15.6 2.6 %collective-permute-start.1 = (bf16[128,512]{1,0:T(8,128)(2,1)S(1)}, bf16[128,512]{1,0:T(8,128)(2,1)S(1)}, u32[]{:S(2)}, u32[]{:S(2)}) collective-permute-start(bf16[128,512]{1,0:T(8,128)(2,1)S(1)} %copy-done.4), channel_id=1, source_target_pairs={{0,64},{32,96},{64,0},{96,32},{1,65},{33,97},{65,1},{97,33},{2,66}... | collective-permute-start | bytes 393224 | tf_op jit(solution)/shard_map/ppermute | solution.py:223
  18.2 1.1 collective-permute-start.2
  19.3 0.4 collective-permute-done.refs_1_
  19.7 3.9 %collective-permute-done.1.refs_2_ = bf16[128,512]{1,0:T(8,128)(2,1)S(1)} collective-permute-done((bf16[128,512]{1,0:T(8,128)(2,1)S(1)}, bf16[128,512]{1,0:T(8,128)(2,1)S(1)}, u32[]{:S(2)}, u32[]{:S(2)}) %collective-permute-start.1) | collective-permute-done | bytes 131104 | tf_op jit(solution)/shard_map/ppermute | solution.py:223
  23.6 0.8 all-to-all-done
  24.4 0.7 copy-done.2
  25.1 2.3 %project.1 = bf16[256,512]{1,0:T(8,128)(2,1)} custom-call(bf16[256,512]{1,0:T(8,128)(2,1)} %bitcast.19, bf16[128,512]{1,0:T(8,128)(2,1)} %get-tuple-element.25.refs_0_, bf16[128,512]{1,0:T(8,128)(2,1)} %copy-done.5, bf16[128,512]{1,0:T(8,128)(2,1)} %copy-done.6, bf16[128,512]{1,0:T(8,128)(2,1)} %copy-done.7), custom_call_target="tpu_custom_call" | custom-call | tf_op jit(solution)/shard_map/project/pallas_call | solution.py:81
  27.4 17.8 %all_to_all.54 = bf16[16,16,512]{2,1,0:T(8,128)(2,1)S(1)} all-to-all(bf16[16,16,512]{2,1,0:T(8,128)(2,1)} %bitcast.25), channel_id=1, replica_groups=mesh['dp'=2,'y'=4,'xh'=2,'z'=8,'mp'=2] {'xh','z'}, dimensions={0} | all-to-all | bytes 524288 | tf_op jit(solution)/shard_map/all_to_all | solution.py:241
  45.2 0.1 multiply_reduce_fusion.3
  45.4 0.1 multiply_convert_fusion.1
  45.5 13.9 %all_to_all.55 = bf16[16,16,512]{2,1,0:T(8,128)(2,1)S(1)} all-to-all(bf16[16,16,512]{2,1,0:T(8,128)(2,1)S(1)} %broadcast_in_dim.10), channel_id=1, replica_groups=mesh['dp'=2,'y'=4,'xh'=2,'z'=8,'mp'=2] {'xh','z'}, dimensions={0} | all-to-all | bytes 524288 | tf_op jit(solution)/shard_map/all_to_all | solution.py:236
  59.4 0.2 collective-permute-start.6
  59.7 4.1 %collective-permute-start.7 = (bf16[256,256]{1,0:T(8,128)(2,1)S(1)}, bf16[256,256]{1,0:T(8,128)(2,1)S(1)}, u32[]{:S(2)}, u32[]{:S(2)}) collective-permute-start(bf16[256,256]{1,0:T(8,128)(2,1)S(1)} %get-tuple-element.51.refs_0_), channel_id=1, source_target_pairs={{0,64},{32,96},{64,0},{96,32},{1,65},{33,97},{65,1},{97,33},{2,66}... | collective-permute-start | bytes 393224 | tf_op jit(solution)/shard_map/ppermute | solution.py:223
  63.8 1.5 collective-permute-start.3
  65.3 2.4 %collective-permute-start.5 = (bf16[256,256]{1,0:T(8,128)(2,1)S(1)}, bf16[256,256]{1,0:T(8,128)(2,1)S(1)}, u32[]{:S(2)}, u32[]{:S(2)}) collective-permute-start(bf16[256,256]{1,0:T(8,128)(2,1)S(1)} %get-tuple-element.52.refs_0_), channel_id=1, source_target_pairs={{0,96},{32,0},{64,32},{96,64},{1,97},{33,1},{65,33},{97,65},{2,98}... | collective-permute-start | bytes 393224 | tf_op jit(solution)/shard_map/ppermute | solution.py:223
  67.7 8.8 %attend.2 = (bf16[256,2048]{1,0:T(8,128)(2,1)}, bf16[256,2048]{1,0:T(8,128)(2,1)}, bf16[256,256]{1,0:T(8,128)(2,1)S(1)}, bf16[256,256]{1,0:T(8,128)(2,1)S(1)}, b...) custom-call(bf16[256,2048]{1,0:T(8,128)(2,1)S(1)} %bitcast.15, bf16[256,2048]{1,0:T(8,128)(2,1)S(1)} %bitcast.17, ...), custom_call_target="tpu_custom_call" | custom-call | flops 3221225472 | bytes 2097152 | tf_op jit(solution)/shard_map/attend/pallas_call | solution.py:200
  76.5 1.9 %collective-permute-start.10 = (bf16[256,256]{1,0:T(8,128)(2,1)S(1)}, bf16[256,256]{1,0:T(8,128)(2,1)S(1)}, u32[]{:S(2)}, u32[]{:S(2)}) collective-permute-start(bf16[256,256]{1,0:T(8,128)(2,1)S(1)} %get-tuple-element.32), channel_id=1, source_target_pairs={{0,64},{32,96},{64,0},{96,32},{1,65},{33,97},{65,1},{97,33},{2,66}... | collective-permute-start | bytes 393224 | tf_op jit(solution)/shard_map/ppermute | solution.py:223
  78.3 0.5 collective-permute-start.11
  78.8 2.2 %collective-permute-start.9 = (bf16[256,256]{1,0:T(8,128)(2,1)S(1)}, bf16[256,256]{1,0:T(8,128)(2,1)S(1)}, u32[]{:S(2)}, u32[]{:S(2)}) collective-permute-start(bf16[256,256]{1,0:T(8,128)(2,1)S(1)} %get-tuple-element.31), channel_id=1, source_target_pairs={{0,96},{32,0},{64,32},{96,64},{1,97},{33,1},{65,33},{97,65},{2,98}... | collective-permute-start | bytes 393224 | tf_op jit(solution)/shard_map/ppermute | solution.py:223
  81.0 8.8 %attend.3 = (bf16[256,2048]{1,0:T(8,128)(2,1)}, bf16[256,2048]{1,0:T(8,128)(2,1)}, bf16[256,256]{1,0:T(8,128)(2,1)S(1)}, bf16[256,256]{1,0:T(8,128)(2,1)S(1)}, b...) custom-call(bf16[256,2048]{1,0:T(8,128)(2,1)S(1)} %bitcast.16, ...), custom_call_target="tpu_custom_call", output_to_operand_aliasing={{0}: (6, {}), {1}: (7, {})} | custom-call | flops 3221225472 | bytes 2097152 | tf_op jit(solution)/shard_map/attend/pallas_call | solution.py:200
  89.8 1.0 collective-permute-start.13
  90.8 0.4 collective-permute-start.14
  91.3 0.1 add_convert_fusion.2
  91.4 2.3 %collective-permute-done.12 = bf16[256,256]{1,0:T(8,128)(2,1)S(1)} collective-permute-done((bf16[256,256]{1,0:T(8,128)(2,1)S(1)}, bf16[256,256]{1,0:T(8,128)(2,1)S(1)}, u32[]{:S(2)}, u32[]{:S(2)}) %collective-permute-start.12) | collective-permute-done | bytes 131104 | tf_op jit(solution)/shard_map/ppermute | solution.py:223
  93.6 1.6 collective-permute-done.13
  95.2 1.3 collective-permute-done.14
  96.7 13.5 %all_to_all.56 = bf16[16,16,512]{2,1,0:T(8,128)(2,1)S(1)} all-to-all(bf16[16,16,512]{2,1,0:T(8,128)(2,1)S(1)} %pad_maximum_fusion), channel_id=1, replica_groups=mesh['dp'=2,'y'=4,'xh'=2,'z'=8,'mp'=2] {'xh','z'}, dimensions={0} | all-to-all | bytes 524288 | tf_op jit(solution)/shard_map/all_to_all | solution.py:241
  110.2 0.1 multiply_reduce_fusion.1
  110.3 0.1 subtract_convert_fusion.1
  110.5 13.4 %all_to_all.57 = bf16[16,16,512]{2,1,0:T(8,128)(2,1)} all-to-all(bf16[16,16,512]{2,1,0:T(8,128)(2,1)S(1)} %broadcast_in_dim.13), channel_id=1, replica_groups=mesh['dp'=2,'y'=4,'xh'=2,'z'=8,'mp'=2] {'xh','z'}, dimensions={0} | all-to-all | bytes 524288 | tf_op jit(solution)/shard_map/all_to_all | solution.py:236
  123.8 2.5 %tail.1 = (bf16[256,512]{1,0:T(8,128)(2,1)}, bf16[128,512]{1,0:T(8,128)(2,1)}, bf16[128,512]{1,0:T(8,128)(2,1)}, bf16[128,512]{1,0:T(8,128)(2,1)}, bf16[128,512]{1,0:T(8,128)(2,1)}) custom-call(bf16[256,512]{1,0:T(8,128)(2,1)} %bitcast.20, bf16[256,512]{1,0:T(8,128)(2,1)} %bitcast.24, bf16[128,512]{1,0:T(8,128)(2,1)} %get-tuple-element.25.refs_0_, ...), custom_call_target="tpu_custom_call" | custom-call | tf_op jit(solution)/shard_map/tail/pallas_call | solution.py:101
  126.4 0.8 collective-permute-start.16
  127.2 0.8 collective-permute-start.17
  128.0 0.2 collective-permute-start.18
  128.2 4.0 %all-to-all-start.5 = ((bf16[16,16,512]{2,1,0:T(8,128)(2,1)}), bf16[16,16,512]{2,1,0:T(8,128)(2,1)S(1)}, u32[]{:S(2)}, u32[]{:S(2)}) async-start(bf16[16,16,512]{2,1,0:T(8,128)(2,1)} %bitcast.30), calls=%async_computation.5 | async-start | bytes 524288 | tf_op jit(solution)/shard_map/all_to_all | solution.py:279
  132.2 0.9 collective-permute-done.17
  133.1 1.4 collective-permute-done.18
  134.6 0.4 collective-permute-start.19
  135.0 4.2 %collective-permute-done.19 = bf16[128,512]{1,0:T(8,128)(2,1)S(1)} collective-permute-done((bf16[128,512]{1,0:T(8,128)(2,1)S(1)}, bf16[128,512]{1,0:T(8,128)(2,1)S(1)}, u32[]{:S(2)}, u32[]{:S(2)}) %collective-permute-start.19) | collective-permute-done | bytes 131104 | tf_op jit(solution)/shard_map/ppermute | solution.py:219
  139.2 2.2 %all-to-all-done.5 = bf16[16,16,512]{2,1,0:T(8,128)(2,1)S(1)} async-done(((bf16[16,16,512]{2,1,0:T(8,128)(2,1)}), bf16[16,16,512]{2,1,0:T(8,128)(2,1)S(1)}, u32[]{:S(2)}, u32[]{:S(2)}) %all-to-all-start.5) | async-done | bytes 262176 | tf_op jit(solution)/shard_map/all_to_all | solution.py:279
  141.5 14.6 %collective-permute-start.15 = (bf16[256,512]{1,0:T(8,128)(2,1)S(1)}, bf16[256,512]{1,0:T(8,128)(2,1)S(1)}, u32[]{:S(2)}, u32[]{:S(2)}) collective-permute-start(bf16[256,512]{1,0:T(8,128)(2,1)S(1)} %bitcast.21), channel_id=1, source_target_pairs={{0,1},{1,0},{2,3},{3,2},{4,5},{5,4},{6,7},{7,6},{8,9},{9,8},{10,11... | collective-permute-start | bytes 786440 | tf_op jit(solution)/shard_map/ppermute | solution.py:219
  156.1 0.7 pad_maximum_fusion.2
  156.8 0.7 pad_maximum_fusion.1
  157.5 0.7 copy-done.8
  158.2 1.8 %unpack.1 = bf16[16,8192]{1,0:T(8,128)(2,1)} custom-call(bf16[256,512]{1,0:T(8,128)(2,1)} %bitcast.22, bf16[256,512]{1,0:T(8,128)(2,1)} %copy-done.8), custom_call_target="tpu_custom_call" | custom-call | tf_op jit(solution)/shard_map/unpack/pallas_call | solution.py:125
  (52 shorter events, 0.5 us)
Async XLA Ops:
  2.5 11.7 %copy-start.4 = (bf16[128,512]{1,0:T(8,128)(2,1)S(1)}, bf16[128,512]{1,0:T(8,128)(2,1)}, u32[]{:S(2)}) copy-start(bf16[128,512]{1,0:T(8,128)(2,1)} %get-tuple-element.25.refs_0_) | copy-start | bytes 393220
  2.5 22.0 %all-to-all-start = ((bf16[16,16,512]{2,1,0:T(8,128)(2,1)}), bf16[16,16,512]{2,1,0:T(8,128)(2,1)S(1)}, u32[]{:S(2)}, u32[]{:S(2)}) async-start(bf16[16,16,512]{2,1,0:T(8,128)(2,1)} %bitcast.31), calls=%async_computation | async-start | bytes 524288 | tf_op jit(solution)/shard_map/all_to_all | solution.py:250
  14.2 5.5 %collective-permute-start = (bf16[128,512]{1,0:T(8,128)(2,1)S(1)}, bf16[128,512]{1,0:T(8,128)(2,1)S(1)}, u32[]{:S(2)}, u32[]{:S(2)}) collective-permute-start(bf16[128,512]{1,0:T(8,128)(2,1)S(1)} %copy-done.4), channel_id=1, source_target_pairs={{0,32},{32,64},{64,96},{96,0},{1,33},{33,65},{65,97},{97,1},{2,34}... | collective-permute-start | bytes 393224 | tf_op jit(solution)/shard_map/ppermute | solution.py:223
  15.6 8.0 %collective-permute-start.1 = (bf16[128,512]{1,0:T(8,128)(2,1)S(1)}, bf16[128,512]{1,0:T(8,128)(2,1)S(1)}, u32[]{:S(2)}, u32[]{:S(2)}) collective-permute-start(bf16[128,512]{1,0:T(8,128)(2,1)S(1)} %copy-done.4), channel_id=1, source_target_pairs={{0,64},{32,96},{64,0},{96,32},{1,65},{33,97},{65,1},{97,33},{2,66}... | collective-permute-start | bytes 393224 | tf_op jit(solution)/shard_map/ppermute | solution.py:223
  18.2 5.4 %collective-permute-start.2 = (bf16[128,512]{1,0:T(8,128)(2,1)S(1)}, bf16[128,512]{1,0:T(8,128)(2,1)S(1)}, u32[]{:S(2)}, u32[]{:S(2)}) collective-permute-start(bf16[128,512]{1,0:T(8,128)(2,1)S(1)} %copy-done.4), channel_id=1, source_target_pairs={{0,96},{32,0},{64,32},{96,64},{1,97},{33,1},{65,33},{97,65},{2,98}... | collective-permute-start | bytes 393224 | tf_op jit(solution)/shard_map/ppermute | solution.py:223
  19.7 4.8 %copy-start.5 = (bf16[128,512]{1,0:T(8,128)(2,1)}, bf16[128,512]{1,0:T(8,128)(2,1)S(1)}, u32[]{:S(2)}) copy-start(bf16[128,512]{1,0:T(8,128)(2,1)S(1)} %collective-permute-done.refs_1_) | copy-start | bytes 393220
  23.6 0.8 copy-start.6
  23.6 0.8 copy-start.7
  24.4 0.7 copy-start.2
  27.4 40.3 %copy-start = (bf16[1,256,2048]{2,1,0:T(8,128)(2,1)S(1)}, bf16[1,256,2048]{2,1,0:T(8,128)(2,1)}, u32[]{:S(2)}) copy-start(bf16[1,256,2048]{2,1,0:T(8,128)(2,1)} %param.5) | copy-start | bytes 3145732
  27.4 40.3 %copy-start.1 = (bf16[1,256,2048]{2,1,0:T(8,128)(2,1)S(1)}, bf16[1,256,2048]{2,1,0:T(8,128)(2,1)}, u32[]{:S(2)}) copy-start(bf16[1,256,2048]{2,1,0:T(8,128)(2,1)} %param.9) | copy-start | bytes 3145732
  59.4 5.8 %collective-permute-start.6 = (bf16[256,256]{1,0:T(8,128)(2,1)S(1)}, bf16[256,256]{1,0:T(8,128)(2,1)S(1)}, u32[]{:S(2)}, u32[]{:S(2)}) collective-permute-start(bf16[256,256]{1,0:T(8,128)(2,1)S(1)} %get-tuple-element.51.refs_0_), channel_id=1, source_target_pairs={{0,32},{32,64},{64,96},{96,0},{1,33},{33,65},{65,97},{97,1},{2,34}... | collective-permute-start | bytes 393224 | tf_op jit(solution)/shard_map/ppermute | solution.py:223
  59.7 8.0 %collective-permute-start.7 = (bf16[256,256]{1,0:T(8,128)(2,1)S(1)}, bf16[256,256]{1,0:T(8,128)(2,1)S(1)}, u32[]{:S(2)}, u32[]{:S(2)}) collective-permute-start(bf16[256,256]{1,0:T(8,128)(2,1)S(1)} %get-tuple-element.51.refs_0_), channel_id=1, source_target_pairs={{0,64},{32,96},{64,0},{96,32},{1,65},{33,97},{65,1},{97,33},{2,66}... | collective-permute-start | bytes 393224 | tf_op jit(solution)/shard_map/ppermute | solution.py:223
  63.8 3.9 %collective-permute-start.8 = (bf16[256,256]{1,0:T(8,128)(2,1)S(1)}, bf16[256,256]{1,0:T(8,128)(2,1)S(1)}, u32[]{:S(2)}, u32[]{:S(2)}) collective-permute-start(bf16[256,256]{1,0:T(8,128)(2,1)S(1)} %get-tuple-element.51.refs_0_), channel_id=1, source_target_pairs={{0,96},{32,0},{64,32},{96,64},{1,97},{33,1},{65,33},{97,65},{2,98}... | collective-permute-start | bytes 393224 | tf_op jit(solution)/shard_map/ppermute | solution.py:223
  63.8 15.0 %collective-permute-start.3 = (bf16[256,256]{1,0:T(8,128)(2,1)S(1)}, bf16[256,256]{1,0:T(8,128)(2,1)S(1)}, u32[]{:S(2)}, u32[]{:S(2)}) collective-permute-start(bf16[256,256]{1,0:T(8,128)(2,1)S(1)} %get-tuple-element.52.refs_0_), channel_id=1, source_target_pairs={{0,32},{32,64},{64,96},{96,0},{1,33},{33,65},{65,97},{97,1},{2,34}... | collective-permute-start | bytes 393224 | tf_op jit(solution)/shard_map/ppermute | solution.py:223
  65.3 15.8 %collective-permute-start.4 = (bf16[256,256]{1,0:T(8,128)(2,1)S(1)}, bf16[256,256]{1,0:T(8,128)(2,1)S(1)}, u32[]{:S(2)}, u32[]{:S(2)}) collective-permute-start(bf16[256,256]{1,0:T(8,128)(2,1)S(1)} %get-tuple-element.52.refs_0_), channel_id=1, source_target_pairs={{0,64},{32,96},{64,0},{96,32},{1,65},{33,97},{65,1},{97,33},{2,66}... | collective-permute-start | bytes 393224 | tf_op jit(solution)/shard_map/ppermute | solution.py:223
  65.3 15.8 %collective-permute-start.5 = (bf16[256,256]{1,0:T(8,128)(2,1)S(1)}, bf16[256,256]{1,0:T(8,128)(2,1)S(1)}, u32[]{:S(2)}, u32[]{:S(2)}) collective-permute-start(bf16[256,256]{1,0:T(8,128)(2,1)S(1)} %get-tuple-element.52.refs_0_), channel_id=1, source_target_pairs={{0,96},{32,0},{64,32},{96,64},{1,97},{33,1},{65,33},{97,65},{2,98}... | collective-permute-start | bytes 393224 | tf_op jit(solution)/shard_map/ppermute | solution.py:223
  76.5 14.4 %collective-permute-start.10 = (bf16[256,256]{1,0:T(8,128)(2,1)S(1)}, bf16[256,256]{1,0:T(8,128)(2,1)S(1)}, u32[]{:S(2)}, u32[]{:S(2)}) collective-permute-start(bf16[256,256]{1,0:T(8,128)(2,1)S(1)} %get-tuple-element.32), channel_id=1, source_target_pairs={{0,64},{32,96},{64,0},{96,32},{1,65},{33,97},{65,1},{97,33},{2,66}... | collective-permute-start | bytes 393224 | tf_op jit(solution)/shard_map/ppermute | solution.py:223
  78.3 12.9 %collective-permute-start.11 = (bf16[256,256]{1,0:T(8,128)(2,1)S(1)}, bf16[256,256]{1,0:T(8,128)(2,1)S(1)}, u32[]{:S(2)}, u32[]{:S(2)}) collective-permute-start(bf16[256,256]{1,0:T(8,128)(2,1)S(1)} %get-tuple-element.33), channel_id=1, source_target_pairs={{0,32},{32,64},{64,96},{96,0},{1,33},{33,65},{65,97},{97,1},{2,34}... | collective-permute-start | bytes 393224 | tf_op jit(solution)/shard_map/ppermute | solution.py:223
  78.8 12.5 %collective-permute-start.9 = (bf16[256,256]{1,0:T(8,128)(2,1)S(1)}, bf16[256,256]{1,0:T(8,128)(2,1)S(1)}, u32[]{:S(2)}, u32[]{:S(2)}) collective-permute-start(bf16[256,256]{1,0:T(8,128)(2,1)S(1)} %get-tuple-element.31), channel_id=1, source_target_pairs={{0,96},{32,0},{64,32},{96,64},{1,97},{33,1},{65,33},{97,65},{2,98}... | collective-permute-start | bytes 393224 | tf_op jit(solution)/shard_map/ppermute | solution.py:223
  89.8 3.8 %collective-permute-start.12 = (bf16[256,256]{1,0:T(8,128)(2,1)S(1)}, bf16[256,256]{1,0:T(8,128)(2,1)S(1)}, u32[]{:S(2)}, u32[]{:S(2)}) collective-permute-start(bf16[256,256]{1,0:T(8,128)(2,1)S(1)} %get-tuple-element.35), channel_id=1, source_target_pairs={{0,96},{32,0},{64,32},{96,64},{1,97},{33,1},{65,33},{97,65},{2,98}... | collective-permute-start | bytes 393224 | tf_op jit(solution)/shard_map/ppermute | solution.py:223
  89.8 5.4 %collective-permute-start.13 = (bf16[256,256]{1,0:T(8,128)(2,1)S(1)}, bf16[256,256]{1,0:T(8,128)(2,1)S(1)}, u32[]{:S(2)}, u32[]{:S(2)}) collective-permute-start(bf16[256,256]{1,0:T(8,128)(2,1)S(1)} %get-tuple-element.36), channel_id=1, source_target_pairs={{0,64},{32,96},{64,0},{96,32},{1,65},{33,97},{65,1},{97,33},{2,66}... | collective-permute-start | bytes 393224 | tf_op jit(solution)/shard_map/ppermute | solution.py:223
  90.8 5.7 %collective-permute-start.14 = (bf16[256,256]{1,0:T(8,128)(2,1)S(1)}, bf16[256,256]{1,0:T(8,128)(2,1)S(1)}, u32[]{:S(2)}, u32[]{:S(2)}) collective-permute-start(bf16[256,256]{1,0:T(8,128)(2,1)S(1)} %get-tuple-element.37), channel_id=1, source_target_pairs={{0,32},{32,64},{64,96},{96,0},{1,33},{33,65},{65,97},{97,1},{2,34}... | collective-permute-start | bytes 393224 | tf_op jit(solution)/shard_map/ppermute | solution.py:223
  126.4 5.8 %collective-permute-start.16 = (bf16[128,512]{1,0:T(8,128)(2,1)}, bf16[128,512]{1,0:T(8,128)(2,1)S(1)}, u32[]{:S(2)}, u32[]{:S(2)}) collective-permute-start(bf16[128,512]{1,0:T(8,128)(2,1)} %get-tuple-element.40), channel_id=1, source_target_pairs={{0,96},{32,0},{64,32},{96,64},{1,97},{33,1},{65,33},{97,65},{2,98}... | collective-permute-start | bytes 393224 | tf_op jit(solution)/shard_map/ppermute | solution.py:223
  127.2 5.9 %collective-permute-start.17 = (bf16[128,512]{1,0:T(8,128)(2,1)}, bf16[128,512]{1,0:T(8,128)(2,1)S(1)}, u32[]{:S(2)}, u32[]{:S(2)}) collective-permute-start(bf16[128,512]{1,0:T(8,128)(2,1)} %get-tuple-element.41), channel_id=1, source_target_pairs={{0,64},{32,96},{64,0},{96,32},{1,65},{33,97},{65,1},{97,33},{2,66}... | collective-permute-start | bytes 393224 | tf_op jit(solution)/shard_map/ppermute | solution.py:223
  128.0 6.5 %collective-permute-start.18 = (bf16[128,512]{1,0:T(8,128)(2,1)}, bf16[128,512]{1,0:T(8,128)(2,1)S(1)}, u32[]{:S(2)}, u32[]{:S(2)}) collective-permute-start(bf16[128,512]{1,0:T(8,128)(2,1)} %get-tuple-element.42), channel_id=1, source_target_pairs={{0,32},{32,64},{64,96},{96,0},{1,33},{33,65},{65,97},{97,1},{2,34}... | collective-permute-start | bytes 393224 | tf_op jit(solution)/shard_map/ppermute | solution.py:223
  128.2 6.3 %copy-start.9 = (bf16[128,512]{1,0:T(8,128)(2,1)S(1)}, bf16[128,512]{1,0:T(8,128)(2,1)}, u32[]{:S(2)}) copy-start(bf16[128,512]{1,0:T(8,128)(2,1)} %get-tuple-element.39) | copy-start | bytes 393220
  128.2 13.2 %all-to-all-start.5 = ((bf16[16,16,512]{2,1,0:T(8,128)(2,1)}), bf16[16,16,512]{2,1,0:T(8,128)(2,1)S(1)}, u32[]{:S(2)}, u32[]{:S(2)}) async-start(bf16[16,16,512]{2,1,0:T(8,128)(2,1)} %bitcast.30), calls=%async_computation.5 | async-start | bytes 524288 | tf_op jit(solution)/shard_map/all_to_all | solution.py:279
  134.6 4.6 %collective-permute-start.19 = (bf16[128,512]{1,0:T(8,128)(2,1)S(1)}, bf16[128,512]{1,0:T(8,128)(2,1)S(1)}, u32[]{:S(2)}, u32[]{:S(2)}) collective-permute-start(bf16[128,512]{1,0:T(8,128)(2,1)S(1)} %add_convert_fusion), channel_id=1, source_target_pairs={{0,128},{128,0},{1,129},{129,1},{2,130},{130,2},{3,131},{131,3},{4... | collective-permute-start | bytes 393224 | tf_op jit(solution)/shard_map/ppermute | solution.py:219
  141.5 14.6 %copy-start.3 = (bf16[16,16,512]{2,1,0:T(8,128)(2,1)}, bf16[16,16,512]{2,1,0:T(8,128)(2,1)S(1)}, u32[]{:S(2)}) copy-start(bf16[16,16,512]{2,1,0:T(8,128)(2,1)S(1)} %all-to-all-done.5) | copy-start | bytes 786436
  141.5 16.0 %collective-permute-start.15 = (bf16[256,512]{1,0:T(8,128)(2,1)S(1)}, bf16[256,512]{1,0:T(8,128)(2,1)S(1)}, u32[]{:S(2)}, u32[]{:S(2)}) collective-permute-start(bf16[256,512]{1,0:T(8,128)(2,1)S(1)} %bitcast.21), channel_id=1, source_target_pairs={{0,1},{1,0},{2,3},{3,2},{4,5},{5,4},{6,7},{7,6},{8,9},{9,8},{10,11... | collective-permute-start | bytes 786440 | tf_op jit(solution)/shard_map/ppermute | solution.py:219
  157.5 0.7 copy-start.8

commit v3 on v2

--- a/solution.py
+++ b/solution.py
@@ -22,7 +22,9 @@
 COL = ("xh", "z")
 Y_COUNT = 4
 COL_COUNT = 16
+FAR_FIRST = (2, 1, 3, 0)
 VMEM = 48 * 1024 * 1024
+HEADS_AT_ONCE = 8
 
 
 def dot(a, b, dims):
@@ -46,10 +48,9 @@
             columns_ref[j * count : (j + 1) * count, by * wide : (by + 1) * wide] = vision_ref[
                 :, pl.ds(pl.multiple_of(start + j * wide, wide), wide)
             ]
-    for head in range(key_ref.shape[1] // HEAD):
-        cols = slice(head * HEAD, (head + 1) * HEAD)
-        weights_ref[:, 2 * head * HEAD : (2 * head + 1) * HEAD] = key_ref[:, cols]
-        weights_ref[:, (2 * head + 1) * HEAD : (2 * head + 2) * HEAD] = value_ref[:, cols]
+    kv_width = key_ref.shape[1]
+    weights_ref[:, :kv_width] = key_ref[...]
+    weights_ref[:, kv_width:] = value_ref[...]
 
 
 def pack(own_rows, key_matrix, value_matrix):
@@ -65,48 +66,6 @@
         ],
         name="pack",
     )(own_rows, key_matrix, value_matrix)
-
-
-def project_kernel(vision_ref, *refs):
-    part_ref = refs[-1]
-    total = None
-    for by, weights_ref in enumerate(refs[:-1]):
-        wide = weights_ref.shape[0]
-        term = dot(vision_ref[:, by * wide : (by + 1) * wide], weights_ref[...], NN)
-        total = term if total is None else total + term
-    part_ref[...] = total.astype(BF)
-
-
-def project(vision_block, weights):
-    return pl.pallas_call(
-        project_kernel,
-        in_specs=[whole()] * 5,
-        out_specs=whole(),
-        out_shape=jax.ShapeDtypeStruct((vision_block.shape[0], weights[0].shape[1]), BF),
-        name="project",
-    )(vision_block, *weights)
-
-
-def tail_kernel(vision_ref, grad_ref, *refs):
-    weights, vision_part, parts = refs[:Y_COUNT], refs[Y_COUNT], refs[Y_COUNT + 1 :]
-    grad = grad_ref[...]
-    for by in range(Y_COUNT):
-        wide = weights[by].shape[0]
-        cols = slice(by * wide, (by + 1) * wide)
-        vision_part[:, cols] = dot(grad, weights[by][...], NT).astype(BF)
-        parts[by][...] = dot(vision_ref[:, cols], grad, TN).astype(BF)
-
-
-def tail(vision_block, grad_block, weights):
-    out = pl.pallas_call(
-        tail_kernel,
-        in_specs=[whole()] * 6,
-        out_specs=[whole()] * 5,
-        out_shape=[jax.ShapeDtypeStruct(vision_block.shape, BF)]
-        + [jax.ShapeDtypeStruct(weights[0].shape, BF)] * Y_COUNT,
-        name="tail",
-    )(vision_block, grad_block, *weights)
-    return out[0], out[1:]
 
 
 def unpack_kernel(mine_ref, other_ref, out_ref):
@@ -188,20 +147,19 @@
             grads[by][:, HEAD:] = dv_sum[rows, :].astype(BF)
 
 
-def attend(queries, cotangent, blocks, kv_head, kv_heads, before, heads=2):
+def attend(queries, cotangent, blocks, kv_head, kv_heads, before, heads=HEADS_AT_ONCE):
     rows, width = queries.shape
     count = blocks[0].shape[0]
     steps = width // HEAD // kv_heads // heads
     q_spec = pl.BlockSpec((rows, heads * HEAD), lambda g: (0, kv_head * steps + g))
-    b_spec = pl.BlockSpec((count, 2 * HEAD), lambda g: (0, 0))
     any_spec = pl.BlockSpec(memory_space=pl.ANY)
     vis_total = Y_COUNT * count
     flops = 12 * rows * (width // kv_heads) * vis_total
     out = pl.pallas_call(
         functools.partial(attend_kernel, heads, steps, len(before)),
         grid=(steps,),
-        in_specs=[q_spec, q_spec] + [b_spec] * Y_COUNT + [any_spec] * len(before),
-        out_specs=[q_spec, q_spec] + [b_spec] * Y_COUNT,
+        in_specs=[q_spec, q_spec] + [whole()] * Y_COUNT + [any_spec] * len(before),
+        out_specs=[q_spec, q_spec] + [whole()] * Y_COUNT,
         out_shape=[jax.ShapeDtypeStruct((rows, width), BF)] * 2
         + [jax.ShapeDtypeStruct((count, 2 * HEAD), BF)] * Y_COUNT,
         scratch_shapes=[pltpu.VMEM((vis_total, HEAD), BF)] * 2 + [pltpu.VMEM((vis_total, HEAD), F32)] * 2,
@@ -224,11 +182,12 @@
 
 
 def from_behind(x):
-    return [shift(x, by) for by in range(Y_COUNT)]
+    pieces = {by: shift(x, by) for by in FAR_FIRST}
+    return [pieces[by] for by in range(Y_COUNT)]
 
 
 def sum_behind(pieces):
-    return sum(shift(piece, Y_COUNT - by if by else 0).astype(F32) for by, piece in enumerate(pieces))
+    return sum(shift(pieces[by], (Y_COUNT - by) % Y_COUNT).astype(F32) for by in FAR_FIRST)
 
 
 def gather_col(x):
@@ -248,12 +207,13 @@
 
     columns, weights = pack(own_rows, key_matrix, value_matrix)
     vision_block = lax.all_to_all(columns, COL, 0, 0, tiled=True)
-    weight_blocks = from_behind(weights)
-    raw_own = sum_col(project(vision_block, weight_blocks))
-    heads = [(raw_own[:, 2 * a * HEAD : (2 * a + 1) * HEAD], raw_own[:, (2 * a + 1) * HEAD : 2 * (a + 1) * HEAD]) for a in range(kv_heads)]
-
-    factors = [lax.rsqrt(jnp.mean(key * key, axis=-1, keepdims=True) + EPS) for key, _ in heads]
-    kv_own = [x for (key, value), factor in zip(heads, factors) for x in (key * factor, value)]
+    weight_block = jnp.concatenate(from_behind(weights), axis=0)
+    raw_own = sum_col(dot(vision_block, weight_block, NN).astype(BF))
+    keys = [raw_own[:, a * HEAD : (a + 1) * HEAD] for a in range(kv_heads)]
+    values = [raw_own[:, (kv_heads + a) * HEAD : (kv_heads + a + 1) * HEAD] for a in range(kv_heads)]
+
+    factors = [lax.rsqrt(jnp.mean(key * key, axis=-1, keepdims=True) + EPS) for key in keys]
+    kv_own = [x for key, factor, value in zip(keys, factors, values) for x in (key * factor, value)]
     kv_own = jnp.concatenate(kv_own, axis=1).astype(BF)
     kv_block = gather_col(kv_own)
 
@@ -267,23 +227,26 @@
 
     kv_grad = sum_col(jnp.concatenate(sums, axis=1).astype(BF))
     raw_grad = []
-    for a, ((key, _), factor) in enumerate(zip(heads, factors)):
+    for a, (key, factor) in enumerate(zip(keys, factors)):
         upstream = kv_grad[:, 2 * a * HEAD : (2 * a + 1) * HEAD]
         inner = jnp.mean(key * upstream, axis=-1, keepdims=True)
         raw_grad.append(factor * upstream - key * (factor * factor * factor) * inner)
-        raw_grad.append(kv_grad[:, (2 * a + 1) * HEAD : 2 * (a + 1) * HEAD])
+    raw_grad += [kv_grad[:, (2 * a + 1) * HEAD : 2 * (a + 1) * HEAD] for a in range(kv_heads)]
     raw_grad = jnp.concatenate(raw_grad, axis=1).astype(BF)
 
     grad_block = gather_col(raw_grad)
-    vision_part, weight_parts = tail(vision_block, grad_block, weight_blocks)
+    vision_part = dot(grad_block, weight_block, NT).astype(BF)
     vision_own = lax.all_to_all(vision_part, COL, 0, 0, tiled=True)
     d_vision = unpack(vision_own, swap(vision_own, "mp"))
 
-    weight_sum = sum_behind(weight_parts).astype(BF)
+    wide = weights.shape[0]
+    weight_part = [
+        dot(vision_block[:, by * wide : (by + 1) * wide], grad_block, TN).astype(BF) for by in range(Y_COUNT)
+    ]
+    weight_sum = sum_behind(weight_part).astype(BF)
     total = weight_sum.astype(F32) + swap(weight_sum, "dp").astype(F32)
-    pieces = [total[:, c * HEAD : (c + 1) * HEAD] for c in range(2 * kv_heads)]
-    d_k = jnp.concatenate(pieces[0::2], axis=1)
-    d_v = jnp.concatenate(pieces[1::2], axis=1)
+    kv_width = key_matrix.shape[1]
+    d_k, d_v = total[:, :kv_width], total[:, kv_width:]
     return attended[None], d_queries[None], d_vision[None], d_k, d_v
 
 

time: 161 us -> 156 us (0.969)
  Pallas kernels: 26 us -> 19.5 us
  matrix products: 0 us -> 2.16 us
    all_to_all x1, waiting for transfers between devices: 2.24 us -> 8.22 us  [body(): vision_own = lax.all_to_all(vision_part, COL, 0, 0, tiled=True)]
    pallas_call x2 -> x0, Pallas kernels: 4.81 us -> none  [the longest x1 2.53 us: tail(): pl.pallas_call(tail_kernel, in_specs=[whole()] * 6, out_specs=[whole()] *...]
    ppermute x2, waiting for transfers between devices: 4.19 us -> 0.4 us  [swap(): return lax.ppermute(x, axis, [(0, 1), (1, 0)])]
    dot_general x0 -> x6, matrix products: none -> 2.16 us  [dot(): return lax.dot_general(a, b, (dims, ((), ())), preferred_element_type=F32)]
    ppermute x18, waiting for transfers between devices: 11.9 us -> 9.72 us  [shift(): lax.ppermute(x, 'y', [(i, (i + by) % Y_COUNT) for i in range(Y_COUNT)])]
    pallas_call x2, Pallas kernels: 17.6 us -> 15.9 us  [attend(): pl.pallas_call(functools.partial(attend_kernel, heads, steps, len(before)...]
  transfers between devices with their start and end apart: 22 -> 22, of which waited for: 10 -> 9; matrix products, arithmetic and copies ran while one was open for 1% -> 1% of each run, Pallas kernels for 11% -> 10%
where the time goes in v3:
time: 156 us; the launch traced here: 155 us
  blocking collectives  58 us (37%)
  starting transfers between devices  53.2 us (34%)
  Pallas kernels  19.5 us (12%)
  waiting for transfers between devices  19.1 us (12%)
  matrix products  2.16 us (1%)
    all_to_all x2, blocking collectives, sum_col(): parts = lax.all_to_all(x, COL, 0, 0, tiled=True)  30.9 us
    all_to_all x2, blocking collectives, gather_col(): return lax.all_to_all(copies, COL, 0, 0, tiled=True)  27.2 us
    ppermute x18, starting transfers between devices, shift(): lax.ppermute(x, 'y', [(i, (i + by) % Y_COUNT) for i in range(Y_COUNT)])  22.3 us
    pallas_call x2, Pallas kernels, attend(): pl.pallas_call(functools.partial(attend_kernel, heads, steps, len(before)...  15.9 us
    ppermute x2, starting transfers between devices, swap(): return lax.ppermute(x, axis, [(0, 1), (1, 0)])  15.2 us
    all_to_all x1, starting transfers between devices, body(): vision_block = lax.all_to_all(columns, COL, 0, 0, tiled=True)  11.7 us
    ppermute x18, waiting for transfers between devices, shift(): lax.ppermute(x, 'y', [(i, (i + by) % Y_COUNT) for i in range(Y_COUNT)])  9.72 us
    all_to_all x1, waiting for transfers between devices, body(): vision_own = lax.all_to_all(vision_part, COL, 0, 0, tiled=True)  8.22 us
  transfers between devices with their start and end apart: 22, of which 9 were waited for; matrix products, arithmetic and copies ran while one was open for 1% of the time, Pallas kernels for 10%

profile of v3, /device:TPU:1, one launch (start us, length us, event | category | flops | bytes accessed | tf_op | source)
XLA Modules:
  0.0 155.1 jit_solution(8888408911316456868)
XLA Ops:
  0.6 1.8 %pack.1 = (bf16[256,512]{1,0:T(8,128)(2,1)}, bf16[128,512]{1,0:T(8,128)(2,1)}) custom-call(bf16[16,8192]{1,0:T(8,128)(2,1)} %bitcast.44, bf16[128,256]{1,0:T(8,128)(2,1)} %key_ref.1, bf16[128,256]{1,0:T(8,128)(2,1)} %value_ref.1), custom_call_target="tpu_custom_call" | custom-call | tf_op jit(solution)/shard_map/pack/pallas_call | solution.py:59
  2.5 11.7 %all-to-all-start = ((bf16[16,16,512]{2,1,0:T(8,128)(2,1)}), bf16[16,16,512]{2,1,0:T(8,128)(2,1)S(1)}, u32[]{:S(2)}, u32[]{:S(2)}) async-start(bf16[16,16,512]{2,1,0:T(8,128)(2,1)} %bitcast.45), calls=%async_computation | async-start | bytes 524288 | tf_op jit(solution)/shard_map/all_to_all | solution.py:209
  14.2 1.4 collective-permute-start
  15.6 2.6 %collective-permute-start.1 = (bf16[128,512]{1,0:T(8,128)(2,1)S(1)}, bf16[128,512]{1,0:T(8,128)(2,1)S(1)}, u32[]{:S(2)}, u32[]{:S(2)}) collective-permute-start(bf16[128,512]{1,0:T(8,128)(2,1)S(1)} %copy-done.4), channel_id=1, source_target_pairs={{0,64},{32,96},{64,0},{96,32},{1,65},{33,97},{65,1},{97,33},{2,66}... | collective-permute-start | bytes 393224 | tf_op jit(solution)/shard_map/ppermute | solution.py:181
  18.2 1.1 collective-permute-start.2
  19.3 0.4 collective-permute-done
  19.7 3.9 %collective-permute-done.1 = bf16[128,512]{1,0:T(8,128)(2,1)S(1)} collective-permute-done((bf16[128,512]{1,0:T(8,128)(2,1)S(1)}, bf16[128,512]{1,0:T(8,128)(2,1)S(1)}, u32[]{:S(2)}, u32[]{:S(2)}) %collective-permute-start.1) | collective-permute-done | bytes 131104 | tf_op jit(solution)/shard_map/ppermute | solution.py:181
  23.6 0.8 all-to-all-done
  24.4 0.3 convolution_convert_fusion.1
  24.7 17.6 %all_to_all.56 = bf16[16,16,512]{2,1,0:T(8,128)(2,1)S(1)} all-to-all(bf16[16,16,512]{2,1,0:T(8,128)(2,1)S(1)} %bitcast.40), channel_id=1, replica_groups=mesh['dp'=2,'y'=4,'xh'=2,'z'=8,'mp'=2] {'xh','z'}, dimensions={0} | all-to-all | bytes 524288 | tf_op jit(solution)/shard_map/all_to_all | solution.py:200
  42.3 0.1 multiply_reduce_fusion.3
  42.5 0.1 multiply_convert_fusion.1
  42.6 14.0 %all_to_all.57 = bf16[16,16,512]{2,1,0:T(8,128)(2,1)S(1)} all-to-all(bf16[16,16,512]{2,1,0:T(8,128)(2,1)S(1)} %broadcast_in_dim.10), channel_id=1, replica_groups=mesh['dp'=2,'y'=4,'xh'=2,'z'=8,'mp'=2] {'xh','z'}, dimensions={0} | all-to-all | bytes 524288 | tf_op jit(solution)/shard_map/all_to_all | solution.py:195
  56.6 0.2 collective-permute-start.6
  56.8 4.1 %collective-permute-start.7 = (bf16[256,256]{1,0:T(8,128)(2,1)S(1)}, bf16[256,256]{1,0:T(8,128)(2,1)S(1)}, u32[]{:S(2)}, u32[]{:S(2)}) collective-permute-start(bf16[256,256]{1,0:T(8,128)(2,1)S(1)} %get-tuple-element.39.refs_0_), channel_id=1, source_target_pairs={{0,64},{32,96},{64,0},{96,32},{1,65},{33,97},{65,1},{97,33},{2,66}... | collective-permute-start | bytes 393224 | tf_op jit(solution)/shard_map/ppermute | solution.py:181
  60.9 1.5 collective-permute-start.3
  62.4 2.4 %collective-permute-start.5 = (bf16[256,256]{1,0:T(8,128)(2,1)S(1)}, bf16[256,256]{1,0:T(8,128)(2,1)S(1)}, u32[]{:S(2)}, u32[]{:S(2)}) collective-permute-start(bf16[256,256]{1,0:T(8,128)(2,1)S(1)} %get-tuple-element.40.refs_0_), channel_id=1, source_target_pairs={{0,96},{32,0},{64,32},{96,64},{1,97},{33,1},{65,33},{97,65},{2,98}... | collective-permute-start | bytes 393224 | tf_op jit(solution)/shard_map/ppermute | solution.py:181
  64.8 8.0 %attend.2 = (bf16[256,2048]{1,0:T(8,128)(2,1)}, bf16[256,2048]{1,0:T(8,128)(2,1)}, bf16[256,256]{1,0:T(8,128)(2,1)S(1)}, bf16[256,256]{1,0:T(8,128)(2,1)S(1)}, b...) custom-call(bf16[256,2048]{1,0:T(8,128)(2,1)S(1)} %bitcast.23, bf16[256,2048]{1,0:T(8,128)(2,1)S(1)} %bitcast.25, ...), custom_call_target="tpu_custom_call" | custom-call | flops 3221225472 | bytes 2097152 | tf_op jit(solution)/shard_map/attend/pallas_call | solution.py:158
  72.8 1.8 %collective-permute-start.10 = (bf16[256,256]{1,0:T(8,128)(2,1)S(1)}, bf16[256,256]{1,0:T(8,128)(2,1)S(1)}, u32[]{:S(2)}, u32[]{:S(2)}) collective-permute-start(bf16[256,256]{1,0:T(8,128)(2,1)S(1)} %get-tuple-element.26), channel_id=1, source_target_pairs={{0,96},{32,0},{64,32},{96,64},{1,97},{33,1},{65,33},{97,65},{2,98}... | collective-permute-start | bytes 393224 | tf_op jit(solution)/shard_map/ppermute | solution.py:181
  74.5 1.6 %collective-permute-start.9 = (bf16[256,256]{1,0:T(8,128)(2,1)S(1)}, bf16[256,256]{1,0:T(8,128)(2,1)S(1)}, u32[]{:S(2)}, u32[]{:S(2)}) collective-permute-start(bf16[256,256]{1,0:T(8,128)(2,1)S(1)} %get-tuple-element.25), channel_id=1, source_target_pairs={{0,64},{32,96},{64,0},{96,32},{1,65},{33,97},{65,1},{97,33},{2,66}... | collective-permute-start | bytes 393224 | tf_op jit(solution)/shard_map/ppermute | solution.py:181
  76.1 8.0 %attend.3 = (bf16[256,2048]{1,0:T(8,128)(2,1)}, bf16[256,2048]{1,0:T(8,128)(2,1)}, bf16[256,256]{1,0:T(8,128)(2,1)S(1)}, bf16[256,256]{1,0:T(8,128)(2,1)S(1)}, b...) custom-call(bf16[256,2048]{1,0:T(8,128)(2,1)S(1)} %bitcast.24, ...), custom_call_target="tpu_custom_call", output_to_operand_aliasing={{0}: (6, {}), {1}: (7, {})} | custom-call | flops 3221225472 | bytes 2097152 | tf_op jit(solution)/shard_map/attend/pallas_call | solution.py:158
  84.1 1.4 collective-permute-start.12
  85.5 2.7 %collective-permute-start.13 = (bf16[256,256]{1,0:T(8,128)(2,1)S(1)}, bf16[256,256]{1,0:T(8,128)(2,1)S(1)}, u32[]{:S(2)}, u32[]{:S(2)}) collective-permute-start(bf16[256,256]{1,0:T(8,128)(2,1)S(1)} %get-tuple-element.30), channel_id=1, source_target_pairs={{0,96},{32,0},{64,32},{96,64},{1,97},{33,1},{65,33},{97,65},{2,98}... | collective-permute-start | bytes 393224 | tf_op jit(solution)/shard_map/ppermute | solution.py:181
  88.2 0.1 add_convert_fusion.2
  88.2 1.2 collective-permute-done.12
  89.4 1.5 collective-permute-done.13
  90.9 2.2 %collective-permute-done.14 = bf16[256,256]{1,0:T(8,128)(2,1)S(1)} collective-permute-done((bf16[256,256]{1,0:T(8,128)(2,1)S(1)}, bf16[256,256]{1,0:T(8,128)(2,1)S(1)}, u32[]{:S(2)}, u32[]{:S(2)}) %collective-permute-start.14) | collective-permute-done | bytes 131104 | tf_op jit(solution)/shard_map/ppermute | solution.py:181
  93.3 13.3 %all_to_all.58 = bf16[16,16,512]{2,1,0:T(8,128)(2,1)S(1)} all-to-all(bf16[16,16,512]{2,1,0:T(8,128)(2,1)S(1)} %pad_maximum_fusion), channel_id=1, replica_groups=mesh['dp'=2,'y'=4,'xh'=2,'z'=8,'mp'=2] {'xh','z'}, dimensions={0} | all-to-all | bytes 524288 | tf_op jit(solution)/shard_map/all_to_all | solution.py:200
  106.6 0.1 multiply_reduce_fusion.1
  106.8 0.1 subtract_convert_fusion.1
  106.9 13.2 %all_to_all.59 = bf16[16,16,512]{2,1,0:T(8,128)(2,1)S(1)} all-to-all(bf16[16,16,512]{2,1,0:T(8,128)(2,1)S(1)} %broadcast_in_dim.13), channel_id=1, replica_groups=mesh['dp'=2,'y'=4,'xh'=2,'z'=8,'mp'=2] {'xh','z'}, dimensions={0} | all-to-all | bytes 524288 | tf_op jit(solution)/shard_map/all_to_all | solution.py:195
  120.1 0.2 convolution_convert_fusion.5
  120.3 0.2 convolution_convert_fusion.4
  120.5 0.2 convolution_convert_fusion.3
  120.7 0.1 collective-permute-start.16
  120.8 1.4 collective-permute-start.17
  122.3 0.1 collective-permute-start.18
  122.4 1.0 convolution_convert_fusion
  123.4 4.0 %all-to-all-start.5 = ((bf16[16,16,512]{2,1,0:T(8,128)(2,1)}), bf16[16,16,512]{2,1,0:T(8,128)(2,1)S(1)}, u32[]{:S(2)}, u32[]{:S(2)}) async-start(bf16[16,16,512]{2,1,0:T(8,128)(2,1)} %bitcast.12), calls=%async_computation.5 | async-start | bytes 524288 | tf_op jit(solution)/shard_map/all_to_all | solution.py:239
  127.4 0.4 collective-permute-done.18
  127.8 0.2 add_convert_fusion
  128.0 0.4 collective-permute-start.19
  128.4 8.2 %all-to-all-done.5 = bf16[16,16,512]{2,1,0:T(8,128)(2,1)S(1)} async-done(((bf16[16,16,512]{2,1,0:T(8,128)(2,1)}), bf16[16,16,512]{2,1,0:T(8,128)(2,1)S(1)}, u32[]{:S(2)}, u32[]{:S(2)}) %all-to-all-start.5) | async-done | bytes 262176 | tf_op jit(solution)/shard_map/all_to_all | solution.py:239
  136.7 14.8 %collective-permute-start.15 = (bf16[256,512]{1,0:T(8,128)(2,1)S(1)}, bf16[256,512]{1,0:T(8,128)(2,1)S(1)}, u32[]{:S(2)}, u32[]{:S(2)}) collective-permute-start(bf16[256,512]{1,0:T(8,128)(2,1)S(1)} %bitcast.37), channel_id=1, source_target_pairs={{0,1},{1,0},{2,3},{3,2},{4,5},{5,4},{6,7},{7,6},{8,9},{9,8},{10,11... | collective-permute-start | bytes 786440 | tf_op jit(solution)/shard_map/ppermute | solution.py:177
  151.5 0.7 fusion.7
  152.2 0.4 collective-permute-done.15.other_ref
  152.6 0.7 copy-done.3
  153.3 1.8 %unpack.1 = bf16[16,8192]{1,0:T(8,128)(2,1)} custom-call(bf16[256,512]{1,0:T(8,128)(2,1)} %bitcast.38, bf16[256,512]{1,0:T(8,128)(2,1)} %copy-done.3), custom_call_target="tpu_custom_call" | custom-call | tf_op jit(solution)/shard_map/unpack/pallas_call | solution.py:84
  (47 shorter events, 0.4 us)
Async XLA Ops:
  2.5 11.7 %copy-start.4 = (bf16[128,512]{1,0:T(8,128)(2,1)S(1)}, bf16[128,512]{1,0:T(8,128)(2,1)}, u32[]{:S(2)}) copy-start(bf16[128,512]{1,0:T(8,128)(2,1)} %get-tuple-element.20) | copy-start | bytes 393220
  2.5 22.0 %all-to-all-start = ((bf16[16,16,512]{2,1,0:T(8,128)(2,1)}), bf16[16,16,512]{2,1,0:T(8,128)(2,1)S(1)}, u32[]{:S(2)}, u32[]{:S(2)}) async-start(bf16[16,16,512]{2,1,0:T(8,128)(2,1)} %bitcast.45), calls=%async_computation | async-start | bytes 524288 | tf_op jit(solution)/shard_map/all_to_all | solution.py:209
  14.2 5.5 %collective-permute-start = (bf16[128,512]{1,0:T(8,128)(2,1)S(1)}, bf16[128,512]{1,0:T(8,128)(2,1)S(1)}, u32[]{:S(2)}, u32[]{:S(2)}) collective-permute-start(bf16[128,512]{1,0:T(8,128)(2,1)S(1)} %copy-done.4), channel_id=1, source_target_pairs={{0,32},{32,64},{64,96},{96,0},{1,33},{33,65},{65,97},{97,1},{2,34}... | collective-permute-start | bytes 393224 | tf_op jit(solution)/shard_map/ppermute | solution.py:181
  15.6 8.0 %collective-permute-start.1 = (bf16[128,512]{1,0:T(8,128)(2,1)S(1)}, bf16[128,512]{1,0:T(8,128)(2,1)S(1)}, u32[]{:S(2)}, u32[]{:S(2)}) collective-permute-start(bf16[128,512]{1,0:T(8,128)(2,1)S(1)} %copy-done.4), channel_id=1, source_target_pairs={{0,64},{32,96},{64,0},{96,32},{1,65},{33,97},{65,1},{97,33},{2,66}... | collective-permute-start | bytes 393224 | tf_op jit(solution)/shard_map/ppermute | solution.py:181
  18.2 5.4 %collective-permute-start.2 = (bf16[128,512]{1,0:T(8,128)(2,1)S(1)}, bf16[128,512]{1,0:T(8,128)(2,1)S(1)}, u32[]{:S(2)}, u32[]{:S(2)}) collective-permute-start(bf16[128,512]{1,0:T(8,128)(2,1)S(1)} %copy-done.4), channel_id=1, source_target_pairs={{0,96},{32,0},{64,32},{96,64},{1,97},{33,1},{65,33},{97,65},{2,98}... | collective-permute-start | bytes 393224 | tf_op jit(solution)/shard_map/ppermute | solution.py:181
  24.7 40.1 %copy-start = (bf16[1,256,2048]{2,1,0:T(8,128)(2,1)S(1)}, bf16[1,256,2048]{2,1,0:T(8,128)(2,1)}, u32[]{:S(2)}) copy-start(bf16[1,256,2048]{2,1,0:T(8,128)(2,1)} %param.5) | copy-start | bytes 3145732
  24.7 40.1 %copy-start.1 = (bf16[1,256,2048]{2,1,0:T(8,128)(2,1)S(1)}, bf16[1,256,2048]{2,1,0:T(8,128)(2,1)}, u32[]{:S(2)}) copy-start(bf16[1,256,2048]{2,1,0:T(8,128)(2,1)} %param.9) | copy-start | bytes 3145732
  56.6 5.8 %collective-permute-start.6 = (bf16[256,256]{1,0:T(8,128)(2,1)S(1)}, bf16[256,256]{1,0:T(8,128)(2,1)S(1)}, u32[]{:S(2)}, u32[]{:S(2)}) collective-permute-start(bf16[256,256]{1,0:T(8,128)(2,1)S(1)} %get-tuple-element.39.refs_0_), channel_id=1, source_target_pairs={{0,32},{32,64},{64,96},{96,0},{1,33},{33,65},{65,97},{97,1},{2,34}... | collective-permute-start | bytes 393224 | tf_op jit(solution)/shard_map/ppermute | solution.py:181
  56.8 8.0 %collective-permute-start.7 = (bf16[256,256]{1,0:T(8,128)(2,1)S(1)}, bf16[256,256]{1,0:T(8,128)(2,1)S(1)}, u32[]{:S(2)}, u32[]{:S(2)}) collective-permute-start(bf16[256,256]{1,0:T(8,128)(2,1)S(1)} %get-tuple-element.39.refs_0_), channel_id=1, source_target_pairs={{0,64},{32,96},{64,0},{96,32},{1,65},{33,97},{65,1},{97,33},{2,66}... | collective-permute-start | bytes 393224 | tf_op jit(solution)/shard_map/ppermute | solution.py:181
  60.9 3.9 %collective-permute-start.8 = (bf16[256,256]{1,0:T(8,128)(2,1)S(1)}, bf16[256,256]{1,0:T(8,128)(2,1)S(1)}, u32[]{:S(2)}, u32[]{:S(2)}) collective-permute-start(bf16[256,256]{1,0:T(8,128)(2,1)S(1)} %get-tuple-element.39.refs_0_), channel_id=1, source_target_pairs={{0,96},{32,0},{64,32},{96,64},{1,97},{33,1},{65,33},{97,65},{2,98}... | collective-permute-start | bytes 393224 | tf_op jit(solution)/shard_map/ppermute | solution.py:181
  60.9 13.6 %collective-permute-start.3 = (bf16[256,256]{1,0:T(8,128)(2,1)S(1)}, bf16[256,256]{1,0:T(8,128)(2,1)S(1)}, u32[]{:S(2)}, u32[]{:S(2)}) collective-permute-start(bf16[256,256]{1,0:T(8,128)(2,1)S(1)} %get-tuple-element.40.refs_0_), channel_id=1, source_target_pairs={{0,32},{32,64},{64,96},{96,0},{1,33},{33,65},{65,97},{97,1},{2,34}... | collective-permute-start | bytes 393224 | tf_op jit(solution)/shard_map/ppermute | solution.py:181
  62.4 13.7 %collective-permute-start.4 = (bf16[256,256]{1,0:T(8,128)(2,1)S(1)}, bf16[256,256]{1,0:T(8,128)(2,1)S(1)}, u32[]{:S(2)}, u32[]{:S(2)}) collective-permute-start(bf16[256,256]{1,0:T(8,128)(2,1)S(1)} %get-tuple-element.40.refs_0_), channel_id=1, source_target_pairs={{0,64},{32,96},{64,0},{96,32},{1,65},{33,97},{65,1},{97,33},{2,66}... | collective-permute-start | bytes 393224 | tf_op jit(solution)/shard_map/ppermute | solution.py:181
  62.4 13.7 %collective-permute-start.5 = (bf16[256,256]{1,0:T(8,128)(2,1)S(1)}, bf16[256,256]{1,0:T(8,128)(2,1)S(1)}, u32[]{:S(2)}, u32[]{:S(2)}) collective-permute-start(bf16[256,256]{1,0:T(8,128)(2,1)S(1)} %get-tuple-element.40.refs_0_), channel_id=1, source_target_pairs={{0,96},{32,0},{64,32},{96,64},{1,97},{33,1},{65,33},{97,65},{2,98}... | collective-permute-start | bytes 393224 | tf_op jit(solution)/shard_map/ppermute | solution.py:181
  72.8 15.4 %collective-permute-start.10 = (bf16[256,256]{1,0:T(8,128)(2,1)S(1)}, bf16[256,256]{1,0:T(8,128)(2,1)S(1)}, u32[]{:S(2)}, u32[]{:S(2)}) collective-permute-start(bf16[256,256]{1,0:T(8,128)(2,1)S(1)} %get-tuple-element.26), channel_id=1, source_target_pairs={{0,96},{32,0},{64,32},{96,64},{1,97},{33,1},{65,33},{97,65},{2,98}... | collective-permute-start | bytes 393224 | tf_op jit(solution)/shard_map/ppermute | solution.py:181
  74.5 13.6 %collective-permute-start.11 = (bf16[256,256]{1,0:T(8,128)(2,1)S(1)}, bf16[256,256]{1,0:T(8,128)(2,1)S(1)}, u32[]{:S(2)}, u32[]{:S(2)}) collective-permute-start(bf16[256,256]{1,0:T(8,128)(2,1)S(1)} %get-tuple-element.27), channel_id=1, source_target_pairs={{0,32},{32,64},{64,96},{96,0},{1,33},{33,65},{65,97},{97,1},{2,34}... | collective-permute-start | bytes 393224 | tf_op jit(solution)/shard_map/ppermute | solution.py:181
  74.5 13.6 %collective-permute-start.9 = (bf16[256,256]{1,0:T(8,128)(2,1)S(1)}, bf16[256,256]{1,0:T(8,128)(2,1)S(1)}, u32[]{:S(2)}, u32[]{:S(2)}) collective-permute-start(bf16[256,256]{1,0:T(8,128)(2,1)S(1)} %get-tuple-element.25), channel_id=1, source_target_pairs={{0,64},{32,96},{64,0},{96,32},{1,65},{33,97},{65,1},{97,33},{2,66}... | collective-permute-start | bytes 393224 | tf_op jit(solution)/shard_map/ppermute | solution.py:181
  84.1 5.4 %collective-permute-start.12 = (bf16[256,256]{1,0:T(8,128)(2,1)S(1)}, bf16[256,256]{1,0:T(8,128)(2,1)S(1)}, u32[]{:S(2)}, u32[]{:S(2)}) collective-permute-start(bf16[256,256]{1,0:T(8,128)(2,1)S(1)} %get-tuple-element.29), channel_id=1, source_target_pairs={{0,64},{32,96},{64,0},{96,32},{1,65},{33,97},{65,1},{97,33},{2,66}... | collective-permute-start | bytes 393224 | tf_op jit(solution)/shard_map/ppermute | solution.py:181
  85.5 5.5 %collective-permute-start.13 = (bf16[256,256]{1,0:T(8,128)(2,1)S(1)}, bf16[256,256]{1,0:T(8,128)(2,1)S(1)}, u32[]{:S(2)}, u32[]{:S(2)}) collective-permute-start(bf16[256,256]{1,0:T(8,128)(2,1)S(1)} %get-tuple-element.30), channel_id=1, source_target_pairs={{0,96},{32,0},{64,32},{96,64},{1,97},{33,1},{65,33},{97,65},{2,98}... | collective-permute-start | bytes 393224 | tf_op jit(solution)/shard_map/ppermute | solution.py:181
  88.1 5.0 %collective-permute-start.14 = (bf16[256,256]{1,0:T(8,128)(2,1)S(1)}, bf16[256,256]{1,0:T(8,128)(2,1)S(1)}, u32[]{:S(2)}, u32[]{:S(2)}) collective-permute-start(bf16[256,256]{1,0:T(8,128)(2,1)S(1)} %get-tuple-element.31), channel_id=1, source_target_pairs={{0,32},{32,64},{64,96},{96,0},{1,33},{33,65},{65,97},{97,1},{2,34}... | collective-permute-start | bytes 393224 | tf_op jit(solution)/shard_map/ppermute | solution.py:181
  120.7 6.7 %collective-permute-start.16 = (bf16[128,512]{1,0:T(8,128)(2,1)S(1)}, bf16[128,512]{1,0:T(8,128)(2,1)S(1)}, u32[]{:S(2)}, u32[]{:S(2)}) collective-permute-start(bf16[128,512]{1,0:T(8,128)(2,1)S(1)} %convolution_convert_fusion.5), channel_id=1, source_target_pairs={{0,64},{32,96},{64,0},{96,32},{1,65},{33,97},{65,1},{97,33},{2,66}... | collective-permute-start | bytes 393224 | tf_op jit(solution)/shard_map/ppermute | solution.py:181
  120.8 6.5 %collective-permute-start.17 = (bf16[128,512]{1,0:T(8,128)(2,1)S(1)}, bf16[128,512]{1,0:T(8,128)(2,1)S(1)}, u32[]{:S(2)}, u32[]{:S(2)}) collective-permute-start(bf16[128,512]{1,0:T(8,128)(2,1)S(1)} %convolution_convert_fusion.4), channel_id=1, source_target_pairs={{0,96},{32,0},{64,32},{96,64},{1,97},{33,1},{65,33},{97,65},{2,98}... | collective-permute-start | bytes 393224 | tf_op jit(solution)/shard_map/ppermute | solution.py:181
  122.3 5.6 %collective-permute-start.18 = (bf16[128,512]{1,0:T(8,128)(2,1)S(1)}, bf16[128,512]{1,0:T(8,128)(2,1)S(1)}, u32[]{:S(2)}, u32[]{:S(2)}) collective-permute-start(bf16[128,512]{1,0:T(8,128)(2,1)S(1)} %convolution_convert_fusion.3), channel_id=1, source_target_pairs={{0,32},{32,64},{64,96},{96,0},{1,33},{33,65},{65,97},{97,1},{2,34}... | collective-permute-start | bytes 393224 | tf_op jit(solution)/shard_map/ppermute | solution.py:181
  123.4 13.3 %all-to-all-start.5 = ((bf16[16,16,512]{2,1,0:T(8,128)(2,1)}), bf16[16,16,512]{2,1,0:T(8,128)(2,1)S(1)}, u32[]{:S(2)}, u32[]{:S(2)}) async-start(bf16[16,16,512]{2,1,0:T(8,128)(2,1)} %bitcast.12), calls=%async_computation.5 | async-start | bytes 524288 | tf_op jit(solution)/shard_map/all_to_all | solution.py:239
  128.0 23.4 %collective-permute-start.19 = (bf16[128,512]{1,0:T(8,128)(2,1)S(1)}, bf16[128,512]{1,0:T(8,128)(2,1)S(1)}, u32[]{:S(2)}, u32[]{:S(2)}) collective-permute-start(bf16[128,512]{1,0:T(8,128)(2,1)S(1)} %add_convert_fusion), channel_id=1, source_target_pairs={{0,128},{128,0},{1,129},{129,1},{2,130},{130,2},{3,131},{131,3},{4... | collective-permute-start | bytes 393224 | tf_op jit(solution)/shard_map/ppermute | solution.py:177
  136.7 14.9 %copy-start.2 = (bf16[16,16,512]{2,1,0:T(8,128)(2,1)}, bf16[16,16,512]{2,1,0:T(8,128)(2,1)S(1)}, u32[]{:S(2)}) copy-start(bf16[16,16,512]{2,1,0:T(8,128)(2,1)S(1)} %all-to-all-done.5) | copy-start | bytes 786436
  136.7 16.0 %collective-permute-start.15 = (bf16[256,512]{1,0:T(8,128)(2,1)S(1)}, bf16[256,512]{1,0:T(8,128)(2,1)S(1)}, u32[]{:S(2)}, u32[]{:S(2)}) collective-permute-start(bf16[256,512]{1,0:T(8,128)(2,1)S(1)} %bitcast.37), channel_id=1, source_target_pairs={{0,1},{1,0},{2,3},{3,2},{4,5},{5,4},{6,7},{7,6},{8,9},{9,8},{10,11... | collective-permute-start | bytes 786440 | tf_op jit(solution)/shard_map/ppermute | solution.py:177
  152.6 0.7 copy-start.3

commit v4 on v3

--- a/solution.py
+++ b/solution.py
@@ -23,7 +23,8 @@
 Y_COUNT = 4
 COL_COUNT = 16
 FAR_FIRST = (2, 1, 3, 0)
-VMEM = 48 * 1024 * 1024
+VMEM = 24 * 1024 * 1024
+SMALL = 4 * 1024 * 1024
 HEADS_AT_ONCE = 8
 
 
@@ -68,7 +69,7 @@
     )(own_rows, key_matrix, value_matrix)
 
 
-def unpack_kernel(mine_ref, other_ref, out_ref):
+def finish_kernel(mine_ref, other_ref, weight_ref, weight_other_ref, out_ref, key_ref, value_ref):
     count = out_ref.shape[0]
     wide = mine_ref.shape[1] // Y_COUNT
     for by in range(Y_COUNT):
@@ -77,17 +78,24 @@
             place = (slice(j * count, (j + 1) * count), slice(by * wide, (by + 1) * wide))
             total = mine_ref[place].astype(F32) + other_ref[place].astype(F32)
             out_ref[:, pl.ds(pl.multiple_of(start + j * wide, wide), wide)] = total.astype(BF)
-
-
-def unpack(mine, other):
+    kv_width = key_ref.shape[1]
+    total = weight_ref[...].astype(F32) + weight_other_ref[...].astype(F32)
+    key_ref[...] = total[:, :kv_width]
+    value_ref[...] = total[:, kv_width:]
+
+
+def finish(mine, other, weight_sum, weight_other):
     count = mine.shape[0] // COL_COUNT
+    weight_rows, width = weight_sum.shape
     return pl.pallas_call(
-        unpack_kernel,
-        in_specs=[whole()] * 2,
-        out_specs=whole(),
-        out_shape=jax.ShapeDtypeStruct((count, COL_COUNT * mine.shape[1]), BF),
-        name="unpack",
-    )(mine, other)
+        finish_kernel,
+        in_specs=[whole()] * 4,
+        out_specs=[whole()] * 3,
+        out_shape=[jax.ShapeDtypeStruct((count, COL_COUNT * mine.shape[1]), BF)]
+        + [jax.ShapeDtypeStruct((weight_rows, width // 2), F32)] * 2,
+        compiler_params=pltpu.CompilerParams(vmem_limit_bytes=SMALL),
+        name="finish",
+    )(mine, other, weight_sum, weight_other)
 
 
 def attend_one(query, cotangent, key_rows, value_rows):
@@ -237,16 +245,14 @@
     grad_block = gather_col(raw_grad)
     vision_part = dot(grad_block, weight_block, NT).astype(BF)
     vision_own = lax.all_to_all(vision_part, COL, 0, 0, tiled=True)
-    d_vision = unpack(vision_own, swap(vision_own, "mp"))
-
     wide = weights.shape[0]
     weight_part = [
         dot(vision_block[:, by * wide : (by + 1) * wide], grad_block, TN).astype(BF) for by in range(Y_COUNT)
     ]
     weight_sum = sum_behind(weight_part).astype(BF)
-    total = weight_sum.astype(F32) + swap(weight_sum, "dp").astype(F32)
-    kv_width = key_matrix.shape[1]
-    d_k, d_v = total[:, :kv_width], total[:, kv_width:]
+    weight_other = swap(weight_sum, "dp")
+    vision_own, weight_other = lax.optimization_barrier((vision_own, weight_other))
+    d_vision, d_k, d_v = finish(vision_own, swap(vision_own, "mp"), weight_sum, weight_other)
     return attended[None], d_queries[None], d_vision[None], d_k, d_v
 
 

time: 156 us -> 154 us (0.987)
    ppermute x2, waiting for transfers between devices: 0.4 us -> 5.19 us  [swap(): return lax.ppermute(x, axis, [(0, 1), (1, 0)])]
    all_to_all x1, waiting for transfers between devices: 8.22 us -> 4.19 us  [body(): vision_own = lax.all_to_all(vision_part, COL, 0, 0, tiled=True)]
  transfers between devices with their start and end apart: 22 -> 22, of which waited for: 9 -> 10; matrix products, arithmetic and copies ran while one was open for 1% -> 1% of each run, Pallas kernels for 10% -> 10%
where the time goes in v4:
time: 154 us
  blocking collectives  58 us (38%)
  starting transfers between devices  53.2 us (35%)
  waiting for transfers between devices  19.9 us (13%)
  Pallas kernels  18.6 us (12%)
  matrix products  2.16 us (1%)
    all_to_all x2, blocking collectives, sum_col(): parts = lax.all_to_all(x, COL, 0, 0, tiled=True)  30.9 us
    all_to_all x2, blocking collectives, gather_col(): return lax.all_to_all(copies, COL, 0, 0, tiled=True)  27.2 us
    ppermute x18, starting transfers between devices, shift(): lax.ppermute(x, 'y', [(i, (i + by) % Y_COUNT) for i in range(Y_COUNT)])  22.3 us
    pallas_call x2, Pallas kernels, attend(): pl.pallas_call(functools.partial(attend_kernel, heads, steps, len(before)...  15.9 us
    ppermute x2, starting transfers between devices, swap(): return lax.ppermute(x, axis, [(0, 1), (1, 0)])  15.2 us
    all_to_all x1, starting transfers between devices, body(): vision_block = lax.all_to_all(columns, COL, 0, 0, tiled=True)  11.7 us
    ppermute x18, waiting for transfers between devices, shift(): lax.ppermute(x, 'y', [(i, (i + by) % Y_COUNT) for i in range(Y_COUNT)])  9.72 us
    ppermute x2, waiting for transfers between devices, swap(): return lax.ppermute(x, axis, [(0, 1), (1, 0)])  5.19 us
  transfers between devices with their start and end apart: 22, of which 10 were waited for; matrix products, arithmetic and copies ran while one was open for 1% of the time, Pallas kernels for 10%

profile of v4, /device:TPU:1, one launch (start us, length us, event | category | flops | bytes accessed | tf_op | source)
XLA Modules:
  0.0 153.5 jit_solution(2627966342572059137)
XLA Ops:
  0.6 1.8 %pack.1 = (bf16[256,512]{1,0:T(8,128)(2,1)}, bf16[128,512]{1,0:T(8,128)(2,1)}) custom-call(bf16[16,8192]{1,0:T(8,128)(2,1)} %bitcast.43, bf16[128,256]{1,0:T(8,128)(2,1)} %key_ref.1, bf16[128,256]{1,0:T(8,128)(2,1)} %value_ref.1), custom_call_target="tpu_custom_call" | custom-call | tf_op jit(solution)/shard_map/pack/pallas_call | solution.py:60
  2.5 11.7 %all-to-all-start = ((bf16[16,16,512]{2,1,0:T(8,128)(2,1)}), bf16[16,16,512]{2,1,0:T(8,128)(2,1)S(1)}, u32[]{:S(2)}, u32[]{:S(2)}) async-start(bf16[16,16,512]{2,1,0:T(8,128)(2,1)} %bitcast.44), calls=%async_computation | async-start | bytes 524288 | tf_op jit(solution)/shard_map/all_to_all | solution.py:217
  14.2 1.4 collective-permute-start
  15.6 2.6 %collective-permute-start.1 = (bf16[128,512]{1,0:T(8,128)(2,1)S(1)}, bf16[128,512]{1,0:T(8,128)(2,1)S(1)}, u32[]{:S(2)}, u32[]{:S(2)}) collective-permute-start(bf16[128,512]{1,0:T(8,128)(2,1)S(1)} %copy-done.2), channel_id=1, source_target_pairs={{0,64},{32,96},{64,0},{96,32},{1,65},{33,97},{65,1},{97,33},{2,66}... | collective-permute-start | bytes 393224 | tf_op jit(solution)/shard_map/ppermute | solution.py:189
  18.2 1.1 collective-permute-start.2
  19.3 0.4 collective-permute-done
  19.7 3.9 %collective-permute-done.1 = bf16[128,512]{1,0:T(8,128)(2,1)S(1)} collective-permute-done((bf16[128,512]{1,0:T(8,128)(2,1)S(1)}, bf16[128,512]{1,0:T(8,128)(2,1)S(1)}, u32[]{:S(2)}, u32[]{:S(2)}) %collective-permute-start.1) | collective-permute-done | bytes 131104 | tf_op jit(solution)/shard_map/ppermute | solution.py:189
  23.6 0.8 all-to-all-done
  24.4 0.3 convolution_convert_fusion.1
  24.7 17.6 %all_to_all.57 = bf16[16,16,512]{2,1,0:T(8,128)(2,1)S(1)} all-to-all(bf16[16,16,512]{2,1,0:T(8,128)(2,1)S(1)} %bitcast.40), channel_id=1, replica_groups=mesh['dp'=2,'y'=4,'xh'=2,'z'=8,'mp'=2] {'xh','z'}, dimensions={0} | all-to-all | bytes 524288 | tf_op jit(solution)/shard_map/all_to_all | solution.py:208
  42.3 0.1 multiply_reduce_fusion.3
  42.5 0.1 multiply_convert_fusion.1
  42.6 14.0 %all_to_all.58 = bf16[16,16,512]{2,1,0:T(8,128)(2,1)S(1)} all-to-all(bf16[16,16,512]{2,1,0:T(8,128)(2,1)S(1)} %broadcast_in_dim.10), channel_id=1, replica_groups=mesh['dp'=2,'y'=4,'xh'=2,'z'=8,'mp'=2] {'xh','z'}, dimensions={0} | all-to-all | bytes 524288 | tf_op jit(solution)/shard_map/all_to_all | solution.py:203
  56.6 0.2 collective-permute-start.6
  56.8 4.1 %collective-permute-start.7 = (bf16[256,256]{1,0:T(8,128)(2,1)S(1)}, bf16[256,256]{1,0:T(8,128)(2,1)S(1)}, u32[]{:S(2)}, u32[]{:S(2)}) collective-permute-start(bf16[256,256]{1,0:T(8,128)(2,1)S(1)} %get-tuple-element.47.refs_0_), channel_id=1, source_target_pairs={{0,64},{32,96},{64,0},{96,32},{1,65},{33,97},{65,1},{97,33},{2,66}... | collective-permute-start | bytes 393224 | tf_op jit(solution)/shard_map/ppermute | solution.py:189
  60.9 1.5 collective-permute-start.3
  62.4 2.4 %collective-permute-start.5 = (bf16[256,256]{1,0:T(8,128)(2,1)S(1)}, bf16[256,256]{1,0:T(8,128)(2,1)S(1)}, u32[]{:S(2)}, u32[]{:S(2)}) collective-permute-start(bf16[256,256]{1,0:T(8,128)(2,1)S(1)} %get-tuple-element.48.refs_0_), channel_id=1, source_target_pairs={{0,96},{32,0},{64,32},{96,64},{1,97},{33,1},{65,33},{97,65},{2,98}... | collective-permute-start | bytes 393224 | tf_op jit(solution)/shard_map/ppermute | solution.py:189
  64.8 8.0 %attend.2 = (bf16[256,2048]{1,0:T(8,128)(2,1)}, bf16[256,2048]{1,0:T(8,128)(2,1)}, bf16[256,256]{1,0:T(8,128)(2,1)S(1)}, bf16[256,256]{1,0:T(8,128)(2,1)S(1)}, b...) custom-call(bf16[256,2048]{1,0:T(8,128)(2,1)S(1)} %bitcast.25, bf16[256,2048]{1,0:T(8,128)(2,1)S(1)} %bitcast.27, ...), custom_call_target="tpu_custom_call" | custom-call | flops 3221225472 | bytes 2097152 | tf_op jit(solution)/shard_map/attend/pallas_call | solution.py:166
  72.8 1.8 %collective-permute-start.10 = (bf16[256,256]{1,0:T(8,128)(2,1)S(1)}, bf16[256,256]{1,0:T(8,128)(2,1)S(1)}, u32[]{:S(2)}, u32[]{:S(2)}) collective-permute-start(bf16[256,256]{1,0:T(8,128)(2,1)S(1)} %get-tuple-element.31), channel_id=1, source_target_pairs={{0,96},{32,0},{64,32},{96,64},{1,97},{33,1},{65,33},{97,65},{2,98}... | collective-permute-start | bytes 393224 | tf_op jit(solution)/shard_map/ppermute | solution.py:189
  74.5 1.6 %collective-permute-start.9 = (bf16[256,256]{1,0:T(8,128)(2,1)S(1)}, bf16[256,256]{1,0:T(8,128)(2,1)S(1)}, u32[]{:S(2)}, u32[]{:S(2)}) collective-permute-start(bf16[256,256]{1,0:T(8,128)(2,1)S(1)} %get-tuple-element.30), channel_id=1, source_target_pairs={{0,64},{32,96},{64,0},{96,32},{1,65},{33,97},{65,1},{97,33},{2,66}... | collective-permute-start | bytes 393224 | tf_op jit(solution)/shard_map/ppermute | solution.py:189
  76.1 8.0 %attend.3 = (bf16[256,2048]{1,0:T(8,128)(2,1)}, bf16[256,2048]{1,0:T(8,128)(2,1)}, bf16[256,256]{1,0:T(8,128)(2,1)S(1)}, bf16[256,256]{1,0:T(8,128)(2,1)S(1)}, b...) custom-call(bf16[256,2048]{1,0:T(8,128)(2,1)S(1)} %bitcast.26, ...), custom_call_target="tpu_custom_call", output_to_operand_aliasing={{0}: (6, {}), {1}: (7, {})} | custom-call | flops 3221225472 | bytes 2097152 | tf_op jit(solution)/shard_map/attend/pallas_call | solution.py:166
  84.1 1.4 collective-permute-start.12
  85.5 2.7 %collective-permute-start.13 = (bf16[256,256]{1,0:T(8,128)(2,1)S(1)}, bf16[256,256]{1,0:T(8,128)(2,1)S(1)}, u32[]{:S(2)}, u32[]{:S(2)}) collective-permute-start(bf16[256,256]{1,0:T(8,128)(2,1)S(1)} %get-tuple-element.35), channel_id=1, source_target_pairs={{0,96},{32,0},{64,32},{96,64},{1,97},{33,1},{65,33},{97,65},{2,98}... | collective-permute-start | bytes 393224 | tf_op jit(solution)/shard_map/ppermute | solution.py:189
  88.2 0.1 add_convert_fusion.2
  88.2 1.2 collective-permute-done.12
  89.4 1.5 collective-permute-done.13
  90.9 2.2 %collective-permute-done.14 = bf16[256,256]{1,0:T(8,128)(2,1)S(1)} collective-permute-done((bf16[256,256]{1,0:T(8,128)(2,1)S(1)}, bf16[256,256]{1,0:T(8,128)(2,1)S(1)}, u32[]{:S(2)}, u32[]{:S(2)}) %collective-permute-start.14) | collective-permute-done | bytes 131104 | tf_op jit(solution)/shard_map/ppermute | solution.py:189
  93.2 0.1 add_convert_fusion.1
  93.3 13.3 %all_to_all.59 = bf16[16,16,512]{2,1,0:T(8,128)(2,1)S(1)} all-to-all(bf16[16,16,512]{2,1,0:T(8,128)(2,1)S(1)} %pad_maximum_fusion), channel_id=1, replica_groups=mesh['dp'=2,'y'=4,'xh'=2,'z'=8,'mp'=2] {'xh','z'}, dimensions={0} | all-to-all | bytes 524288 | tf_op jit(solution)/shard_map/all_to_all | solution.py:208
  106.6 0.1 multiply_reduce_fusion.1
  106.8 0.1 subtract_convert_fusion.1
  106.9 13.2 %all_to_all.60 = bf16[16,16,512]{2,1,0:T(8,128)(2,1)S(1)} all-to-all(bf16[16,16,512]{2,1,0:T(8,128)(2,1)S(1)} %broadcast_in_dim.13), channel_id=1, replica_groups=mesh['dp'=2,'y'=4,'xh'=2,'z'=8,'mp'=2] {'xh','z'}, dimensions={0} | all-to-all | bytes 524288 | tf_op jit(solution)/shard_map/all_to_all | solution.py:203
  120.1 0.2 convolution_convert_fusion.5
  120.3 0.2 convolution_convert_fusion.4
  120.5 0.2 convolution_convert_fusion.3
  120.7 0.1 collective-permute-start.15
  120.8 1.4 collective-permute-start.16
  122.3 0.1 collective-permute-start.17
  122.4 1.0 convolution_convert_fusion
  123.4 4.0 %all-to-all-start.5 = ((bf16[16,16,512]{2,1,0:T(8,128)(2,1)}), bf16[16,16,512]{2,1,0:T(8,128)(2,1)S(1)}, u32[]{:S(2)}, u32[]{:S(2)}) async-start(bf16[16,16,512]{2,1,0:T(8,128)(2,1)} %bitcast.12), calls=%async_computation.5 | async-start | bytes 524288 | tf_op jit(solution)/shard_map/all_to_all | solution.py:247
  127.4 0.4 collective-permute-done.17
  127.8 0.2 add_convert_fusion.weight_ref
  128.0 0.4 collective-permute-start.18
  128.4 4.0 %collective-permute-done.18.weight_other_ref = bf16[128,512]{1,0:T(8,128)(2,1)S(1)} collective-permute-done((bf16[128,512]{1,0:T(8,128)(2,1)S(1)}, bf16[128,512]{1,0:T(8,128)(2,1)S(1)}, u32[]{:S(2)}, u32[]{:S(2)}) %collective-permute-start.18) | collective-permute-done | bytes 131104 | tf_op jit(solution)/shard_map/ppermute | solution.py:185
  132.5 4.2 %all-to-all-done.5 = bf16[16,16,512]{2,1,0:T(8,128)(2,1)S(1)} async-done(((bf16[16,16,512]{2,1,0:T(8,128)(2,1)}), bf16[16,16,512]{2,1,0:T(8,128)(2,1)S(1)}, u32[]{:S(2)}, u32[]{:S(2)}) %all-to-all-start.5) | async-done | bytes 262176 | tf_op jit(solution)/shard_map/all_to_all | solution.py:247
  136.7 14.8 %collective-permute-start.19 = (bf16[256,512]{1,0:T(8,128)(2,1)S(1)}, bf16[256,512]{1,0:T(8,128)(2,1)S(1)}, u32[]{:S(2)}, u32[]{:S(2)}) collective-permute-start(bf16[256,512]{1,0:T(8,128)(2,1)S(1)} %bitcast.23), channel_id=1, source_target_pairs={{0,1},{1,0},{2,3},{3,2},{4,5},{5,4},{6,7},{7,6},{8,9},{9,8},{10,11... | collective-permute-start | bytes 786440 | tf_op jit(solution)/shard_map/ppermute | solution.py:185
  151.5 1.2 collective-permute-done.19.other_ref
  152.6 0.9 finish.1
  (41 shorter events, 0.3 us)
Async XLA Ops:
  2.5 11.7 %copy-start.2 = (bf16[128,512]{1,0:T(8,128)(2,1)S(1)}, bf16[128,512]{1,0:T(8,128)(2,1)}, u32[]{:S(2)}) copy-start(bf16[128,512]{1,0:T(8,128)(2,1)} %get-tuple-element.25) | copy-start | bytes 393220
  2.5 22.0 %all-to-all-start = ((bf16[16,16,512]{2,1,0:T(8,128)(2,1)}), bf16[16,16,512]{2,1,0:T(8,128)(2,1)S(1)}, u32[]{:S(2)}, u32[]{:S(2)}) async-start(bf16[16,16,512]{2,1,0:T(8,128)(2,1)} %bitcast.44), calls=%async_computation | async-start | bytes 524288 | tf_op jit(solution)/shard_map/all_to_all | solution.py:217
  14.2 5.5 %collective-permute-start = (bf16[128,512]{1,0:T(8,128)(2,1)S(1)}, bf16[128,512]{1,0:T(8,128)(2,1)S(1)}, u32[]{:S(2)}, u32[]{:S(2)}) collective-permute-start(bf16[128,512]{1,0:T(8,128)(2,1)S(1)} %copy-done.2), channel_id=1, source_target_pairs={{0,32},{32,64},{64,96},{96,0},{1,33},{33,65},{65,97},{97,1},{2,34}... | collective-permute-start | bytes 393224 | tf_op jit(solution)/shard_map/ppermute | solution.py:189
  15.6 8.0 %collective-permute-start.1 = (bf16[128,512]{1,0:T(8,128)(2,1)S(1)}, bf16[128,512]{1,0:T(8,128)(2,1)S(1)}, u32[]{:S(2)}, u32[]{:S(2)}) collective-permute-start(bf16[128,512]{1,0:T(8,128)(2,1)S(1)} %copy-done.2), channel_id=1, source_target_pairs={{0,64},{32,96},{64,0},{96,32},{1,65},{33,97},{65,1},{97,33},{2,66}... | collective-permute-start | bytes 393224 | tf_op jit(solution)/shard_map/ppermute | solution.py:189
  18.2 5.4 %collective-permute-start.2 = (bf16[128,512]{1,0:T(8,128)(2,1)S(1)}, bf16[128,512]{1,0:T(8,128)(2,1)S(1)}, u32[]{:S(2)}, u32[]{:S(2)}) collective-permute-start(bf16[128,512]{1,0:T(8,128)(2,1)S(1)} %copy-done.2), channel_id=1, source_target_pairs={{0,96},{32,0},{64,32},{96,64},{1,97},{33,1},{65,33},{97,65},{2,98}... | collective-permute-start | bytes 393224 | tf_op jit(solution)/shard_map/ppermute | solution.py:189
  24.7 40.1 %copy-start = (bf16[1,256,2048]{2,1,0:T(8,128)(2,1)S(1)}, bf16[1,256,2048]{2,1,0:T(8,128)(2,1)}, u32[]{:S(2)}) copy-start(bf16[1,256,2048]{2,1,0:T(8,128)(2,1)} %param.5) | copy-start | bytes 3145732
  24.7 40.1 %copy-start.1 = (bf16[1,256,2048]{2,1,0:T(8,128)(2,1)S(1)}, bf16[1,256,2048]{2,1,0:T(8,128)(2,1)}, u32[]{:S(2)}) copy-start(bf16[1,256,2048]{2,1,0:T(8,128)(2,1)} %param.9) | copy-start | bytes 3145732
  56.6 5.8 %collective-permute-start.6 = (bf16[256,256]{1,0:T(8,128)(2,1)S(1)}, bf16[256,256]{1,0:T(8,128)(2,1)S(1)}, u32[]{:S(2)}, u32[]{:S(2)}) collective-permute-start(bf16[256,256]{1,0:T(8,128)(2,1)S(1)} %get-tuple-element.47.refs_0_), channel_id=1, source_target_pairs={{0,32},{32,64},{64,96},{96,0},{1,33},{33,65},{65,97},{97,1},{2,34}... | collective-permute-start | bytes 393224 | tf_op jit(solution)/shard_map/ppermute | solution.py:189
  56.8 8.0 %collective-permute-start.7 = (bf16[256,256]{1,0:T(8,128)(2,1)S(1)}, bf16[256,256]{1,0:T(8,128)(2,1)S(1)}, u32[]{:S(2)}, u32[]{:S(2)}) collective-permute-start(bf16[256,256]{1,0:T(8,128)(2,1)S(1)} %get-tuple-element.47.refs_0_), channel_id=1, source_target_pairs={{0,64},{32,96},{64,0},{96,32},{1,65},{33,97},{65,1},{97,33},{2,66}... | collective-permute-start | bytes 393224 | tf_op jit(solution)/shard_map/ppermute | solution.py:189
  60.9 3.9 %collective-permute-start.8 = (bf16[256,256]{1,0:T(8,128)(2,1)S(1)}, bf16[256,256]{1,0:T(8,128)(2,1)S(1)}, u32[]{:S(2)}, u32[]{:S(2)}) collective-permute-start(bf16[256,256]{1,0:T(8,128)(2,1)S(1)} %get-tuple-element.47.refs_0_), channel_id=1, source_target_pairs={{0,96},{32,0},{64,32},{96,64},{1,97},{33,1},{65,33},{97,65},{2,98}... | collective-permute-start | bytes 393224 | tf_op jit(solution)/shard_map/ppermute | solution.py:189
  60.9 13.6 %collective-permute-start.3 = (bf16[256,256]{1,0:T(8,128)(2,1)S(1)}, bf16[256,256]{1,0:T(8,128)(2,1)S(1)}, u32[]{:S(2)}, u32[]{:S(2)}) collective-permute-start(bf16[256,256]{1,0:T(8,128)(2,1)S(1)} %get-tuple-element.48.refs_0_), channel_id=1, source_target_pairs={{0,32},{32,64},{64,96},{96,0},{1,33},{33,65},{65,97},{97,1},{2,34}... | collective-permute-start | bytes 393224 | tf_op jit(solution)/shard_map/ppermute | solution.py:189
  62.4 13.7 %collective-permute-start.4 = (bf16[256,256]{1,0:T(8,128)(2,1)S(1)}, bf16[256,256]{1,0:T(8,128)(2,1)S(1)}, u32[]{:S(2)}, u32[]{:S(2)}) collective-permute-start(bf16[256,256]{1,0:T(8,128)(2,1)S(1)} %get-tuple-element.48.refs_0_), channel_id=1, source_target_pairs={{0,64},{32,96},{64,0},{96,32},{1,65},{33,97},{65,1},{97,33},{2,66}... | collective-permute-start | bytes 393224 | tf_op jit(solution)/shard_map/ppermute | solution.py:189
  62.4 13.7 %collective-permute-start.5 = (bf16[256,256]{1,0:T(8,128)(2,1)S(1)}, bf16[256,256]{1,0:T(8,128)(2,1)S(1)}, u32[]{:S(2)}, u32[]{:S(2)}) collective-permute-start(bf16[256,256]{1,0:T(8,128)(2,1)S(1)} %get-tuple-element.48.refs_0_), channel_id=1, source_target_pairs={{0,96},{32,0},{64,32},{96,64},{1,97},{33,1},{65,33},{97,65},{2,98}... | collective-permute-start | bytes 393224 | tf_op jit(solution)/shard_map/ppermute | solution.py:189
  72.8 15.4 %collective-permute-start.10 = (bf16[256,256]{1,0:T(8,128)(2,1)S(1)}, bf16[256,256]{1,0:T(8,128)(2,1)S(1)}, u32[]{:S(2)}, u32[]{:S(2)}) collective-permute-start(bf16[256,256]{1,0:T(8,128)(2,1)S(1)} %get-tuple-element.31), channel_id=1, source_target_pairs={{0,96},{32,0},{64,32},{96,64},{1,97},{33,1},{65,33},{97,65},{2,98}... | collective-permute-start | bytes 393224 | tf_op jit(solution)/shard_map/ppermute | solution.py:189
  74.5 13.6 %collective-permute-start.11 = (bf16[256,256]{1,0:T(8,128)(2,1)S(1)}, bf16[256,256]{1,0:T(8,128)(2,1)S(1)}, u32[]{:S(2)}, u32[]{:S(2)}) collective-permute-start(bf16[256,256]{1,0:T(8,128)(2,1)S(1)} %get-tuple-element.32), channel_id=1, source_target_pairs={{0,32},{32,64},{64,96},{96,0},{1,33},{33,65},{65,97},{97,1},{2,34}... | collective-permute-start | bytes 393224 | tf_op jit(solution)/shard_map/ppermute | solution.py:189
  74.5 13.6 %collective-permute-start.9 = (bf16[256,256]{1,0:T(8,128)(2,1)S(1)}, bf16[256,256]{1,0:T(8,128)(2,1)S(1)}, u32[]{:S(2)}, u32[]{:S(2)}) collective-permute-start(bf16[256,256]{1,0:T(8,128)(2,1)S(1)} %get-tuple-element.30), channel_id=1, source_target_pairs={{0,64},{32,96},{64,0},{96,32},{1,65},{33,97},{65,1},{97,33},{2,66}... | collective-permute-start | bytes 393224 | tf_op jit(solution)/shard_map/ppermute | solution.py:189
  84.1 5.4 %collective-permute-start.12 = (bf16[256,256]{1,0:T(8,128)(2,1)S(1)}, bf16[256,256]{1,0:T(8,128)(2,1)S(1)}, u32[]{:S(2)}, u32[]{:S(2)}) collective-permute-start(bf16[256,256]{1,0:T(8,128)(2,1)S(1)} %get-tuple-element.34), channel_id=1, source_target_pairs={{0,64},{32,96},{64,0},{96,32},{1,65},{33,97},{65,1},{97,33},{2,66}... | collective-permute-start | bytes 393224 | tf_op jit(solution)/shard_map/ppermute | solution.py:189
  85.5 5.5 %collective-permute-start.13 = (bf16[256,256]{1,0:T(8,128)(2,1)S(1)}, bf16[256,256]{1,0:T(8,128)(2,1)S(1)}, u32[]{:S(2)}, u32[]{:S(2)}) collective-permute-start(bf16[256,256]{1,0:T(8,128)(2,1)S(1)} %get-tuple-element.35), channel_id=1, source_target_pairs={{0,96},{32,0},{64,32},{96,64},{1,97},{33,1},{65,33},{97,65},{2,98}... | collective-permute-start | bytes 393224 | tf_op jit(solution)/shard_map/ppermute | solution.py:189
  88.1 5.0 %collective-permute-start.14 = (bf16[256,256]{1,0:T(8,128)(2,1)S(1)}, bf16[256,256]{1,0:T(8,128)(2,1)S(1)}, u32[]{:S(2)}, u32[]{:S(2)}) collective-permute-start(bf16[256,256]{1,0:T(8,128)(2,1)S(1)} %get-tuple-element.36), channel_id=1, source_target_pairs={{0,32},{32,64},{64,96},{96,0},{1,33},{33,65},{65,97},{97,1},{2,34}... | collective-permute-start | bytes 393224 | tf_op jit(solution)/shard_map/ppermute | solution.py:189
  120.7 6.7 %collective-permute-start.15 = (bf16[128,512]{1,0:T(8,128)(2,1)S(1)}, bf16[128,512]{1,0:T(8,128)(2,1)S(1)}, u32[]{:S(2)}, u32[]{:S(2)}) collective-permute-start(bf16[128,512]{1,0:T(8,128)(2,1)S(1)} %convolution_convert_fusion.5), channel_id=1, source_target_pairs={{0,64},{32,96},{64,0},{96,32},{1,65},{33,97},{65,1},{97,33},{2,66}... | collective-permute-start | bytes 393224 | tf_op jit(solution)/shard_map/ppermute | solution.py:189
  120.8 6.5 %collective-permute-start.16 = (bf16[128,512]{1,0:T(8,128)(2,1)S(1)}, bf16[128,512]{1,0:T(8,128)(2,1)S(1)}, u32[]{:S(2)}, u32[]{:S(2)}) collective-permute-start(bf16[128,512]{1,0:T(8,128)(2,1)S(1)} %convolution_convert_fusion.4), channel_id=1, source_target_pairs={{0,96},{32,0},{64,32},{96,64},{1,97},{33,1},{65,33},{97,65},{2,98}... | collective-permute-start | bytes 393224 | tf_op jit(solution)/shard_map/ppermute | solution.py:189
  122.3 5.6 %collective-permute-start.17 = (bf16[128,512]{1,0:T(8,128)(2,1)S(1)}, bf16[128,512]{1,0:T(8,128)(2,1)S(1)}, u32[]{:S(2)}, u32[]{:S(2)}) collective-permute-start(bf16[128,512]{1,0:T(8,128)(2,1)S(1)} %convolution_convert_fusion.3), channel_id=1, source_target_pairs={{0,32},{32,64},{64,96},{96,0},{1,33},{33,65},{65,97},{97,1},{2,34}... | collective-permute-start | bytes 393224 | tf_op jit(solution)/shard_map/ppermute | solution.py:189
  123.4 13.3 %all-to-all-start.5 = ((bf16[16,16,512]{2,1,0:T(8,128)(2,1)}), bf16[16,16,512]{2,1,0:T(8,128)(2,1)S(1)}, u32[]{:S(2)}, u32[]{:S(2)}) async-start(bf16[16,16,512]{2,1,0:T(8,128)(2,1)} %bitcast.12), calls=%async_computation.5 | async-start | bytes 524288 | tf_op jit(solution)/shard_map/all_to_all | solution.py:247
  128.0 4.4 %collective-permute-start.18 = (bf16[128,512]{1,0:T(8,128)(2,1)S(1)}, bf16[128,512]{1,0:T(8,128)(2,1)S(1)}, u32[]{:S(2)}, u32[]{:S(2)}) collective-permute-start(bf16[128,512]{1,0:T(8,128)(2,1)S(1)} %add_convert_fusion.weight_ref), channel_id=1, source_target_pairs={{0,128},{128,0},{1,129},{129,1},{2,130},{130,2},{3,131},{131,3},{4... | collective-permute-start | bytes 393224 | tf_op jit(solution)/shard_map/ppermute | solution.py:185
  136.7 16.0 %collective-permute-start.19 = (bf16[256,512]{1,0:T(8,128)(2,1)S(1)}, bf16[256,512]{1,0:T(8,128)(2,1)S(1)}, u32[]{:S(2)}, u32[]{:S(2)}) collective-permute-start(bf16[256,512]{1,0:T(8,128)(2,1)S(1)} %bitcast.23), channel_id=1, source_target_pairs={{0,1},{1,0},{2,3},{3,2},{4,5},{5,4},{6,7},{7,6},{8,9},{9,8},{10,11... | collective-permute-start | bytes 786440 | tf_op jit(solution)/shard_map/ppermute | solution.py:185

commit v5 on v4

--- a/solution.py
+++ b/solution.py
@@ -22,7 +22,7 @@
 COL = ("xh", "z")
 Y_COUNT = 4
 COL_COUNT = 16
-FAR_FIRST = (2, 1, 3, 0)
+Y_BACK = (2, 1, 3, 0)
 VMEM = 24 * 1024 * 1024
 SMALL = 4 * 1024 * 1024
 HEADS_AT_ONCE = 8
@@ -36,8 +36,8 @@
     return pl.BlockSpec(memory_space=pltpu.VMEM)
 
 
-def back(by):
-    return lax.rem(lax.axis_index("y") + Y_COUNT - by, Y_COUNT)
+def back(piece):
+    return lax.rem(lax.axis_index("y") + Y_COUNT - Y_BACK[piece], Y_COUNT)
 
 
 def pack_kernel(vision_ref, key_ref, value_ref, columns_ref, weights_ref):
@@ -107,14 +107,13 @@
     inverse = 1.0 / jnp.sum(expo, axis=1, keepdims=True)
     expo_low = expo.astype(BF)
     out = dot(expo_low, value_rows, NN) * inverse
-    scaled = cotangent.astype(F32) * inverse
-    scaled_low = scaled.astype(BF)
-    score_grad = dot(scaled_low, value_rows, NT)
-    delta = jnp.sum(scaled * out, axis=1, keepdims=True)
+    scaled = (cotangent.astype(F32) * inverse).astype(BF)
+    score_grad = dot(scaled, value_rows, NT)
+    delta = jnp.sum(scaled.astype(F32) * out, axis=1, keepdims=True)
     logit_grad = (expo * (score_grad - delta)).astype(BF)
     norm_grad = dot(logit_grad, key_rows, NN) * SCALE
     key_grad = dot(logit_grad, query_norm, TN)
-    value_grad = dot(expo_low, scaled_low, TN)
+    value_grad = dot(expo_low, scaled, TN)
     inner = jnp.mean(query_f * norm_grad, axis=-1, keepdims=True)
     d_query = factor * norm_grad - query_f * (factor * factor * factor) * inner
     return out.astype(BF), d_query.astype(BF), key_grad, value_grad
@@ -190,12 +189,11 @@
 
 
 def from_behind(x):
-    pieces = {by: shift(x, by) for by in FAR_FIRST}
-    return [pieces[by] for by in range(Y_COUNT)]
+    return [shift(x, by) for by in Y_BACK]
 
 
 def sum_behind(pieces):
-    return sum(shift(pieces[by], (Y_COUNT - by) % Y_COUNT).astype(F32) for by in FAR_FIRST)
+    return sum(shift(piece, (Y_COUNT - by) % Y_COUNT).astype(F32) for by, piece in zip(Y_BACK, pieces))
 
 
 def gather_col(x):
@@ -247,7 +245,7 @@
     vision_own = lax.all_to_all(vision_part, COL, 0, 0, tiled=True)
     wide = weights.shape[0]
     weight_part = [
-        dot(vision_block[:, by * wide : (by + 1) * wide], grad_block, TN).astype(BF) for by in range(Y_COUNT)
+        dot(vision_block[:, p * wide : (p + 1) * wide], grad_block, TN).astype(BF) for p in range(Y_COUNT)
     ]
     weight_sum = sum_behind(weight_part).astype(BF)
     weight_other = swap(weight_sum, "dp")

time: 154 us -> 154 us (level)
  blocking collectives: 58 us -> 60.2 us
  waiting for transfers between devices: 19.9 us -> 17.7 us
    all_to_all x1, waiting for transfers between devices: 0.78 us -> 4.17 us  [body(): vision_block = lax.all_to_all(columns, COL, 0, 0, tiled=True)]
    all_to_all x1, waiting for transfers between devices: 4.19 us -> 1.8 us  [body(): vision_own = lax.all_to_all(vision_part, COL, 0, 0, tiled=True)]
    ppermute x18, waiting for transfers between devices: 9.72 us -> 7.9 us  [shift(): lax.ppermute(x, 'y', [(i, (i + by) % Y_COUNT) for i in range(Y_COUNT)])]
  transfers between devices with their start and end apart: 22 -> 22, of which waited for: 10 -> 9; matrix products, arithmetic and copies ran while one was open for 1% -> 1% of each run, Pallas kernels for 10% -> 10%
where the time goes in v5:
time: 154 us; the launch traced here: 153 us
  blocking collectives  60.2 us (39%)
  starting transfers between devices  52.6 us (34%)
  Pallas kernels  18.6 us (12%)
  waiting for transfers between devices  17.7 us (11%)
  matrix products  2.16 us (1%)
    all_to_all x2, blocking collectives, sum_col(): parts = lax.all_to_all(x, COL, 0, 0, tiled=True)  32 us
    all_to_all x2, blocking collectives, gather_col(): return lax.all_to_all(copies, COL, 0, 0, tiled=True)  28.2 us
    ppermute x18, starting transfers between devices, shift(): lax.ppermute(x, 'y', [(i, (i + by) % Y_COUNT) for i in range(Y_COUNT)])  21.5 us
    ppermute x2, starting transfers between devices, swap(): return lax.ppermute(x, axis, [(0, 1), (1, 0)])  16.2 us
    pallas_call x2, Pallas kernels, attend(): pl.pallas_call(functools.partial(attend_kernel, heads, steps, len(before)...  15.9 us
    all_to_all x1, starting transfers between devices, body(): vision_block = lax.all_to_all(columns, COL, 0, 0, tiled=True)  10.9 us
    ppermute x18, waiting for transfers between devices, shift(): lax.ppermute(x, 'y', [(i, (i + by) % Y_COUNT) for i in range(Y_COUNT)])  7.9 us
    all_to_all x1, waiting for transfers between devices, body(): vision_block = lax.all_to_all(columns, COL, 0, 0, tiled=True)  4.17 us
  transfers between devices with their start and end apart: 22, of which 9 were waited for; matrix products, arithmetic and copies ran while one was open for 1% of the time, Pallas kernels for 10%

profile of v5, /device:TPU:1, one launch (start us, length us, event | category | flops | bytes accessed | tf_op | source)
XLA Modules:
  0.0 153.0 jit_solution(9901363067537231783)
XLA Ops:
  0.6 1.8 %pack.1 = (bf16[256,512]{1,0:T(8,128)(2,1)}, bf16[128,512]{1,0:T(8,128)(2,1)}) custom-call(bf16[16,8192]{1,0:T(8,128)(2,1)} %bitcast.43, bf16[128,256]{1,0:T(8,128)(2,1)} %key_ref.1, bf16[128,256]{1,0:T(8,128)(2,1)} %value_ref.1), custom_call_target="tpu_custom_call" | custom-call | tf_op jit(solution)/shard_map/pack/pallas_call | solution.py:60
  2.5 3.7 %collective-permute-start = (bf16[128,512]{1,0:T(8,128)(2,1)}, bf16[128,512]{1,0:T(8,128)(2,1)S(1)}, u32[]{:S(2)}, u32[]{:S(2)}) collective-permute-start(bf16[128,512]{1,0:T(8,128)(2,1)} %get-tuple-element.25), channel_id=1, source_target_pairs={{0,64},{32,96},{64,0},{96,32},{1,65},{33,97},{65,1},{97,33},{2,66}... | collective-permute-start | bytes 393224 | tf_op jit(solution)/shard_map/ppermute | solution.py:188
  6.2 10.9 %all-to-all-start = ((bf16[16,16,512]{2,1,0:T(8,128)(2,1)}), bf16[16,16,512]{2,1,0:T(8,128)(2,1)S(1)}, u32[]{:S(2)}, u32[]{:S(2)}) async-start(bf16[16,16,512]{2,1,0:T(8,128)(2,1)} %bitcast.44), calls=%async_computation | async-start | bytes 524288 | tf_op jit(solution)/shard_map/all_to_all | solution.py:215
  17.1 0.5 collective-permute-start.1
  17.6 2.3 %collective-permute-start.2 = (bf16[128,512]{1,0:T(8,128)(2,1)S(1)}, bf16[128,512]{1,0:T(8,128)(2,1)S(1)}, u32[]{:S(2)}, u32[]{:S(2)}) collective-permute-start(bf16[128,512]{1,0:T(8,128)(2,1)S(1)} %copy-done.2), channel_id=1, source_target_pairs={{0,96},{32,0},{64,32},{96,64},{1,97},{33,1},{65,33},{97,65},{2,98}... | collective-permute-start | bytes 393224 | tf_op jit(solution)/shard_map/ppermute | solution.py:188
  19.9 2.3 %collective-permute-done.1 = bf16[128,512]{1,0:T(8,128)(2,1)S(1)} collective-permute-done((bf16[128,512]{1,0:T(8,128)(2,1)S(1)}, bf16[128,512]{1,0:T(8,128)(2,1)S(1)}, u32[]{:S(2)}, u32[]{:S(2)}) %collective-permute-start.1) | collective-permute-done | bytes 131104 | tf_op jit(solution)/shard_map/ppermute | solution.py:188
  22.3 4.2 %all-to-all-done = bf16[16,16,512]{2,1,0:T(8,128)(2,1)S(1)} async-done(((bf16[16,16,512]{2,1,0:T(8,128)(2,1)}), bf16[16,16,512]{2,1,0:T(8,128)(2,1)S(1)}, u32[]{:S(2)}, u32[]{:S(2)}) %all-to-all-start) | async-done | bytes 262176 | tf_op jit(solution)/shard_map/all_to_all | solution.py:215
  26.4 0.3 convolution_convert_fusion.1
  26.8 15.5 %all_to_all.57 = bf16[16,16,512]{2,1,0:T(8,128)(2,1)S(1)} all-to-all(bf16[16,16,512]{2,1,0:T(8,128)(2,1)S(1)} %bitcast.40), channel_id=1, replica_groups=mesh['dp'=2,'y'=4,'xh'=2,'z'=8,'mp'=2] {'xh','z'}, dimensions={0} | all-to-all | bytes 524288 | tf_op jit(solution)/shard_map/all_to_all | solution.py:206
  42.4 0.1 multiply_reduce_fusion.3
  42.5 0.1 multiply_convert_fusion.1
  42.6 15.1 %all_to_all.58 = bf16[16,16,512]{2,1,0:T(8,128)(2,1)S(1)} all-to-all(bf16[16,16,512]{2,1,0:T(8,128)(2,1)S(1)} %broadcast_in_dim.10), channel_id=1, replica_groups=mesh['dp'=2,'y'=4,'xh'=2,'z'=8,'mp'=2] {'xh','z'}, dimensions={0} | all-to-all | bytes 524288 | tf_op jit(solution)/shard_map/all_to_all | solution.py:201
  57.7 0.1 collective-permute-start.6
  57.8 0.5 collective-permute-start.7
  58.3 2.3 %collective-permute-start.8 = (bf16[256,256]{1,0:T(8,128)(2,1)S(1)}, bf16[256,256]{1,0:T(8,128)(2,1)S(1)}, u32[]{:S(2)}, u32[]{:S(2)}) collective-permute-start(bf16[256,256]{1,0:T(8,128)(2,1)S(1)} %get-tuple-element.47.refs_3_), channel_id=1, source_target_pairs={{0,96},{32,0},{64,32},{96,64},{1,97},{33,1},{65,33},{97,65},{2,98}... | collective-permute-start | bytes 393224 | tf_op jit(solution)/shard_map/ppermute | solution.py:188
  60.6 1.6 %collective-permute-start.3 = (bf16[256,256]{1,0:T(8,128)(2,1)S(1)}, bf16[256,256]{1,0:T(8,128)(2,1)S(1)}, u32[]{:S(2)}, u32[]{:S(2)}) collective-permute-start(bf16[256,256]{1,0:T(8,128)(2,1)S(1)} %get-tuple-element.48.refs_3_), channel_id=1, source_target_pairs={{0,64},{32,96},{64,0},{96,32},{1,65},{33,97},{65,1},{97,33},{2,66}... | collective-permute-start | bytes 393224 | tf_op jit(solution)/shard_map/ppermute | solution.py:188
  62.2 0.4 collective-permute-start.4
  62.6 0.6 collective-permute-done.6.refs_0_
  63.2 1.7 %collective-permute-start.5 = (bf16[256,256]{1,0:T(8,128)(2,1)S(1)}, bf16[256,256]{1,0:T(8,128)(2,1)S(1)}, u32[]{:S(2)}, u32[]{:S(2)}) collective-permute-start(bf16[256,256]{1,0:T(8,128)(2,1)S(1)} %get-tuple-element.48.refs_3_), channel_id=1, source_target_pairs={{0,96},{32,0},{64,32},{96,64},{1,97},{33,1},{65,33},{97,65},{2,98}... | collective-permute-start | bytes 393224 | tf_op jit(solution)/shard_map/ppermute | solution.py:188
  64.9 8.0 %attend.2 = (bf16[256,2048]{1,0:T(8,128)(2,1)}, bf16[256,2048]{1,0:T(8,128)(2,1)}, bf16[256,256]{1,0:T(8,128)(2,1)S(1)}, bf16[256,256]{1,0:T(8,128)(2,1)S(1)}, b...) custom-call(bf16[256,2048]{1,0:T(8,128)(2,1)S(1)} %bitcast.25, bf16[256,2048]{1,0:T(8,128)(2,1)S(1)} %bitcast.27, ...), custom_call_target="tpu_custom_call" | custom-call | flops 3221225472 | bytes 2097152 | tf_op jit(solution)/shard_map/attend/pallas_call | solution.py:165
  72.9 0.7 collective-permute-start.10
  73.6 0.8 collective-permute-start.11
  74.4 0.9 collective-permute-start.9
  75.3 8.0 %attend.3 = (bf16[256,2048]{1,0:T(8,128)(2,1)}, bf16[256,2048]{1,0:T(8,128)(2,1)}, bf16[256,256]{1,0:T(8,128)(2,1)S(1)}, bf16[256,256]{1,0:T(8,128)(2,1)S(1)}, b...) custom-call(bf16[256,2048]{1,0:T(8,128)(2,1)S(1)} %bitcast.26, ...), custom_call_target="tpu_custom_call", output_to_operand_aliasing={{0}: (6, {}), {1}: (7, {})} | custom-call | flops 3221225472 | bytes 2097152 | tf_op jit(solution)/shard_map/attend/pallas_call | solution.py:165
  83.3 2.0 %collective-permute-start.12 = (bf16[256,256]{1,0:T(8,128)(2,1)S(1)}, bf16[256,256]{1,0:T(8,128)(2,1)S(1)}, u32[]{:S(2)}, u32[]{:S(2)}) collective-permute-start(bf16[256,256]{1,0:T(8,128)(2,1)S(1)} %get-tuple-element.34), channel_id=1, source_target_pairs={{0,64},{32,96},{64,0},{96,32},{1,65},{33,97},{65,1},{97,33},{2,66}... | collective-permute-start | bytes 393224 | tf_op jit(solution)/shard_map/ppermute | solution.py:188
  85.3 1.9 %collective-permute-start.13 = (bf16[256,256]{1,0:T(8,128)(2,1)S(1)}, bf16[256,256]{1,0:T(8,128)(2,1)S(1)}, u32[]{:S(2)}, u32[]{:S(2)}) collective-permute-start(bf16[256,256]{1,0:T(8,128)(2,1)S(1)} %get-tuple-element.35), channel_id=1, source_target_pairs={{0,96},{32,0},{64,32},{96,64},{1,97},{33,1},{65,33},{97,65},{2,98}... | collective-permute-start | bytes 393224 | tf_op jit(solution)/shard_map/ppermute | solution.py:188
  87.3 2.2 %collective-permute-done.12 = bf16[256,256]{1,0:T(8,128)(2,1)S(1)} collective-permute-done((bf16[256,256]{1,0:T(8,128)(2,1)S(1)}, bf16[256,256]{1,0:T(8,128)(2,1)S(1)}, u32[]{:S(2)}, u32[]{:S(2)}) %collective-permute-start.12) | collective-permute-done | bytes 131104 | tf_op jit(solution)/shard_map/ppermute | solution.py:188
  89.5 1.3 collective-permute-done.13
  90.7 1.5 collective-permute-done.14
  92.3 16.5 %all_to_all.59 = bf16[16,16,512]{2,1,0:T(8,128)(2,1)S(1)} all-to-all(bf16[16,16,512]{2,1,0:T(8,128)(2,1)S(1)} %pad_maximum_fusion), channel_id=1, replica_groups=mesh['dp'=2,'y'=4,'xh'=2,'z'=8,'mp'=2] {'xh','z'}, dimensions={0} | all-to-all | bytes 524288 | tf_op jit(solution)/shard_map/all_to_all | solution.py:206
  108.9 0.1 multiply_reduce_fusion.1
  109.0 0.1 subtract_convert_fusion.1
  109.2 13.1 %all_to_all.60 = bf16[16,16,512]{2,1,0:T(8,128)(2,1)S(1)} all-to-all(bf16[16,16,512]{2,1,0:T(8,128)(2,1)S(1)} %broadcast_in_dim.13), channel_id=1, replica_groups=mesh['dp'=2,'y'=4,'xh'=2,'z'=8,'mp'=2] {'xh','z'}, dimensions={0} | all-to-all | bytes 524288 | tf_op jit(solution)/shard_map/all_to_all | solution.py:201
  122.3 0.2 convolution_convert_fusion.5
  122.5 0.2 convolution_convert_fusion.4
  122.7 0.2 convolution_convert_fusion.3
  122.9 0.6 collective-permute-start.15
  123.5 1.0 collective-permute-start.16
  124.4 0.5 collective-permute-start.17
  124.9 1.0 convolution_convert_fusion
  126.0 4.0 %all-to-all-start.5 = ((bf16[16,16,512]{2,1,0:T(8,128)(2,1)}), bf16[16,16,512]{2,1,0:T(8,128)(2,1)S(1)}, u32[]{:S(2)}, u32[]{:S(2)}) async-start(bf16[16,16,512]{2,1,0:T(8,128)(2,1)} %bitcast.12), calls=%async_computation.5 | async-start | bytes 524288 | tf_op jit(solution)/shard_map/all_to_all | solution.py:245
  130.1 0.2 add_convert_fusion.weight_ref
  130.3 4.6 %collective-permute-start.18 = (bf16[128,512]{1,0:T(8,128)(2,1)S(1)}, bf16[128,512]{1,0:T(8,128)(2,1)S(1)}, u32[]{:S(2)}, u32[]{:S(2)}) collective-permute-start(bf16[128,512]{1,0:T(8,128)(2,1)S(1)} %add_convert_fusion.weight_ref), channel_id=1, source_target_pairs={{0,128},{128,0},{1,129},{129,1},{2,130},{130,2},{3,131},{131,3},{4... | collective-permute-start | bytes 393224 | tf_op jit(solution)/shard_map/ppermute | solution.py:184
  134.8 2.7 %collective-permute-done.18.weight_other_ref = bf16[128,512]{1,0:T(8,128)(2,1)S(1)} collective-permute-done((bf16[128,512]{1,0:T(8,128)(2,1)S(1)}, bf16[128,512]{1,0:T(8,128)(2,1)S(1)}, u32[]{:S(2)}, u32[]{:S(2)}) %collective-permute-start.18) | collective-permute-done | bytes 131104 | tf_op jit(solution)/shard_map/ppermute | solution.py:184
  137.5 1.8 %all-to-all-done.5 = bf16[16,16,512]{2,1,0:T(8,128)(2,1)S(1)} async-done(((bf16[16,16,512]{2,1,0:T(8,128)(2,1)}), bf16[16,16,512]{2,1,0:T(8,128)(2,1)S(1)}, u32[]{:S(2)}, u32[]{:S(2)}) %all-to-all-start.5) | async-done | bytes 262176 | tf_op jit(solution)/shard_map/all_to_all | solution.py:245
  139.3 11.6 %collective-permute-start.19 = (bf16[256,512]{1,0:T(8,128)(2,1)S(1)}, bf16[256,512]{1,0:T(8,128)(2,1)S(1)}, u32[]{:S(2)}, u32[]{:S(2)}) collective-permute-start(bf16[256,512]{1,0:T(8,128)(2,1)S(1)} %bitcast.23), channel_id=1, source_target_pairs={{0,1},{1,0},{2,3},{3,2},{4,5},{5,4},{6,7},{7,6},{8,9},{9,8},{10,11... | collective-permute-start | bytes 786440 | tf_op jit(solution)/shard_map/ppermute | solution.py:184
  150.9 1.2 collective-permute-done.19.other_ref
  152.1 0.9 finish.1
  (41 shorter events, 0.4 us)
Async XLA Ops:
  2.5 17.4 %collective-permute-start = (bf16[128,512]{1,0:T(8,128)(2,1)}, bf16[128,512]{1,0:T(8,128)(2,1)S(1)}, u32[]{:S(2)}, u32[]{:S(2)}) collective-permute-start(bf16[128,512]{1,0:T(8,128)(2,1)} %get-tuple-element.25), channel_id=1, source_target_pairs={{0,64},{32,96},{64,0},{96,32},{1,65},{33,97},{65,1},{97,33},{2,66}... | collective-permute-start | bytes 393224 | tf_op jit(solution)/shard_map/ppermute | solution.py:188
  6.2 10.9 %copy-start.2 = (bf16[128,512]{1,0:T(8,128)(2,1)S(1)}, bf16[128,512]{1,0:T(8,128)(2,1)}, u32[]{:S(2)}) copy-start(bf16[128,512]{1,0:T(8,128)(2,1)} %get-tuple-element.25) | copy-start | bytes 393220
  6.2 20.2 %all-to-all-start = ((bf16[16,16,512]{2,1,0:T(8,128)(2,1)}), bf16[16,16,512]{2,1,0:T(8,128)(2,1)S(1)}, u32[]{:S(2)}, u32[]{:S(2)}) async-start(bf16[16,16,512]{2,1,0:T(8,128)(2,1)} %bitcast.44), calls=%async_computation | async-start | bytes 524288 | tf_op jit(solution)/shard_map/all_to_all | solution.py:215
  17.1 5.1 %collective-permute-start.1 = (bf16[128,512]{1,0:T(8,128)(2,1)S(1)}, bf16[128,512]{1,0:T(8,128)(2,1)S(1)}, u32[]{:S(2)}, u32[]{:S(2)}) collective-permute-start(bf16[128,512]{1,0:T(8,128)(2,1)S(1)} %copy-done.2), channel_id=1, source_target_pairs={{0,32},{32,64},{64,96},{96,0},{1,33},{33,65},{65,97},{97,1},{2,34}... | collective-permute-start | bytes 393224 | tf_op jit(solution)/shard_map/ppermute | solution.py:188
  17.6 4.6 %collective-permute-start.2 = (bf16[128,512]{1,0:T(8,128)(2,1)S(1)}, bf16[128,512]{1,0:T(8,128)(2,1)S(1)}, u32[]{:S(2)}, u32[]{:S(2)}) collective-permute-start(bf16[128,512]{1,0:T(8,128)(2,1)S(1)} %copy-done.2), channel_id=1, source_target_pairs={{0,96},{32,0},{64,32},{96,64},{1,97},{33,1},{65,33},{97,65},{2,98}... | collective-permute-start | bytes 393224 | tf_op jit(solution)/shard_map/ppermute | solution.py:188
  26.7 38.2 %copy-start = (bf16[1,256,2048]{2,1,0:T(8,128)(2,1)S(1)}, bf16[1,256,2048]{2,1,0:T(8,128)(2,1)}, u32[]{:S(2)}) copy-start(bf16[1,256,2048]{2,1,0:T(8,128)(2,1)} %param.5) | copy-start | bytes 3145732
  26.7 38.2 %copy-start.1 = (bf16[1,256,2048]{2,1,0:T(8,128)(2,1)S(1)}, bf16[1,256,2048]{2,1,0:T(8,128)(2,1)}, u32[]{:S(2)}) copy-start(bf16[1,256,2048]{2,1,0:T(8,128)(2,1)} %param.9) | copy-start | bytes 3145732
  57.7 5.5 %collective-permute-start.6 = (bf16[256,256]{1,0:T(8,128)(2,1)S(1)}, bf16[256,256]{1,0:T(8,128)(2,1)S(1)}, u32[]{:S(2)}, u32[]{:S(2)}) collective-permute-start(bf16[256,256]{1,0:T(8,128)(2,1)S(1)} %get-tuple-element.47.refs_3_), channel_id=1, source_target_pairs={{0,64},{32,96},{64,0},{96,32},{1,65},{33,97},{65,1},{97,33},{2,66}... | collective-permute-start | bytes 393224 | tf_op jit(solution)/shard_map/ppermute | solution.py:188
  57.8 7.1 %collective-permute-start.7 = (bf16[256,256]{1,0:T(8,128)(2,1)S(1)}, bf16[256,256]{1,0:T(8,128)(2,1)S(1)}, u32[]{:S(2)}, u32[]{:S(2)}) collective-permute-start(bf16[256,256]{1,0:T(8,128)(2,1)S(1)} %get-tuple-element.47.refs_3_), channel_id=1, source_target_pairs={{0,32},{32,64},{64,96},{96,0},{1,33},{33,65},{65,97},{97,1},{2,34}... | collective-permute-start | bytes 393224 | tf_op jit(solution)/shard_map/ppermute | solution.py:188
  58.3 6.6 %collective-permute-start.8 = (bf16[256,256]{1,0:T(8,128)(2,1)S(1)}, bf16[256,256]{1,0:T(8,128)(2,1)S(1)}, u32[]{:S(2)}, u32[]{:S(2)}) collective-permute-start(bf16[256,256]{1,0:T(8,128)(2,1)S(1)} %get-tuple-element.47.refs_3_), channel_id=1, source_target_pairs={{0,96},{32,0},{64,32},{96,64},{1,97},{33,1},{65,33},{97,65},{2,98}... | collective-permute-start | bytes 393224 | tf_op jit(solution)/shard_map/ppermute | solution.py:188
  60.6 13.8 %collective-permute-start.3 = (bf16[256,256]{1,0:T(8,128)(2,1)S(1)}, bf16[256,256]{1,0:T(8,128)(2,1)S(1)}, u32[]{:S(2)}, u32[]{:S(2)}) collective-permute-start(bf16[256,256]{1,0:T(8,128)(2,1)S(1)} %get-tuple-element.48.refs_3_), channel_id=1, source_target_pairs={{0,64},{32,96},{64,0},{96,32},{1,65},{33,97},{65,1},{97,33},{2,66}... | collective-permute-start | bytes 393224 | tf_op jit(solution)/shard_map/ppermute | solution.py:188
  62.2 13.1 %collective-permute-start.4 = (bf16[256,256]{1,0:T(8,128)(2,1)S(1)}, bf16[256,256]{1,0:T(8,128)(2,1)S(1)}, u32[]{:S(2)}, u32[]{:S(2)}) collective-permute-start(bf16[256,256]{1,0:T(8,128)(2,1)S(1)} %get-tuple-element.48.refs_3_), channel_id=1, source_target_pairs={{0,32},{32,64},{64,96},{96,0},{1,33},{33,65},{65,97},{97,1},{2,34}... | collective-permute-start | bytes 393224 | tf_op jit(solution)/shard_map/ppermute | solution.py:188
  63.2 12.1 %collective-permute-start.5 = (bf16[256,256]{1,0:T(8,128)(2,1)S(1)}, bf16[256,256]{1,0:T(8,128)(2,1)S(1)}, u32[]{:S(2)}, u32[]{:S(2)}) collective-permute-start(bf16[256,256]{1,0:T(8,128)(2,1)S(1)} %get-tuple-element.48.refs_3_), channel_id=1, source_target_pairs={{0,96},{32,0},{64,32},{96,64},{1,97},{33,1},{65,33},{97,65},{2,98}... | collective-permute-start | bytes 393224 | tf_op jit(solution)/shard_map/ppermute | solution.py:188
  72.9 14.3 %collective-permute-start.10 = (bf16[256,256]{1,0:T(8,128)(2,1)S(1)}, bf16[256,256]{1,0:T(8,128)(2,1)S(1)}, u32[]{:S(2)}, u32[]{:S(2)}) collective-permute-start(bf16[256,256]{1,0:T(8,128)(2,1)S(1)} %get-tuple-element.31), channel_id=1, source_target_pairs={{0,96},{32,0},{64,32},{96,64},{1,97},{33,1},{65,33},{97,65},{2,98}... | collective-permute-start | bytes 393224 | tf_op jit(solution)/shard_map/ppermute | solution.py:188
  73.6 13.6 %collective-permute-start.11 = (bf16[256,256]{1,0:T(8,128)(2,1)S(1)}, bf16[256,256]{1,0:T(8,128)(2,1)S(1)}, u32[]{:S(2)}, u32[]{:S(2)}) collective-permute-start(bf16[256,256]{1,0:T(8,128)(2,1)S(1)} %get-tuple-element.32), channel_id=1, source_target_pairs={{0,32},{32,64},{64,96},{96,0},{1,33},{33,65},{65,97},{97,1},{2,34}... | collective-permute-start | bytes 393224 | tf_op jit(solution)/shard_map/ppermute | solution.py:188
  74.4 12.8 %collective-permute-start.9 = (bf16[256,256]{1,0:T(8,128)(2,1)S(1)}, bf16[256,256]{1,0:T(8,128)(2,1)S(1)}, u32[]{:S(2)}, u32[]{:S(2)}) collective-permute-start(bf16[256,256]{1,0:T(8,128)(2,1)S(1)} %get-tuple-element.30), channel_id=1, source_target_pairs={{0,64},{32,96},{64,0},{96,32},{1,65},{33,97},{65,1},{97,33},{2,66}... | collective-permute-start | bytes 393224 | tf_op jit(solution)/shard_map/ppermute | solution.py:188
  83.3 6.2 %collective-permute-start.12 = (bf16[256,256]{1,0:T(8,128)(2,1)S(1)}, bf16[256,256]{1,0:T(8,128)(2,1)S(1)}, u32[]{:S(2)}, u32[]{:S(2)}) collective-permute-start(bf16[256,256]{1,0:T(8,128)(2,1)S(1)} %get-tuple-element.34), channel_id=1, source_target_pairs={{0,64},{32,96},{64,0},{96,32},{1,65},{33,97},{65,1},{97,33},{2,66}... | collective-permute-start | bytes 393224 | tf_op jit(solution)/shard_map/ppermute | solution.py:188
  85.3 5.4 %collective-permute-start.13 = (bf16[256,256]{1,0:T(8,128)(2,1)S(1)}, bf16[256,256]{1,0:T(8,128)(2,1)S(1)}, u32[]{:S(2)}, u32[]{:S(2)}) collective-permute-start(bf16[256,256]{1,0:T(8,128)(2,1)S(1)} %get-tuple-element.35), channel_id=1, source_target_pairs={{0,96},{32,0},{64,32},{96,64},{1,97},{33,1},{65,33},{97,65},{2,98}... | collective-permute-start | bytes 393224 | tf_op jit(solution)/shard_map/ppermute | solution.py:188
  87.2 5.0 %collective-permute-start.14 = (bf16[256,256]{1,0:T(8,128)(2,1)S(1)}, bf16[256,256]{1,0:T(8,128)(2,1)S(1)}, u32[]{:S(2)}, u32[]{:S(2)}) collective-permute-start(bf16[256,256]{1,0:T(8,128)(2,1)S(1)} %get-tuple-element.36), channel_id=1, source_target_pairs={{0,32},{32,64},{64,96},{96,0},{1,33},{33,65},{65,97},{97,1},{2,34}... | collective-permute-start | bytes 393224 | tf_op jit(solution)/shard_map/ppermute | solution.py:188
  122.9 7.1 %collective-permute-start.15 = (bf16[128,512]{1,0:T(8,128)(2,1)S(1)}, bf16[128,512]{1,0:T(8,128)(2,1)S(1)}, u32[]{:S(2)}, u32[]{:S(2)}) collective-permute-start(bf16[128,512]{1,0:T(8,128)(2,1)S(1)} %convolution_convert_fusion.5), channel_id=1, source_target_pairs={{0,64},{32,96},{64,0},{96,32},{1,65},{33,97},{65,1},{97,33},{2,66}... | collective-permute-start | bytes 393224 | tf_op jit(solution)/shard_map/ppermute | solution.py:188
  123.5 6.6 %collective-permute-start.16 = (bf16[128,512]{1,0:T(8,128)(2,1)S(1)}, bf16[128,512]{1,0:T(8,128)(2,1)S(1)}, u32[]{:S(2)}, u32[]{:S(2)}) collective-permute-start(bf16[128,512]{1,0:T(8,128)(2,1)S(1)} %convolution_convert_fusion.4), channel_id=1, source_target_pairs={{0,96},{32,0},{64,32},{96,64},{1,97},{33,1},{65,33},{97,65},{2,98}... | collective-permute-start | bytes 393224 | tf_op jit(solution)/shard_map/ppermute | solution.py:188
  124.4 5.6 %collective-permute-start.17 = (bf16[128,512]{1,0:T(8,128)(2,1)S(1)}, bf16[128,512]{1,0:T(8,128)(2,1)S(1)}, u32[]{:S(2)}, u32[]{:S(2)}) collective-permute-start(bf16[128,512]{1,0:T(8,128)(2,1)S(1)} %convolution_convert_fusion.3), channel_id=1, source_target_pairs={{0,32},{32,64},{64,96},{96,0},{1,33},{33,65},{65,97},{97,1},{2,34}... | collective-permute-start | bytes 393224 | tf_op jit(solution)/shard_map/ppermute | solution.py:188
  126.0 13.3 %all-to-all-start.5 = ((bf16[16,16,512]{2,1,0:T(8,128)(2,1)}), bf16[16,16,512]{2,1,0:T(8,128)(2,1)S(1)}, u32[]{:S(2)}, u32[]{:S(2)}) async-start(bf16[16,16,512]{2,1,0:T(8,128)(2,1)} %bitcast.12), calls=%async_computation.5 | async-start | bytes 524288 | tf_op jit(solution)/shard_map/all_to_all | solution.py:245
  130.3 7.2 %collective-permute-start.18 = (bf16[128,512]{1,0:T(8,128)(2,1)S(1)}, bf16[128,512]{1,0:T(8,128)(2,1)S(1)}, u32[]{:S(2)}, u32[]{:S(2)}) collective-permute-start(bf16[128,512]{1,0:T(8,128)(2,1)S(1)} %add_convert_fusion.weight_ref), channel_id=1, source_target_pairs={{0,128},{128,0},{1,129},{129,1},{2,130},{130,2},{3,131},{131,3},{4... | collective-permute-start | bytes 393224 | tf_op jit(solution)/shard_map/ppermute | solution.py:184
  139.3 12.8 %collective-permute-start.19 = (bf16[256,512]{1,0:T(8,128)(2,1)S(1)}, bf16[256,512]{1,0:T(8,128)(2,1)S(1)}, u32[]{:S(2)}, u32[]{:S(2)}) collective-permute-start(bf16[256,512]{1,0:T(8,128)(2,1)S(1)} %bitcast.23), channel_id=1, source_target_pairs={{0,1},{1,0},{2,3},{3,2},{4,5},{5,4},{6,7},{7,6},{8,9},{9,8},{10,11... | collective-permute-start | bytes 786440 | tf_op jit(solution)/shard_map/ppermute | solution.py:184

commit v6 on v5

--- a/solution.py
+++ b/solution.py
@@ -244,9 +244,8 @@
     vision_part = dot(grad_block, weight_block, NT).astype(BF)
     vision_own = lax.all_to_all(vision_part, COL, 0, 0, tiled=True)
     wide = weights.shape[0]
-    weight_part = [
-        dot(vision_block[:, p * wide : (p + 1) * wide], grad_block, TN).astype(BF) for p in range(Y_COUNT)
-    ]
+    weight_part = dot(vision_block, grad_block, TN).astype(BF)
+    weight_part = [weight_part[p * wide : (p + 1) * wide] for p in range(Y_COUNT)]
     weight_sum = sum_behind(weight_part).astype(BF)
     weight_other = swap(weight_sum, "dp")
     vision_own, weight_other = lax.optimization_barrier((vision_own, weight_other))

time: 154 us -> 153 us (level)
  no operation moved by 1% of the time
where the time goes in v6:
time: 153 us
  blocking collectives  60.2 us (39%)
  starting transfers between devices  52.5 us (34%)
  Pallas kernels  18.6 us (12%)
  waiting for transfers between devices  17.8 us (12%)
  matrix products  1.67 us (1%)
    all_to_all x2, blocking collectives, sum_col(): parts = lax.all_to_all(x, COL, 0, 0, tiled=True)  32 us
    all_to_all x2, blocking collectives, gather_col(): return lax.all_to_all(copies, COL, 0, 0, tiled=True)  28.2 us
    ppermute x18, starting transfers between devices, shift(): lax.ppermute(x, 'y', [(i, (i + by) % Y_COUNT) for i in range(Y_COUNT)])  21.5 us
    ppermute x2, starting transfers between devices, swap(): return lax.ppermute(x, axis, [(0, 1), (1, 0)])  16.2 us
    pallas_call x2, Pallas kernels, attend(): pl.pallas_call(functools.partial(attend_kernel, heads, steps, len(before)...  15.9 us
    all_to_all x1, starting transfers between devices, body(): vision_block = lax.all_to_all(columns, COL, 0, 0, tiled=True)  10.9 us
    ppermute x18, waiting for transfers between devices, shift(): lax.ppermute(x, 'y', [(i, (i + by) % Y_COUNT) for i in range(Y_COUNT)])  7.9 us
    all_to_all x1, waiting for transfers between devices, body(): vision_block = lax.all_to_all(columns, COL, 0, 0, tiled=True)  4.17 us
  transfers between devices with their start and end apart: 22, of which 9 were waited for; matrix products, arithmetic and copies ran while one was open for 1% of the time, Pallas kernels for 10%

profile of v6, /device:TPU:1, one launch (start us, length us, event | category | flops | bytes accessed | tf_op | source)
XLA Modules:
  0.0 152.7 jit_solution(17494400766778434398)
XLA Ops:
  0.6 1.8 %pack.1 = (bf16[256,512]{1,0:T(8,128)(2,1)}, bf16[128,512]{1,0:T(8,128)(2,1)}) custom-call(bf16[16,8192]{1,0:T(8,128)(2,1)} %bitcast.37, bf16[128,256]{1,0:T(8,128)(2,1)} %key_ref.1, bf16[128,256]{1,0:T(8,128)(2,1)} %value_ref.1), custom_call_target="tpu_custom_call" | custom-call | tf_op jit(solution)/shard_map/pack/pallas_call | solution.py:60
  2.5 3.7 %collective-permute-start = (bf16[128,512]{1,0:T(8,128)(2,1)}, bf16[128,512]{1,0:T(8,128)(2,1)S(1)}, u32[]{:S(2)}, u32[]{:S(2)}) collective-permute-start(bf16[128,512]{1,0:T(8,128)(2,1)} %get-tuple-element.25), channel_id=1, source_target_pairs={{0,64},{32,96},{64,0},{96,32},{1,65},{33,97},{65,1},{97,33},{2,66}... | collective-permute-start | bytes 393224 | tf_op jit(solution)/shard_map/ppermute | solution.py:188
  6.2 10.9 %all-to-all-start = ((bf16[16,16,512]{2,1,0:T(8,128)(2,1)}), bf16[16,16,512]{2,1,0:T(8,128)(2,1)S(1)}, u32[]{:S(2)}, u32[]{:S(2)}) async-start(bf16[16,16,512]{2,1,0:T(8,128)(2,1)} %bitcast.38), calls=%async_computation | async-start | bytes 524288 | tf_op jit(solution)/shard_map/all_to_all | solution.py:215
  17.1 0.5 collective-permute-start.1
  17.6 2.3 %collective-permute-start.2 = (bf16[128,512]{1,0:T(8,128)(2,1)S(1)}, bf16[128,512]{1,0:T(8,128)(2,1)S(1)}, u32[]{:S(2)}, u32[]{:S(2)}) collective-permute-start(bf16[128,512]{1,0:T(8,128)(2,1)S(1)} %copy-done.2), channel_id=1, source_target_pairs={{0,96},{32,0},{64,32},{96,64},{1,97},{33,1},{65,33},{97,65},{2,98}... | collective-permute-start | bytes 393224 | tf_op jit(solution)/shard_map/ppermute | solution.py:188
  19.9 2.3 %collective-permute-done.1 = bf16[128,512]{1,0:T(8,128)(2,1)S(1)} collective-permute-done((bf16[128,512]{1,0:T(8,128)(2,1)S(1)}, bf16[128,512]{1,0:T(8,128)(2,1)S(1)}, u32[]{:S(2)}, u32[]{:S(2)}) %collective-permute-start.1) | collective-permute-done | bytes 131104 | tf_op jit(solution)/shard_map/ppermute | solution.py:188
  22.3 4.2 %all-to-all-done = bf16[16,16,512]{2,1,0:T(8,128)(2,1)S(1)} async-done(((bf16[16,16,512]{2,1,0:T(8,128)(2,1)}), bf16[16,16,512]{2,1,0:T(8,128)(2,1)S(1)}, u32[]{:S(2)}, u32[]{:S(2)}) %all-to-all-start) | async-done | bytes 262176 | tf_op jit(solution)/shard_map/all_to_all | solution.py:215
  26.4 0.3 convolution_convert_fusion.1
  26.8 15.5 %all_to_all.57 = bf16[16,16,512]{2,1,0:T(8,128)(2,1)S(1)} all-to-all(bf16[16,16,512]{2,1,0:T(8,128)(2,1)S(1)} %bitcast.34), channel_id=1, replica_groups=mesh['dp'=2,'y'=4,'xh'=2,'z'=8,'mp'=2] {'xh','z'}, dimensions={0} | all-to-all | bytes 524288 | tf_op jit(solution)/shard_map/all_to_all | solution.py:206
  42.4 0.1 multiply_reduce_fusion.3
  42.5 0.1 multiply_convert_fusion.1
  42.6 15.1 %all_to_all.58 = bf16[16,16,512]{2,1,0:T(8,128)(2,1)S(1)} all-to-all(bf16[16,16,512]{2,1,0:T(8,128)(2,1)S(1)} %broadcast_in_dim.10), channel_id=1, replica_groups=mesh['dp'=2,'y'=4,'xh'=2,'z'=8,'mp'=2] {'xh','z'}, dimensions={0} | all-to-all | bytes 524288 | tf_op jit(solution)/shard_map/all_to_all | solution.py:201
  57.7 0.1 collective-permute-start.6
  57.8 0.5 collective-permute-start.7
  58.3 2.3 %collective-permute-start.8 = (bf16[256,256]{1,0:T(8,128)(2,1)S(1)}, bf16[256,256]{1,0:T(8,128)(2,1)S(1)}, u32[]{:S(2)}, u32[]{:S(2)}) collective-permute-start(bf16[256,256]{1,0:T(8,128)(2,1)S(1)} %get-tuple-element.50.refs_3_), channel_id=1, source_target_pairs={{0,96},{32,0},{64,32},{96,64},{1,97},{33,1},{65,33},{97,65},{2,98}... | collective-permute-start | bytes 393224 | tf_op jit(solution)/shard_map/ppermute | solution.py:188
  60.6 1.6 %collective-permute-start.3 = (bf16[256,256]{1,0:T(8,128)(2,1)S(1)}, bf16[256,256]{1,0:T(8,128)(2,1)S(1)}, u32[]{:S(2)}, u32[]{:S(2)}) collective-permute-start(bf16[256,256]{1,0:T(8,128)(2,1)S(1)} %get-tuple-element.51.refs_3_), channel_id=1, source_target_pairs={{0,64},{32,96},{64,0},{96,32},{1,65},{33,97},{65,1},{97,33},{2,66}... | collective-permute-start | bytes 393224 | tf_op jit(solution)/shard_map/ppermute | solution.py:188
  62.2 0.4 collective-permute-start.4
  62.6 0.6 collective-permute-done.6.refs_0_
  63.2 1.7 %collective-permute-start.5 = (bf16[256,256]{1,0:T(8,128)(2,1)S(1)}, bf16[256,256]{1,0:T(8,128)(2,1)S(1)}, u32[]{:S(2)}, u32[]{:S(2)}) collective-permute-start(bf16[256,256]{1,0:T(8,128)(2,1)S(1)} %get-tuple-element.51.refs_3_), channel_id=1, source_target_pairs={{0,96},{32,0},{64,32},{96,64},{1,97},{33,1},{65,33},{97,65},{2,98}... | collective-permute-start | bytes 393224 | tf_op jit(solution)/shard_map/ppermute | solution.py:188
  64.9 8.0 %attend.2 = (bf16[256,2048]{1,0:T(8,128)(2,1)}, bf16[256,2048]{1,0:T(8,128)(2,1)}, bf16[256,256]{1,0:T(8,128)(2,1)S(1)}, bf16[256,256]{1,0:T(8,128)(2,1)S(1)}, b...) custom-call(bf16[256,2048]{1,0:T(8,128)(2,1)S(1)} %bitcast.27, bf16[256,2048]{1,0:T(8,128)(2,1)S(1)} %bitcast.29, ...), custom_call_target="tpu_custom_call" | custom-call | flops 3221225472 | bytes 2097152 | tf_op jit(solution)/shard_map/attend/pallas_call | solution.py:165
  72.9 0.7 collective-permute-start.10
  73.6 0.8 collective-permute-start.11
  74.4 0.9 collective-permute-start.9
  75.3 8.0 %attend.3 = (bf16[256,2048]{1,0:T(8,128)(2,1)}, bf16[256,2048]{1,0:T(8,128)(2,1)}, bf16[256,256]{1,0:T(8,128)(2,1)S(1)}, bf16[256,256]{1,0:T(8,128)(2,1)S(1)}, b...) custom-call(bf16[256,2048]{1,0:T(8,128)(2,1)S(1)} %bitcast.28, ...), custom_call_target="tpu_custom_call", output_to_operand_aliasing={{0}: (6, {}), {1}: (7, {})} | custom-call | flops 3221225472 | bytes 2097152 | tf_op jit(solution)/shard_map/attend/pallas_call | solution.py:165
  83.3 2.0 %collective-permute-start.12 = (bf16[256,256]{1,0:T(8,128)(2,1)S(1)}, bf16[256,256]{1,0:T(8,128)(2,1)S(1)}, u32[]{:S(2)}, u32[]{:S(2)}) collective-permute-start(bf16[256,256]{1,0:T(8,128)(2,1)S(1)} %get-tuple-element.34), channel_id=1, source_target_pairs={{0,64},{32,96},{64,0},{96,32},{1,65},{33,97},{65,1},{97,33},{2,66}... | collective-permute-start | bytes 393224 | tf_op jit(solution)/shard_map/ppermute | solution.py:188
  85.3 1.9 %collective-permute-start.13 = (bf16[256,256]{1,0:T(8,128)(2,1)S(1)}, bf16[256,256]{1,0:T(8,128)(2,1)S(1)}, u32[]{:S(2)}, u32[]{:S(2)}) collective-permute-start(bf16[256,256]{1,0:T(8,128)(2,1)S(1)} %get-tuple-element.35), channel_id=1, source_target_pairs={{0,96},{32,0},{64,32},{96,64},{1,97},{33,1},{65,33},{97,65},{2,98}... | collective-permute-start | bytes 393224 | tf_op jit(solution)/shard_map/ppermute | solution.py:188
  87.2 0.1 add_convert_fusion.2
  87.3 2.2 %collective-permute-done.12 = bf16[256,256]{1,0:T(8,128)(2,1)S(1)} collective-permute-done((bf16[256,256]{1,0:T(8,128)(2,1)S(1)}, bf16[256,256]{1,0:T(8,128)(2,1)S(1)}, u32[]{:S(2)}, u32[]{:S(2)}) %collective-permute-start.12) | collective-permute-done | bytes 131104 | tf_op jit(solution)/shard_map/ppermute | solution.py:188
  89.5 1.3 collective-permute-done.13
  90.7 1.5 collective-permute-done.14
  92.2 0.1 add_convert_fusion.1
  92.3 16.5 %all_to_all.59 = bf16[16,16,512]{2,1,0:T(8,128)(2,1)S(1)} all-to-all(bf16[16,16,512]{2,1,0:T(8,128)(2,1)S(1)} %pad_maximum_fusion), channel_id=1, replica_groups=mesh['dp'=2,'y'=4,'xh'=2,'z'=8,'mp'=2] {'xh','z'}, dimensions={0} | all-to-all | bytes 524288 | tf_op jit(solution)/shard_map/all_to_all | solution.py:206
  108.9 0.1 multiply_reduce_fusion.1
  109.0 0.1 subtract_convert_fusion.1
  109.2 13.1 %all_to_all.60 = bf16[16,16,512]{2,1,0:T(8,128)(2,1)S(1)} all-to-all(bf16[16,16,512]{2,1,0:T(8,128)(2,1)S(1)} %broadcast_in_dim.13), channel_id=1, replica_groups=mesh['dp'=2,'y'=4,'xh'=2,'z'=8,'mp'=2] {'xh','z'}, dimensions={0} | all-to-all | bytes 524288 | tf_op jit(solution)/shard_map/all_to_all | solution.py:201
  122.3 0.3 fusion
  122.6 0.6 collective-permute-start.15
  123.2 1.0 collective-permute-start.16
  124.2 0.5 collective-permute-start.17
  124.7 1.0 convolution_convert_fusion
  125.7 4.0 %all-to-all-start.5 = ((bf16[16,16,512]{2,1,0:T(8,128)(2,1)}), bf16[16,16,512]{2,1,0:T(8,128)(2,1)S(1)}, u32[]{:S(2)}, u32[]{:S(2)}) async-start(bf16[16,16,512]{2,1,0:T(8,128)(2,1)} %bitcast.12), calls=%async_computation.5 | async-start | bytes 524288 | tf_op jit(solution)/shard_map/all_to_all | solution.py:245
  129.8 0.1 add_convert_fusion.weight_ref
  129.9 4.6 %collective-permute-start.18 = (bf16[128,512]{1,0:T(8,128)(2,1)S(1)}, bf16[128,512]{1,0:T(8,128)(2,1)S(1)}, u32[]{:S(2)}, u32[]{:S(2)}) collective-permute-start(bf16[128,512]{1,0:T(8,128)(2,1)S(1)} %add_convert_fusion.weight_ref), channel_id=1, source_target_pairs={{0,128},{128,0},{1,129},{129,1},{2,130},{130,2},{3,131},{131,3},{4... | collective-permute-start | bytes 393224 | tf_op jit(solution)/shard_map/ppermute | solution.py:184
  134.4 2.7 %collective-permute-done.18.weight_other_ref = bf16[128,512]{1,0:T(8,128)(2,1)S(1)} collective-permute-done((bf16[128,512]{1,0:T(8,128)(2,1)S(1)}, bf16[128,512]{1,0:T(8,128)(2,1)S(1)}, u32[]{:S(2)}, u32[]{:S(2)}) %collective-permute-start.18) | collective-permute-done | bytes 131104 | tf_op jit(solution)/shard_map/ppermute | solution.py:184
  137.2 1.9 %all-to-all-done.5 = bf16[16,16,512]{2,1,0:T(8,128)(2,1)S(1)} async-done(((bf16[16,16,512]{2,1,0:T(8,128)(2,1)}), bf16[16,16,512]{2,1,0:T(8,128)(2,1)S(1)}, u32[]{:S(2)}, u32[]{:S(2)}) %all-to-all-start.5) | async-done | bytes 262176 | tf_op jit(solution)/shard_map/all_to_all | solution.py:245
  139.1 11.6 %collective-permute-start.19 = (bf16[256,512]{1,0:T(8,128)(2,1)S(1)}, bf16[256,512]{1,0:T(8,128)(2,1)S(1)}, u32[]{:S(2)}, u32[]{:S(2)}) collective-permute-start(bf16[256,512]{1,0:T(8,128)(2,1)S(1)} %bitcast.25), channel_id=1, source_target_pairs={{0,1},{1,0},{2,3},{3,2},{4,5},{5,4},{6,7},{7,6},{8,9},{9,8},{10,11... | collective-permute-start | bytes 786440 | tf_op jit(solution)/shard_map/ppermute | solution.py:184
  150.7 1.2 collective-permute-done.19.other_ref
  151.8 0.9 finish.1
  (40 shorter events, 0.3 us)
Async XLA Ops:
  2.5 17.4 %collective-permute-start = (bf16[128,512]{1,0:T(8,128)(2,1)}, bf16[128,512]{1,0:T(8,128)(2,1)S(1)}, u32[]{:S(2)}, u32[]{:S(2)}) collective-permute-start(bf16[128,512]{1,0:T(8,128)(2,1)} %get-tuple-element.25), channel_id=1, source_target_pairs={{0,64},{32,96},{64,0},{96,32},{1,65},{33,97},{65,1},{97,33},{2,66}... | collective-permute-start | bytes 393224 | tf_op jit(solution)/shard_map/ppermute | solution.py:188
  6.2 10.9 %copy-start.2 = (bf16[128,512]{1,0:T(8,128)(2,1)S(1)}, bf16[128,512]{1,0:T(8,128)(2,1)}, u32[]{:S(2)}) copy-start(bf16[128,512]{1,0:T(8,128)(2,1)} %get-tuple-element.25) | copy-start | bytes 393220
  6.2 20.2 %all-to-all-start = ((bf16[16,16,512]{2,1,0:T(8,128)(2,1)}), bf16[16,16,512]{2,1,0:T(8,128)(2,1)S(1)}, u32[]{:S(2)}, u32[]{:S(2)}) async-start(bf16[16,16,512]{2,1,0:T(8,128)(2,1)} %bitcast.38), calls=%async_computation | async-start | bytes 524288 | tf_op jit(solution)/shard_map/all_to_all | solution.py:215
  17.1 5.1 %collective-permute-start.1 = (bf16[128,512]{1,0:T(8,128)(2,1)S(1)}, bf16[128,512]{1,0:T(8,128)(2,1)S(1)}, u32[]{:S(2)}, u32[]{:S(2)}) collective-permute-start(bf16[128,512]{1,0:T(8,128)(2,1)S(1)} %copy-done.2), channel_id=1, source_target_pairs={{0,32},{32,64},{64,96},{96,0},{1,33},{33,65},{65,97},{97,1},{2,34}... | collective-permute-start | bytes 393224 | tf_op jit(solution)/shard_map/ppermute | solution.py:188
  17.6 4.6 %collective-permute-start.2 = (bf16[128,512]{1,0:T(8,128)(2,1)S(1)}, bf16[128,512]{1,0:T(8,128)(2,1)S(1)}, u32[]{:S(2)}, u32[]{:S(2)}) collective-permute-start(bf16[128,512]{1,0:T(8,128)(2,1)S(1)} %copy-done.2), channel_id=1, source_target_pairs={{0,96},{32,0},{64,32},{96,64},{1,97},{33,1},{65,33},{97,65},{2,98}... | collective-permute-start | bytes 393224 | tf_op jit(solution)/shard_map/ppermute | solution.py:188
  26.7 38.2 %copy-start = (bf16[1,256,2048]{2,1,0:T(8,128)(2,1)S(1)}, bf16[1,256,2048]{2,1,0:T(8,128)(2,1)}, u32[]{:S(2)}) copy-start(bf16[1,256,2048]{2,1,0:T(8,128)(2,1)} %param.5) | copy-start | bytes 3145732
  26.7 38.2 %copy-start.1 = (bf16[1,256,2048]{2,1,0:T(8,128)(2,1)S(1)}, bf16[1,256,2048]{2,1,0:T(8,128)(2,1)}, u32[]{:S(2)}) copy-start(bf16[1,256,2048]{2,1,0:T(8,128)(2,1)} %param.9) | copy-start | bytes 3145732
  57.7 5.5 %collective-permute-start.6 = (bf16[256,256]{1,0:T(8,128)(2,1)S(1)}, bf16[256,256]{1,0:T(8,128)(2,1)S(1)}, u32[]{:S(2)}, u32[]{:S(2)}) collective-permute-start(bf16[256,256]{1,0:T(8,128)(2,1)S(1)} %get-tuple-element.50.refs_3_), channel_id=1, source_target_pairs={{0,64},{32,96},{64,0},{96,32},{1,65},{33,97},{65,1},{97,33},{2,66}... | collective-permute-start | bytes 393224 | tf_op jit(solution)/shard_map/ppermute | solution.py:188
  57.8 7.1 %collective-permute-start.7 = (bf16[256,256]{1,0:T(8,128)(2,1)S(1)}, bf16[256,256]{1,0:T(8,128)(2,1)S(1)}, u32[]{:S(2)}, u32[]{:S(2)}) collective-permute-start(bf16[256,256]{1,0:T(8,128)(2,1)S(1)} %get-tuple-element.50.refs_3_), channel_id=1, source_target_pairs={{0,32},{32,64},{64,96},{96,0},{1,33},{33,65},{65,97},{97,1},{2,34}... | collective-permute-start | bytes 393224 | tf_op jit(solution)/shard_map/ppermute | solution.py:188
  58.3 6.6 %collective-permute-start.8 = (bf16[256,256]{1,0:T(8,128)(2,1)S(1)}, bf16[256,256]{1,0:T(8,128)(2,1)S(1)}, u32[]{:S(2)}, u32[]{:S(2)}) collective-permute-start(bf16[256,256]{1,0:T(8,128)(2,1)S(1)} %get-tuple-element.50.refs_3_), channel_id=1, source_target_pairs={{0,96},{32,0},{64,32},{96,64},{1,97},{33,1},{65,33},{97,65},{2,98}... | collective-permute-start | bytes 393224 | tf_op jit(solution)/shard_map/ppermute | solution.py:188
  60.6 13.8 %collective-permute-start.3 = (bf16[256,256]{1,0:T(8,128)(2,1)S(1)}, bf16[256,256]{1,0:T(8,128)(2,1)S(1)}, u32[]{:S(2)}, u32[]{:S(2)}) collective-permute-start(bf16[256,256]{1,0:T(8,128)(2,1)S(1)} %get-tuple-element.51.refs_3_), channel_id=1, source_target_pairs={{0,64},{32,96},{64,0},{96,32},{1,65},{33,97},{65,1},{97,33},{2,66}... | collective-permute-start | bytes 393224 | tf_op jit(solution)/shard_map/ppermute | solution.py:188
  62.2 13.1 %collective-permute-start.4 = (bf16[256,256]{1,0:T(8,128)(2,1)S(1)}, bf16[256,256]{1,0:T(8,128)(2,1)S(1)}, u32[]{:S(2)}, u32[]{:S(2)}) collective-permute-start(bf16[256,256]{1,0:T(8,128)(2,1)S(1)} %get-tuple-element.51.refs_3_), channel_id=1, source_target_pairs={{0,32},{32,64},{64,96},{96,0},{1,33},{33,65},{65,97},{97,1},{2,34}... | collective-permute-start | bytes 393224 | tf_op jit(solution)/shard_map/ppermute | solution.py:188
  63.2 12.1 %collective-permute-start.5 = (bf16[256,256]{1,0:T(8,128)(2,1)S(1)}, bf16[256,256]{1,0:T(8,128)(2,1)S(1)}, u32[]{:S(2)}, u32[]{:S(2)}) collective-permute-start(bf16[256,256]{1,0:T(8,128)(2,1)S(1)} %get-tuple-element.51.refs_3_), channel_id=1, source_target_pairs={{0,96},{32,0},{64,32},{96,64},{1,97},{33,1},{65,33},{97,65},{2,98}... | collective-permute-start | bytes 393224 | tf_op jit(solution)/shard_map/ppermute | solution.py:188
  72.9 14.3 %collective-permute-start.10 = (bf16[256,256]{1,0:T(8,128)(2,1)S(1)}, bf16[256,256]{1,0:T(8,128)(2,1)S(1)}, u32[]{:S(2)}, u32[]{:S(2)}) collective-permute-start(bf16[256,256]{1,0:T(8,128)(2,1)S(1)} %get-tuple-element.31), channel_id=1, source_target_pairs={{0,96},{32,0},{64,32},{96,64},{1,97},{33,1},{65,33},{97,65},{2,98}... | collective-permute-start | bytes 393224 | tf_op jit(solution)/shard_map/ppermute | solution.py:188
  73.6 13.6 %collective-permute-start.11 = (bf16[256,256]{1,0:T(8,128)(2,1)S(1)}, bf16[256,256]{1,0:T(8,128)(2,1)S(1)}, u32[]{:S(2)}, u32[]{:S(2)}) collective-permute-start(bf16[256,256]{1,0:T(8,128)(2,1)S(1)} %get-tuple-element.32), channel_id=1, source_target_pairs={{0,32},{32,64},{64,96},{96,0},{1,33},{33,65},{65,97},{97,1},{2,34}... | collective-permute-start | bytes 393224 | tf_op jit(solution)/shard_map/ppermute | solution.py:188
  74.4 12.8 %collective-permute-start.9 = (bf16[256,256]{1,0:T(8,128)(2,1)S(1)}, bf16[256,256]{1,0:T(8,128)(2,1)S(1)}, u32[]{:S(2)}, u32[]{:S(2)}) collective-permute-start(bf16[256,256]{1,0:T(8,128)(2,1)S(1)} %get-tuple-element.30), channel_id=1, source_target_pairs={{0,64},{32,96},{64,0},{96,32},{1,65},{33,97},{65,1},{97,33},{2,66}... | collective-permute-start | bytes 393224 | tf_op jit(solution)/shard_map/ppermute | solution.py:188
  83.3 6.2 %collective-permute-start.12 = (bf16[256,256]{1,0:T(8,128)(2,1)S(1)}, bf16[256,256]{1,0:T(8,128)(2,1)S(1)}, u32[]{:S(2)}, u32[]{:S(2)}) collective-permute-start(bf16[256,256]{1,0:T(8,128)(2,1)S(1)} %get-tuple-element.34), channel_id=1, source_target_pairs={{0,64},{32,96},{64,0},{96,32},{1,65},{33,97},{65,1},{97,33},{2,66}... | collective-permute-start | bytes 393224 | tf_op jit(solution)/shard_map/ppermute | solution.py:188
  85.3 5.4 %collective-permute-start.13 = (bf16[256,256]{1,0:T(8,128)(2,1)S(1)}, bf16[256,256]{1,0:T(8,128)(2,1)S(1)}, u32[]{:S(2)}, u32[]{:S(2)}) collective-permute-start(bf16[256,256]{1,0:T(8,128)(2,1)S(1)} %get-tuple-element.35), channel_id=1, source_target_pairs={{0,96},{32,0},{64,32},{96,64},{1,97},{33,1},{65,33},{97,65},{2,98}... | collective-permute-start | bytes 393224 | tf_op jit(solution)/shard_map/ppermute | solution.py:188
  87.2 5.0 %collective-permute-start.14 = (bf16[256,256]{1,0:T(8,128)(2,1)S(1)}, bf16[256,256]{1,0:T(8,128)(2,1)S(1)}, u32[]{:S(2)}, u32[]{:S(2)}) collective-permute-start(bf16[256,256]{1,0:T(8,128)(2,1)S(1)} %get-tuple-element.36), channel_id=1, source_target_pairs={{0,32},{32,64},{64,96},{96,0},{1,33},{33,65},{65,97},{97,1},{2,34}... | collective-permute-start | bytes 393224 | tf_op jit(solution)/shard_map/ppermute | solution.py:188
  122.6 7.1 %collective-permute-start.15 = (bf16[128,512]{1,0:T(8,128)(2,1)S(1)}, bf16[128,512]{1,0:T(8,128)(2,1)S(1)}, u32[]{:S(2)}, u32[]{:S(2)}) collective-permute-start(bf16[128,512]{1,0:T(8,128)(2,1)S(1)} %get-tuple-element.47), channel_id=1, source_target_pairs={{0,64},{32,96},{64,0},{96,32},{1,65},{33,97},{65,1},{97,33},{2,66}... | collective-permute-start | bytes 393224 | tf_op jit(solution)/shard_map/ppermute | solution.py:188
  123.2 6.6 %collective-permute-start.16 = (bf16[128,512]{1,0:T(8,128)(2,1)S(1)}, bf16[128,512]{1,0:T(8,128)(2,1)S(1)}, u32[]{:S(2)}, u32[]{:S(2)}) collective-permute-start(bf16[128,512]{1,0:T(8,128)(2,1)S(1)} %get-tuple-element.49), channel_id=1, source_target_pairs={{0,96},{32,0},{64,32},{96,64},{1,97},{33,1},{65,33},{97,65},{2,98}... | collective-permute-start | bytes 393224 | tf_op jit(solution)/shard_map/ppermute | solution.py:188
  124.2 5.6 %collective-permute-start.17 = (bf16[128,512]{1,0:T(8,128)(2,1)S(1)}, bf16[128,512]{1,0:T(8,128)(2,1)S(1)}, u32[]{:S(2)}, u32[]{:S(2)}) collective-permute-start(bf16[128,512]{1,0:T(8,128)(2,1)S(1)} %get-tuple-element.48), channel_id=1, source_target_pairs={{0,32},{32,64},{64,96},{96,0},{1,33},{33,65},{65,97},{97,1},{2,34}... | collective-permute-start | bytes 393224 | tf_op jit(solution)/shard_map/ppermute | solution.py:188
  125.7 13.3 %all-to-all-start.5 = ((bf16[16,16,512]{2,1,0:T(8,128)(2,1)}), bf16[16,16,512]{2,1,0:T(8,128)(2,1)S(1)}, u32[]{:S(2)}, u32[]{:S(2)}) async-start(bf16[16,16,512]{2,1,0:T(8,128)(2,1)} %bitcast.12), calls=%async_computation.5 | async-start | bytes 524288 | tf_op jit(solution)/shard_map/all_to_all | solution.py:245
  129.9 7.3 %collective-permute-start.18 = (bf16[128,512]{1,0:T(8,128)(2,1)S(1)}, bf16[128,512]{1,0:T(8,128)(2,1)S(1)}, u32[]{:S(2)}, u32[]{:S(2)}) collective-permute-start(bf16[128,512]{1,0:T(8,128)(2,1)S(1)} %add_convert_fusion.weight_ref), channel_id=1, source_target_pairs={{0,128},{128,0},{1,129},{129,1},{2,130},{130,2},{3,131},{131,3},{4... | collective-permute-start | bytes 393224 | tf_op jit(solution)/shard_map/ppermute | solution.py:184
  139.1 12.8 %collective-permute-start.19 = (bf16[256,512]{1,0:T(8,128)(2,1)S(1)}, bf16[256,512]{1,0:T(8,128)(2,1)S(1)}, u32[]{:S(2)}, u32[]{:S(2)}) collective-permute-start(bf16[256,512]{1,0:T(8,128)(2,1)S(1)} %bitcast.25), channel_id=1, source_target_pairs={{0,1},{1,0},{2,3},{3,2},{4,5},{5,4},{6,7},{7,6},{8,9},{9,8},{10,11... | collective-permute-start | bytes 786440 | tf_op jit(solution)/shard_map/ppermute | solution.py:184
